TPU v7x, 32 devices: a whole 2x2x4 slice. The times are simulated.
32 devices in a mesh: energy: 8 (over z, core), cell: 4 (over y, x).
Axes of the slice: x: 2, y: 2, z: 4, core: 2. Of those that a mesh axis runs over, the one named last changes fastest.
Arguments:
- green: bfloat16 [4, 48, 8, 16, 512], P(None, 'energy', 'cell'), may hold values from -6 to 6
- screened: bfloat16 [4, 48, 8, 16, 512], P(None, 'energy', None, 'cell'), may hold values from -6 to 6
- cell_map: int32 [8], replicated, may hold values from 0 to 7, each once
- shift_table: int32 [8, 8, 3], replicated, may hold values from 0 to 5, as said below
- shift_count: int32 [8, 8], replicated, may hold values from 1 to 3, as said below
Outputs:
- sigma: float32 [4, 48, 8, 16, 512], P(None, 'energy', 'cell')
Inputs may be any that keep to these rules, and one draw needn't show every extreme that they name: `shift_table`: offsets of requested energies within the source group; slots c >= shift_count[g, s] are not read. `shift_count`: some destination group requests 3 energies from every source group. `cell_map`: each cell stands at exactly one position.
All inputs are finite; a program needn't handle non-finite values.
Results may differ from a plain program's by a relative error of at most 0.0003.
Values may be sent and summed in bfloat16 or wider, within the bound.
No kernel may reach another device: no remote copies, remote signals or barrier semaphores. Data moves between devices by JAX's collectives and lax.ppermute only.
A program may use at most 128 MiB of HBM per device.

v0:
```python
import jax
import jax.numpy as jnp
from jax import lax
from jax.sharding import PartitionSpec as P

SCALE = 0.2


def per_device(green, screened, cell_map, shift_table, shift_count):
    groups = lax.axis_size("energy")
    cell_count = lax.axis_size("cell")
    per_energy = green.shape[1]
    per_cell = green.shape[2]
    width = green.shape[4]
    slot_count = shift_table.shape[2]
    wanted = jnp.transpose(cell_map.reshape(cell_count, per_cell)).reshape(-1)
    outgoing = jnp.take(screened, wanted, axis=2)
    outgoing = outgoing.reshape(4, per_energy, per_cell, cell_count, screened.shape[3], width)
    arrived = lax.all_to_all(outgoing, "cell", split_axis=3, concat_axis=3, tiled=True)
    owned = arrived.reshape(4, per_energy, per_cell, green.shape[3], width)
    whole = lax.all_gather(green, "energy", axis=1, tiled=True)
    padding = jnp.zeros((4, per_energy) + whole.shape[2:], whole.dtype)
    padded = jnp.concatenate([padding, whole], axis=1)
    group = lax.axis_index("energy")
    first = group * per_energy
    table_row = shift_table[group]
    counts = shift_count[group]
    every = lax.all_gather(owned, "energy", axis=1, tiled=True)

    def values_of(energy):
        return lax.dynamic_index_in_dim(every, energy, 1, keepdims=False)

    def turn(totals, source):
        sums = list(totals)
        for slot in range(slot_count):
            energy = source * per_energy + table_row[source, slot]
            live = (slot < counts[source]).astype(jnp.float32)
            start = jnp.maximum(first - energy, -per_energy) + per_energy
            window = lax.dynamic_slice_in_dim(padded, start, per_energy, 1)
            value = values_of(energy)
            for kind in range(2):
                g_real = window[2 * kind].astype(jnp.float32)
                g_imag = window[2 * kind + 1].astype(jnp.float32)
                w_real = value[2 * kind].astype(jnp.float32)[None] * live
                w_imag = value[2 * kind + 1].astype(jnp.float32)[None] * live
                sums[2 * kind] = sums[2 * kind] - (g_real * w_imag + g_imag * w_real)
                sums[2 * kind + 1] = sums[2 * kind + 1] + (g_real * w_real - g_imag * w_imag)
        return (tuple(sums), None)

    zeros = jnp.zeros(green.shape[1:], jnp.float32)
    totals, _ = lax.scan(turn, (zeros, zeros, zeros, zeros), jnp.arange(groups, dtype=jnp.int32))
    return jnp.stack(totals, axis=0) * SCALE


def solution(mesh):
    placed = (
        P(None, "energy", "cell", None, None),
        P(None, "energy", None, "cell", None),
        P(),
        P(),
        P(),
    )
    return jax.shard_map(
        per_device,
        mesh=mesh,
        in_specs=placed,
        out_specs=P(None, "energy", "cell", None, None),
        check_vma=False,
    )
```

profile of v0, /device:TPU:0, one launch (start us, length us, event | category | flops | bytes accessed | tf_op | source)
XLA Modules:
  0.0 259.8 jit_solution(13094623347676819058)
XLA Ops:
  10.8 16.3 %all_to_all.5 = bf16[4,6,2,4,4,512]{5,4,2,1,0,3:T(4,128)(2,1)S(1)} all-to-all(bf16[4,6,2,4,4,512]{5,4,2,1,0,3:T(4,128)(2,1)S(1)} %copy.16), channel_id=1, replica_groups=mesh['energy'=8,'cell'=4] {'cell'}, dimensions={3} | all-to-all | bytes 1572864 | tf_op jit(solution)/shard_map/all_to_all | solution.py:19
  27.1 1.7 copy.17
  30.3 46.1 %all-gather.3.cloned.1.call-done = bf16[4,48,2,16,512]{4,3,2,1,0:T(8,128)(2,1)} async-done(((bf16[4,6,2,16,512]{4,3,2,1,0:T(8,128)(2,1)}), bf16[4,48,2,16,512]{4,3,2,1,0:T(8,128)(2,1)}) %all-gather.3.cloned.1.call-update) | async-done | bytes 6291472 | tf_op jit(solution)/shard_map/all_gather | solution.py:21
  76.4 7.1 %concatenate.3 = bf16[4,54,2,16,512]{4,3,2,1,0:T(8,128)(2,1)} pad(bf16[4,48,2,16,512]{4,3,2,1,0:T(8,128)(2,1)} %all-gather.3.cloned.1.call-done, bf16[]{:T(256)} %constant.97.clone.1), padding=0_0x6_0x0_0x0_0x0_0 | pad | bytes 13369346 | tf_op jit(solution)/shard_map/concatenate | solution.py:23
  83.6 57.9 %all-gather.5.cloned.1.call-done = bf16[4,48,2,16,512]{4,2,3,1,0:T(2,128)(2,1)} async-done(((bf16[4,6,2,16,512]{4,2,3,1,0:T(2,128)(2,1)}), bf16[4,48,2,16,512]{4,2,3,1,0:T(2,128)(2,1)}) %all-gather.5.cloned.1.call-update) | async-done | bytes 6291472 | tf_op jit(solution)/shard_map/all_gather | solution.py:28
  141.5 7.4 %copy.18 = bf16[4,48,2,16,512]{4,3,2,1,0:T(8,128)(2,1)} copy(bf16[4,48,2,16,512]{4,2,3,1,0:T(2,128)(2,1)} %all-gather.5.cloned.1.call-done) | data formatting | bytes 12582912
  148.8 102.7 %while.20 = (s32[]{:T(128)}, f32[6,2,16,512]{3,2,1,0:T(8,128)S(1)}, f32[6,2,16,512]{3,2,1,0:T(8,128)S(1)}, f32[6,2,16,512]{3,2,1,0:T(8,128)S(1)}, f32[6,2,16,512...) while((s32[]{:T(128)}, f32[6,2,16,512]{3,2,1,0:T(8,128)S(1)}, ...), condition=%wide.region_1.2_spmd.clone, body=%wide.region_0.1_spmd.clone.sunk | while | flops 6684718 | bytes 7471924 | solution.py:51
  158.1 1.8 fusion.28
  159.9 1.8 fusion.27
  170.9 1.8 fusion.28
  172.7 1.8 fusion.27
  183.8 1.8 fusion.28
  185.6 1.8 fusion.27
  196.6 1.8 fusion.28
  198.4 1.8 fusion.27
  209.5 1.8 fusion.28
  211.3 1.8 fusion.27
  222.3 1.8 fusion.28
  224.1 1.8 fusion.27
  235.1 1.8 fusion.28
  236.9 1.8 fusion.27
  248.0 1.8 fusion.28
  249.8 1.8 fusion.27
  251.5 1.5 maximum_multiply_fusion
  (57 shorter events, 28.5 us)
Async XLA Ops:
  6.5 1.7 copy-start
  6.5 69.9 %all-gather.3.cloned.1.call-start = ((), (), s32[]{:S(2)}) async-start(), calls=%async_computation.1 | async-start | bytes 7077888 | tf_op jit(solution)/shard_map/all_gather | solution.py:21
  7.3 134.2 %all-gather.5.cloned.1.call-start = ((), (), s32[]{:S(2)}) async-start(), calls=%async_computation.2 | async-start | bytes 7077888 | tf_op jit(solution)/shard_map/all_gather | solution.py:28
Sparse Core Ops, SparseCore 0:
  9.0 67.4 all-gather.2
  78.0 63.3 all-gather.4
where the time goes:
time: 262 us; the launch traced here: 260 us
  waiting for transfers between devices  105 us (40%)
  loops' own time  51.6 us (20%)
  other arithmetic  38.7 us (15%)
  local copies, waits for them, and re-layouts  35 us (13%)
  blocking collectives  16.3 us (6%)
  between operations  13.5 us (5%)
    all_gather x1, waiting for transfers between devices, per_device(): every = lax.all_gather(owned, 'energy', axis=1, tiled=True)  57.9 us
    another operation x1, loops' own time, per_device(): lax.scan(turn, (zeros, zeros, zeros, zeros), jnp.arange(groups, dtype=jnp...  51.6 us
    all_gather x1, waiting for transfers between devices, per_device(): whole = lax.all_gather(green, 'energy', axis=1, tiled=True)  46.1 us
    add x16, other arithmetic, turn(): sums[2 * kind + 1] + (g_real * w_real - g_imag * w_imag)  28.3 us
    all_to_all x1, blocking collectives, per_device(): lax.all_to_all(outgoing, 'cell', split_axis=3, concat_axis=3, tiled=True)  16.3 us
    mul x8, other arithmetic, turn(): w_imag = value[2 * kind + 1].astype(jnp.float32)[None] * live  8.47 us
    unnamed x4, local copies, waits for them, and re-layouts  7.36 us
    concatenate x1, local copies, waits for them, and re-layouts, per_device(): padded = jnp.concatenate([padding, whole], axis=1)  7.14 us
  transfers between devices with their start and end apart: 2, of which 2 were waited for; matrix products, arithmetic and copies ran while one was open for 5% of the time, Pallas kernels for 0%

commit v1 on v0

v1 whole, which is shorter than its diff:
```python
import functools

import jax
import jax.numpy as jnp
from jax import lax
from jax.experimental import pallas as pl
from jax.experimental.pallas import tpu as pltpu
from jax.sharding import PartitionSpec as P

SCALE = 0.2
LANES = 128


def slice_of(index, tiles, parts):
    return index // (tiles * parts), (index // parts) % tiles, index % parts


def pack_kernel(groups, tiles, parts, me_ref, whole_ref, *refs):
    outs, sems = refs[:groups], refs[groups]
    me = me_ref[0]
    rows = outs[0].shape[2]
    copies = []
    for k in range(groups):
        cell, tile, part = slice_of(me ^ k, tiles, parts)
        source = whole_ref.at[:, :, cell, pl.ds(part * rows, rows), pl.ds(pl.multiple_of(tile * LANES, LANES), LANES)]
        copies.append(pltpu.make_async_copy(source, outs[k], sems.at[k]))
    for copy in copies:
        copy.start()
    for copy in copies:
        copy.wait()


def pack(me, whole, groups, tiles, parts):
    comps, energies, _, rows, _ = whole.shape
    block = jax.ShapeDtypeStruct((comps, energies, rows // parts, LANES), whole.dtype)
    return pl.pallas_call(
        functools.partial(pack_kernel, groups, tiles, parts),
        out_shape=[block] * groups,
        in_specs=[pl.BlockSpec(memory_space=pltpu.SMEM), pl.BlockSpec(memory_space=pl.ANY)],
        out_specs=[pl.BlockSpec(memory_space=pl.ANY)] * groups,
        scratch_shapes=[pltpu.SemaphoreType.DMA((groups,))],
        name="pack",
    )(me, whole)


def sigma_kernel(groups, per_energy, slots, me_ref, table_ref, count_ref, *refs):
    greens, screens = refs[:groups], refs[groups : 2 * groups]
    outs = refs[2 * groups : 3 * groups]
    g_all, w_all = refs[3 * groups :]
    me = me_ref[0]
    plane = g_all.shape[2:]
    for comp in range(4):
        for j in range(per_energy):
            g_all[comp, j] = jnp.zeros(plane, jnp.float32)
    for k in range(groups):
        source = me ^ k
        for comp in range(4):
            for j in range(per_energy):
                g_all[comp, (source + 1) * per_energy + j] = greens[k][comp, j].astype(jnp.float32)
                w_all[comp, source * per_energy + j] = screens[k][comp, j].astype(jnp.float32)
    for k in range(groups):
        group = me ^ k
        for kind in range(2):

            def turn(source, sums):
                sums = list(sums)
                count = count_ref[group, source]
                for slot in range(slots):
                    shift = jnp.clip(table_ref[group * groups + source, slot], 0, per_energy - 1)
                    live = jnp.where(slot < count, 1.0, 0.0).astype(jnp.float32)
                    energy = source * per_energy + shift
                    start = (group - source + 1) * per_energy - shift
                    w_real = w_all[2 * kind, energy] * live
                    w_imag = w_all[2 * kind + 1, energy] * live
                    for j in range(per_energy):
                        g_real = g_all[2 * kind, start + j]
                        g_imag = g_all[2 * kind + 1, start + j]
                        sums[2 * j] = sums[2 * j] - (g_real * w_imag + g_imag * w_real)
                        sums[2 * j + 1] = sums[2 * j + 1] + (g_real * w_real - g_imag * w_imag)
                return tuple(sums)

            zeros = tuple(jnp.zeros(plane, jnp.float32) for _ in range(2 * per_energy))
            sums = lax.fori_loop(0, group + 1, turn, zeros)
            for j in range(per_energy):
                outs[k][2 * kind, j] = sums[2 * j] * SCALE
                outs[k][2 * kind + 1, j] = sums[2 * j + 1] * SCALE


def compute(me, table, count, greens, screens):
    groups = len(greens)
    comps, per_energy, rows, lanes = greens[0].shape
    slots = table.shape[-1]
    smem, vmem = pl.BlockSpec(memory_space=pltpu.SMEM), pl.BlockSpec(memory_space=pltpu.VMEM)
    return pl.pallas_call(
        functools.partial(sigma_kernel, groups, per_energy, slots),
        out_shape=[jax.ShapeDtypeStruct(greens[0].shape, jnp.float32)] * groups,
        in_specs=[smem] * 3 + [vmem] * (2 * groups),
        out_specs=[vmem] * groups,
        scratch_shapes=[
            pltpu.VMEM((comps, (groups + 1) * per_energy, rows, lanes), jnp.float32),
            pltpu.VMEM((comps, groups * per_energy, rows, lanes), jnp.float32),
        ],
        compiler_params=pltpu.CompilerParams(vmem_limit_bytes=48 * 1024 * 1024),
        name="sigma",
    )(me, table.reshape(groups * groups, slots), count, *greens, *screens)


def unpack_kernel(groups, tiles, parts, me_ref, *refs):
    blocks, whole_ref, sems = refs[:groups], refs[groups], refs[groups + 1]
    me = me_ref[0]
    rows = blocks[0].shape[2]
    copies = []
    for k in range(groups):
        cell, tile, part = slice_of(me ^ k, tiles, parts)
        target = whole_ref.at[:, :, cell, pl.ds(part * rows, rows), pl.ds(pl.multiple_of(tile * LANES, LANES), LANES)]
        copies.append(pltpu.make_async_copy(blocks[k], target, sems.at[k]))
    for copy in copies:
        copy.start()
    for copy in copies:
        copy.wait()


def unpack(me, blocks, shape, tiles, parts):
    groups = len(blocks)
    return pl.pallas_call(
        functools.partial(unpack_kernel, groups, tiles, parts),
        out_shape=jax.ShapeDtypeStruct(shape, blocks[0].dtype),
        in_specs=[pl.BlockSpec(memory_space=pltpu.SMEM)] + [pl.BlockSpec(memory_space=pl.ANY)] * groups,
        out_specs=pl.BlockSpec(memory_space=pl.ANY),
        scratch_shapes=[pltpu.SemaphoreType.DMA((groups,))],
        name="unpack",
    )(me, *blocks)


def exchange(blocks):
    groups = len(blocks)
    got = list(blocks)
    middle = list(range(groups // 2, groups)) + list(range(1, groups // 2))
    for k in middle:
        got[k] = lax.ppermute(blocks[k], "energy", [(i, i ^ k) for i in range(groups)])
    return got


def per_device(green, screened, cell_map, shift_table, shift_count):
    groups = lax.axis_size("energy")
    cell_count = lax.axis_size("cell")
    per_energy, per_cell, rows, width = green.shape[1:]
    tiles = width // LANES
    parts = groups // (per_cell * tiles)
    me = lax.axis_index("energy").astype(jnp.int32).reshape(1)

    greens = exchange(pack(me, green, groups, tiles, parts))

    wanted = jnp.transpose(cell_map.reshape(cell_count, per_cell)).reshape(-1)
    outgoing = jnp.take(screened, wanted, axis=2)
    outgoing = outgoing.reshape(4, per_energy, per_cell, cell_count, screened.shape[3], width)
    arrived = lax.all_to_all(outgoing, "cell", split_axis=3, concat_axis=3, tiled=True)
    owned = arrived.reshape(4, per_energy, per_cell, rows, width)
    screens = exchange(pack(me, owned, groups, tiles, parts))

    sums = compute(me, shift_table, shift_count, greens, screens)
    return unpack(me, exchange(sums), green.shape, tiles, parts)


def solution(mesh):
    placed = (
        P(None, "energy", "cell", None, None),
        P(None, "energy", None, "cell", None),
        P(),
        P(),
        P(),
    )
    return jax.shard_map(
        per_device,
        mesh=mesh,
        in_specs=placed,
        out_specs=P(None, "energy", "cell", None, None),
        check_vma=False,
    )
```

time: 262 us -> 189 us (0.72)
  the two profiles are of different devices: /device:TPU:0 before, /device:TPU:11 now
where the time goes in v1:
time: 189 us; the launch traced here: 188 us
  Pallas kernels  105 us (56%)
  waiting for transfers between devices  50.3 us (27%)
  starting transfers between devices  25.1 us (13%)
  local copies, waits for them, and re-layouts  7.9 us (4%)
    ppermute x21, waiting for transfers between devices, exchange(): lax.ppermute(blocks[k], 'energy', [(i, i ^ k) for i in range(groups)])  50.3 us
    pallas_call x2, Pallas kernels, pack(): pl.pallas_call(functools.partial(pack_kernel, groups, tiles, parts), out_...  50 us
    pallas_call x1, Pallas kernels, unpack(): pl.pallas_call(functools.partial(unpack_kernel, groups, tiles, parts), ou...  48.8 us
    ppermute x21, starting transfers between devices, exchange(): lax.ppermute(blocks[k], 'energy', [(i, i ^ k) for i in range(groups)])  21.4 us
    pallas_call x1, Pallas kernels, compute(): pl.pallas_call(functools.partial(sigma_kernel, groups, per_energy, slots)...  5.71 us
  transfers between devices with their start and end apart: 22, of which 11 were waited for; matrix products, arithmetic and copies ran while one was open for 1% of the time, Pallas kernels for 27%

profile of v1, /device:TPU:11, one launch (start us, length us, event | category | flops | bytes accessed | tf_op | source)
XLA Modules:
  0.0 188.5 jit_solution(7127363619389846752)
XLA Ops:
  4.5 3.7 %all-to-all-start = ((bf16[4,6,2,4,4,512]{5,4,2,1,0,3:T(4,128)(2,1)}), bf16[4,6,2,4,4,512]{5,4,2,1,0,3:T(4,128)(2,1)S(1)}, u32[]{:S(2)}, u32[]{:S(2)}) async-start(bf16[4,6,2,4,4,512]{5,4,2,1,0,3:T(4,128)(2,1)} %copy.21), calls=%async_computation | async-start | bytes 1572864 | tf_op jit(solution)/shard_map/all_to_all | solution.py:157
  8.2 25.0 %pack.2 = (bf16[4,6,16,128]{3,2,1,0:T(8,128)(2,1)}, bf16[4,6,16,128]{3,2,1,0:T(8,128)(2,1)}, bf16[4,6,16,128]{3,2,1,0:T(8,128)(2,1)}, bf16[4,6,16,128]{3,2,1,0:T...) custom-call(s32[1]{0:T(128)} %bitcast.me_ref, ...), custom_call_target="tpu_custom_call" | custom-call | tf_op jit(solution)/shard_map/pack/pallas_call | solution.py:36
  33.2 1.3 collective-permute-start
  34.7 1.5 collective-permute-start.2
  36.2 2.3 %collective-permute-start.3 = (bf16[4,6,16,128]{3,2,1,0:T(8,128)(2,1)}, bf16[4,6,16,128]{3,2,1,0:T(8,128)(2,1)S(1)}, u32[]{:S(2)}, u32[]{:S(2)}) collective-permute-start(bf16[4,6,16,128]{3,2,1,0:T(8,128)(2,1)} %get-tuple-element.33), channel_id=1, source_target_pairs={{0,16},{4,20},{8,24},{12,28},{16,0},{20,4},{24,8},{28,12},{1,17},{... | collective-permute-start | bytes 294920 | tf_op jit(solution)/shard_map/ppermute | solution.py:140
  40.4 25.0 %pack.3 = (bf16[4,6,16,128]{3,2,1,0:T(8,128)(2,1)}, bf16[4,6,16,128]{3,2,1,0:T(8,128)(2,1)}, bf16[4,6,16,128]{3,2,1,0:T(8,128)(2,1)}, bf16[4,6,16,128]{3,2,1,0:T...) custom-call(s32[1]{0:T(128)} %bitcast.me_ref, ...), custom_call_target="tpu_custom_call" | custom-call | tf_op jit(solution)/shard_map/pack/pallas_call | solution.py:36
  65.5 1.4 collective-permute-start.5
  67.4 2.1 %collective-permute-start.8 = (bf16[4,6,16,128]{3,2,1,0:T(8,128)(2,1)}, bf16[4,6,16,128]{3,2,1,0:T(8,128)(2,1)S(1)}, u32[]{:S(2)}, u32[]{:S(2)}) collective-permute-start(bf16[4,6,16,128]{3,2,1,0:T(8,128)(2,1)} %get-tuple-element.39), channel_id=1, source_target_pairs={{0,8},{4,12},{8,0},{12,4},{16,24},{20,28},{24,16},{28,20},{1,9},{5... | collective-permute-start | bytes 294920 | tf_op jit(solution)/shard_map/ppermute | solution.py:140
  69.7 2.3 %collective-permute-done.5.refs_6_ = bf16[4,6,16,128]{3,2,1,0:T(8,128)(2,1)S(1)} collective-permute-done((bf16[4,6,16,128]{3,2,1,0:T(8,128)(2,1)S(1)}, bf16[4,6,16,128]{3,2,1,0:T(8,128)(2,1)S(1)}, u32[]{:S(2)}, u32[]{:S(2)}) %collective-permute-start.5) | collective-permute-done | bytes 98336 | tf_op jit(solution)/shard_map/ppermute | solution.py:140
  72.0 2.1 %collective-permute-start.10 = (bf16[4,6,16,128]{3,2,1,0:T(8,128)(2,1)}, bf16[4,6,16,128]{3,2,1,0:T(8,128)(2,1)S(1)}, u32[]{:S(2)}, u32[]{:S(2)}) collective-permute-start(bf16[4,6,16,128]{3,2,1,0:T(8,128)(2,1)} %get-tuple-element.41), channel_id=1, source_target_pairs={{0,16},{4,20},{8,24},{12,28},{16,0},{20,4},{24,8},{28,12},{1,17},{... | collective-permute-start | bytes 294920 | tf_op jit(solution)/shard_map/ppermute | solution.py:140
  74.0 3.1 %collective-permute-done.6.refs_7_ = bf16[4,6,16,128]{3,2,1,0:T(8,128)(2,1)S(1)} collective-permute-done((bf16[4,6,16,128]{3,2,1,0:T(8,128)(2,1)S(1)}, bf16[4,6,16,128]{3,2,1,0:T(8,128)(2,1)S(1)}, u32[]{:S(2)}, u32[]{:S(2)}) %collective-permute-start.6) | collective-permute-done | bytes 98336 | tf_op jit(solution)/shard_map/ppermute | solution.py:140
  80.3 8.3 %collective-permute-done.11.refs_13_ = bf16[4,6,16,128]{3,2,1,0:T(8,128)(2,1)S(1)} collective-permute-done((bf16[4,6,16,128]{3,2,1,0:T(8,128)(2,1)}, bf16[4,6,16,128]{3,2,1,0:T(8,128)(2,1)S(1)}, u32[]{:S(2)}, u32[]{:S(2)}) %collective-permute-start.11) | collective-permute-done | bytes 98336 | tf_op jit(solution)/shard_map/ppermute | solution.py:140
  88.5 3.2 %collective-permute-done.12.refs_14_ = bf16[4,6,16,128]{3,2,1,0:T(8,128)(2,1)S(1)} collective-permute-done((bf16[4,6,16,128]{3,2,1,0:T(8,128)(2,1)}, bf16[4,6,16,128]{3,2,1,0:T(8,128)(2,1)S(1)}, u32[]{:S(2)}, u32[]{:S(2)}) %collective-permute-start.12) | collective-permute-done | bytes 98336 | tf_op jit(solution)/shard_map/ppermute | solution.py:140
  91.7 2.1 %collective-permute-done.13.refs_15_ = bf16[4,6,16,128]{3,2,1,0:T(8,128)(2,1)S(1)} collective-permute-done((bf16[4,6,16,128]{3,2,1,0:T(8,128)(2,1)}, bf16[4,6,16,128]{3,2,1,0:T(8,128)(2,1)S(1)}, u32[]{:S(2)}, u32[]{:S(2)}) %collective-permute-start.13) | collective-permute-done | bytes 98336 | tf_op jit(solution)/shard_map/ppermute | solution.py:140
  94.8 5.7 %sigma.1 = (f32[4,6,16,128]{3,2,1,0:T(8,128)S(1)}, f32[4,6,16,128]{3,2,1,0:T(8,128)S(1)}, f32[4,6,16,128]{3,2,1,0:T(8,128)S(1)}, f32[4,6,16,128]{3,2,1,0:T(8,128...) custom-call(s32[1]{0:T(128)} %bitcast.me_ref, ...), custom_call_target="tpu_custom_call" | custom-call | tf_op jit(solution)/shard_map/sigma/pallas_call | solution.py:94
  101.5 1.8 collective-permute-start.16
  103.7 2.2 %collective-permute-start.18 = (f32[4,6,16,128]{3,2,1,0:T(8,128)S(1)}, f32[4,6,16,128]{3,2,1,0:T(8,128)S(1)}, u32[]{:S(2)}, u32[]{:S(2)}) collective-permute-start(f32[4,6,16,128]{3,2,1,0:T(8,128)S(1)} %get-tuple-element.50), channel_id=1, source_target_pairs={{0,20},{4,16},{8,28},{12,24},{16,4},{20,0},{24,12},{28,8},{1,21},{... | collective-permute-start | bytes 589832 | tf_op jit(solution)/shard_map/ppermute | solution.py:140
  106.9 6.7 %collective-permute-done.15.refs_2_ = f32[4,6,16,128]{3,2,1,0:T(8,128)S(1)} collective-permute-done((f32[4,6,16,128]{3,2,1,0:T(8,128)S(1)}, f32[4,6,16,128]{3,2,1,0:T(8,128)S(1)}, u32[]{:S(2)}, u32[]{:S(2)}) %collective-permute-start.15) | collective-permute-done | bytes 196640 | tf_op jit(solution)/shard_map/ppermute | solution.py:140
  113.6 1.7 collective-permute-start.20
  115.2 2.7 %collective-permute-done.16.refs_3_ = f32[4,6,16,128]{3,2,1,0:T(8,128)S(1)} collective-permute-done((f32[4,6,16,128]{3,2,1,0:T(8,128)S(1)}, f32[4,6,16,128]{3,2,1,0:T(8,128)S(1)}, u32[]{:S(2)}, u32[]{:S(2)}) %collective-permute-start.16) | collective-permute-done | bytes 196640 | tf_op jit(solution)/shard_map/ppermute | solution.py:140
  117.9 4.2 %collective-permute-done.18.refs_5_ = f32[4,6,16,128]{3,2,1,0:T(8,128)S(1)} collective-permute-done((f32[4,6,16,128]{3,2,1,0:T(8,128)S(1)}, f32[4,6,16,128]{3,2,1,0:T(8,128)S(1)}, u32[]{:S(2)}, u32[]{:S(2)}) %collective-permute-start.18) | collective-permute-done | bytes 196640 | tf_op jit(solution)/shard_map/ppermute | solution.py:140
  122.1 12.1 %collective-permute-done.19.refs_6_ = f32[4,6,16,128]{3,2,1,0:T(8,128)S(1)} collective-permute-done((f32[4,6,16,128]{3,2,1,0:T(8,128)S(1)}, f32[4,6,16,128]{3,2,1,0:T(8,128)S(1)}, u32[]{:S(2)}, u32[]{:S(2)}) %collective-permute-start.19) | collective-permute-done | bytes 196640 | tf_op jit(solution)/shard_map/ppermute | solution.py:140
  134.2 4.7 %collective-permute-done.20.refs_7_ = f32[4,6,16,128]{3,2,1,0:T(8,128)S(1)} collective-permute-done((f32[4,6,16,128]{3,2,1,0:T(8,128)S(1)}, f32[4,6,16,128]{3,2,1,0:T(8,128)S(1)}, u32[]{:S(2)}, u32[]{:S(2)}) %collective-permute-start.20) | collective-permute-done | bytes 196640 | tf_op jit(solution)/shard_map/ppermute | solution.py:140
  139.7 48.8 %unpack.1 = f32[4,6,2,16,512]{4,3,2,1,0:T(8,128)} custom-call(s32[1]{0:T(128)} %bitcast.me_ref, f32[4,6,16,128]{3,2,1,0:T(8,128)} %copy-done.1, f32[4,6,16,128]{3,2,1,0:T(8,128)} %copy-done.5, f32[4,6,16,128]{3,2,1,0:T(8,128)} %copy-done.6, f32[4,6,16,128]{3,2,1,0:T(8,128)} %copy-done.7, f32[4,6,16,128]{3,2,1,0:T(8,128)} %copy-done.8, ...), custom_call_target="tpu_custom_call" | custom-call | tf_op jit(solution)/shard_map/unpack/pallas_call | solution.py:125
  (68 shorter events, 14.4 us)
Async XLA Ops:
  4.5 34.4 %all-to-all-start = ((bf16[4,6,2,4,4,512]{5,4,2,1,0,3:T(4,128)(2,1)}), bf16[4,6,2,4,4,512]{5,4,2,1,0,3:T(4,128)(2,1)S(1)}, u32[]{:S(2)}, u32[]{:S(2)}) async-start(bf16[4,6,2,4,4,512]{5,4,2,1,0,3:T(4,128)(2,1)} %copy.21), calls=%async_computation | async-start | bytes 1572864 | tf_op jit(solution)/shard_map/all_to_all | solution.py:157
  33.2 32.2 %collective-permute-start = (bf16[4,6,16,128]{3,2,1,0:T(8,128)(2,1)}, bf16[4,6,16,128]{3,2,1,0:T(8,128)(2,1)S(1)}, u32[]{:S(2)}, u32[]{:S(2)}) collective-permute-start(bf16[4,6,16,128]{3,2,1,0:T(8,128)(2,1)} %get-tuple-element.30), channel_id=1, source_target_pairs={{0,4},{4,0},{8,12},{12,8},{16,20},{20,16},{24,28},{28,24},{1,5},{5... | collective-permute-start | bytes 294920 | tf_op jit(solution)/shard_map/ppermute | solution.py:140
  34.5 32.3 %collective-permute-start.1 = (bf16[4,6,16,128]{3,2,1,0:T(8,128)(2,1)}, bf16[4,6,16,128]{3,2,1,0:T(8,128)(2,1)S(1)}, u32[]{:S(2)}, u32[]{:S(2)}) collective-permute-start(bf16[4,6,16,128]{3,2,1,0:T(8,128)(2,1)} %get-tuple-element.31), channel_id=1, source_target_pairs={{0,8},{4,12},{8,0},{12,4},{16,24},{20,28},{24,16},{28,20},{1,9},{5... | collective-permute-start | bytes 294920 | tf_op jit(solution)/shard_map/ppermute | solution.py:140
  34.7 32.6 %collective-permute-start.2 = (bf16[4,6,16,128]{3,2,1,0:T(8,128)(2,1)}, bf16[4,6,16,128]{3,2,1,0:T(8,128)(2,1)S(1)}, u32[]{:S(2)}, u32[]{:S(2)}) collective-permute-start(bf16[4,6,16,128]{3,2,1,0:T(8,128)(2,1)} %get-tuple-element.32), channel_id=1, source_target_pairs={{0,12},{4,8},{8,4},{12,0},{16,28},{20,24},{24,20},{28,16},{1,13},{... | collective-permute-start | bytes 294920 | tf_op jit(solution)/shard_map/ppermute | solution.py:140
  36.2 31.2 %collective-permute-start.3 = (bf16[4,6,16,128]{3,2,1,0:T(8,128)(2,1)}, bf16[4,6,16,128]{3,2,1,0:T(8,128)(2,1)S(1)}, u32[]{:S(2)}, u32[]{:S(2)}) collective-permute-start(bf16[4,6,16,128]{3,2,1,0:T(8,128)(2,1)} %get-tuple-element.33), channel_id=1, source_target_pairs={{0,16},{4,20},{8,24},{12,28},{16,0},{20,4},{24,8},{28,12},{1,17},{... | collective-permute-start | bytes 294920 | tf_op jit(solution)/shard_map/ppermute | solution.py:140
  38.5 31.0 %collective-permute-start.4 = (bf16[4,6,16,128]{3,2,1,0:T(8,128)(2,1)}, bf16[4,6,16,128]{3,2,1,0:T(8,128)(2,1)S(1)}, u32[]{:S(2)}, u32[]{:S(2)}) collective-permute-start(bf16[4,6,16,128]{3,2,1,0:T(8,128)(2,1)} %get-tuple-element.34), channel_id=1, source_target_pairs={{0,20},{4,16},{8,28},{12,24},{16,4},{20,0},{24,12},{28,8},{1,21},{... | collective-permute-start | bytes 294920 | tf_op jit(solution)/shard_map/ppermute | solution.py:140
  39.4 54.5 %copy-start.2 = (bf16[4,6,16,128]{3,2,1,0:T(8,128)(2,1)S(1)}, bf16[4,6,16,128]{3,2,1,0:T(8,128)(2,1)}, u32[]{:S(2)}) copy-start(bf16[4,6,16,128]{3,2,1,0:T(8,128)(2,1)} %get-tuple-element.29.refs_0_) | copy-start | bytes 294916
  39.4 54.5 %copy-start.4 = (s32[8,8]{1,0:T(8,128)S(1)}, s32[8,8]{1,0:T(8,128)}, u32[]{:S(2)}) copy-start(s32[8,8]{1,0:T(8,128)} %count_ref.1) | copy-start | bytes 772
  65.5 6.5 %collective-permute-start.5 = (bf16[4,6,16,128]{3,2,1,0:T(8,128)(2,1)S(1)}, bf16[4,6,16,128]{3,2,1,0:T(8,128)(2,1)S(1)}, u32[]{:S(2)}, u32[]{:S(2)}) collective-permute-start(bf16[4,6,16,128]{3,2,1,0:T(8,128)(2,1)S(1)} %copy-done.14), channel_id=1, source_target_pairs={{0,24},{4,28},{8,16},{12,20},{16,8},{20,12},{24,0},{28,4},{1,25},{... | collective-permute-start | bytes 294920 | tf_op jit(solution)/shard_map/ppermute | solution.py:140
  66.8 10.3 %collective-permute-start.6 = (bf16[4,6,16,128]{3,2,1,0:T(8,128)(2,1)S(1)}, bf16[4,6,16,128]{3,2,1,0:T(8,128)(2,1)S(1)}, u32[]{:S(2)}, u32[]{:S(2)}) collective-permute-start(bf16[4,6,16,128]{3,2,1,0:T(8,128)(2,1)S(1)} %copy-done.13), channel_id=1, source_target_pairs={{0,28},{4,24},{8,20},{12,16},{16,12},{20,8},{24,4},{28,0},{1,29},{... | collective-permute-start | bytes 294920 | tf_op jit(solution)/shard_map/ppermute | solution.py:140
  67.3 10.7 %collective-permute-start.7 = (bf16[4,6,16,128]{3,2,1,0:T(8,128)(2,1)}, bf16[4,6,16,128]{3,2,1,0:T(8,128)(2,1)S(1)}, u32[]{:S(2)}, u32[]{:S(2)}) collective-permute-start(bf16[4,6,16,128]{3,2,1,0:T(8,128)(2,1)} %get-tuple-element.38), channel_id=1, source_target_pairs={{0,4},{4,0},{8,12},{12,8},{16,20},{20,16},{24,28},{28,24},{1,5},{5... | collective-permute-start | bytes 294920 | tf_op jit(solution)/shard_map/ppermute | solution.py:140
  67.4 11.8 %collective-permute-start.8 = (bf16[4,6,16,128]{3,2,1,0:T(8,128)(2,1)}, bf16[4,6,16,128]{3,2,1,0:T(8,128)(2,1)S(1)}, u32[]{:S(2)}, u32[]{:S(2)}) collective-permute-start(bf16[4,6,16,128]{3,2,1,0:T(8,128)(2,1)} %get-tuple-element.39), channel_id=1, source_target_pairs={{0,8},{4,12},{8,0},{12,4},{16,24},{20,28},{24,16},{28,20},{1,9},{5... | collective-permute-start | bytes 294920 | tf_op jit(solution)/shard_map/ppermute | solution.py:140
  69.5 9.8 %collective-permute-start.9 = (bf16[4,6,16,128]{3,2,1,0:T(8,128)(2,1)}, bf16[4,6,16,128]{3,2,1,0:T(8,128)(2,1)S(1)}, u32[]{:S(2)}, u32[]{:S(2)}) collective-permute-start(bf16[4,6,16,128]{3,2,1,0:T(8,128)(2,1)} %get-tuple-element.40), channel_id=1, source_target_pairs={{0,12},{4,8},{8,4},{12,0},{16,28},{20,24},{24,20},{28,16},{1,13},{... | collective-permute-start | bytes 294920 | tf_op jit(solution)/shard_map/ppermute | solution.py:140
  72.0 8.3 %collective-permute-start.10 = (bf16[4,6,16,128]{3,2,1,0:T(8,128)(2,1)}, bf16[4,6,16,128]{3,2,1,0:T(8,128)(2,1)S(1)}, u32[]{:S(2)}, u32[]{:S(2)}) collective-permute-start(bf16[4,6,16,128]{3,2,1,0:T(8,128)(2,1)} %get-tuple-element.41), channel_id=1, source_target_pairs={{0,16},{4,20},{8,24},{12,28},{16,0},{20,4},{24,8},{28,12},{1,17},{... | collective-permute-start | bytes 294920 | tf_op jit(solution)/shard_map/ppermute | solution.py:140
  77.1 11.4 %collective-permute-start.11 = (bf16[4,6,16,128]{3,2,1,0:T(8,128)(2,1)}, bf16[4,6,16,128]{3,2,1,0:T(8,128)(2,1)S(1)}, u32[]{:S(2)}, u32[]{:S(2)}) collective-permute-start(bf16[4,6,16,128]{3,2,1,0:T(8,128)(2,1)} %get-tuple-element.42), channel_id=1, source_target_pairs={{0,20},{4,16},{8,28},{12,24},{16,4},{20,0},{24,12},{28,8},{1,21},{... | collective-permute-start | bytes 294920 | tf_op jit(solution)/shard_map/ppermute | solution.py:140
  78.0 13.8 %collective-permute-start.12 = (bf16[4,6,16,128]{3,2,1,0:T(8,128)(2,1)}, bf16[4,6,16,128]{3,2,1,0:T(8,128)(2,1)S(1)}, u32[]{:S(2)}, u32[]{:S(2)}) collective-permute-start(bf16[4,6,16,128]{3,2,1,0:T(8,128)(2,1)} %get-tuple-element.43), channel_id=1, source_target_pairs={{0,24},{4,28},{8,16},{12,20},{16,8},{20,12},{24,0},{28,4},{1,25},{... | collective-permute-start | bytes 294920 | tf_op jit(solution)/shard_map/ppermute | solution.py:140
  79.2 14.6 %collective-permute-start.13 = (bf16[4,6,16,128]{3,2,1,0:T(8,128)(2,1)}, bf16[4,6,16,128]{3,2,1,0:T(8,128)(2,1)S(1)}, u32[]{:S(2)}, u32[]{:S(2)}) collective-permute-start(bf16[4,6,16,128]{3,2,1,0:T(8,128)(2,1)} %get-tuple-element.44), channel_id=1, source_target_pairs={{0,28},{4,24},{8,20},{12,16},{16,12},{20,8},{24,4},{28,0},{1,29},{... | collective-permute-start | bytes 294920 | tf_op jit(solution)/shard_map/ppermute | solution.py:140
  101.1 4.8 %collective-permute-start.14 = (f32[4,6,16,128]{3,2,1,0:T(8,128)S(1)}, f32[4,6,16,128]{3,2,1,0:T(8,128)S(1)}, u32[]{:S(2)}, u32[]{:S(2)}) collective-permute-start(f32[4,6,16,128]{3,2,1,0:T(8,128)S(1)} %get-tuple-element.46), channel_id=1, source_target_pairs={{0,4},{4,0},{8,12},{12,8},{16,20},{20,16},{24,28},{28,24},{1,5},{5... | collective-permute-start | bytes 589832 | tf_op jit(solution)/shard_map/ppermute | solution.py:140
  101.5 12.0 %collective-permute-start.15 = (f32[4,6,16,128]{3,2,1,0:T(8,128)S(1)}, f32[4,6,16,128]{3,2,1,0:T(8,128)S(1)}, u32[]{:S(2)}, u32[]{:S(2)}) collective-permute-start(f32[4,6,16,128]{3,2,1,0:T(8,128)S(1)} %get-tuple-element.47), channel_id=1, source_target_pairs={{0,8},{4,12},{8,0},{12,4},{16,24},{20,28},{24,16},{28,20},{1,9},{5... | collective-permute-start | bytes 589832 | tf_op jit(solution)/shard_map/ppermute | solution.py:140
  101.5 16.4 %collective-permute-start.16 = (f32[4,6,16,128]{3,2,1,0:T(8,128)S(1)}, f32[4,6,16,128]{3,2,1,0:T(8,128)S(1)}, u32[]{:S(2)}, u32[]{:S(2)}) collective-permute-start(f32[4,6,16,128]{3,2,1,0:T(8,128)S(1)} %get-tuple-element.48), channel_id=1, source_target_pairs={{0,12},{4,8},{8,4},{12,0},{16,28},{20,24},{24,20},{28,16},{1,13},{... | collective-permute-start | bytes 589832 | tf_op jit(solution)/shard_map/ppermute | solution.py:140
  103.3 14.6 %collective-permute-start.17 = (f32[4,6,16,128]{3,2,1,0:T(8,128)S(1)}, f32[4,6,16,128]{3,2,1,0:T(8,128)S(1)}, u32[]{:S(2)}, u32[]{:S(2)}) collective-permute-start(f32[4,6,16,128]{3,2,1,0:T(8,128)S(1)} %get-tuple-element.49), channel_id=1, source_target_pairs={{0,16},{4,20},{8,24},{12,28},{16,0},{20,4},{24,8},{28,12},{1,17},{... | collective-permute-start | bytes 589832 | tf_op jit(solution)/shard_map/ppermute | solution.py:140
  103.7 18.4 %collective-permute-start.18 = (f32[4,6,16,128]{3,2,1,0:T(8,128)S(1)}, f32[4,6,16,128]{3,2,1,0:T(8,128)S(1)}, u32[]{:S(2)}, u32[]{:S(2)}) collective-permute-start(f32[4,6,16,128]{3,2,1,0:T(8,128)S(1)} %get-tuple-element.50), channel_id=1, source_target_pairs={{0,20},{4,16},{8,28},{12,24},{16,4},{20,0},{24,12},{28,8},{1,21},{... | collective-permute-start | bytes 589832 | tf_op jit(solution)/shard_map/ppermute | solution.py:140
  105.9 28.3 %collective-permute-start.19 = (f32[4,6,16,128]{3,2,1,0:T(8,128)S(1)}, f32[4,6,16,128]{3,2,1,0:T(8,128)S(1)}, u32[]{:S(2)}, u32[]{:S(2)}) collective-permute-start(f32[4,6,16,128]{3,2,1,0:T(8,128)S(1)} %get-tuple-element.51), channel_id=1, source_target_pairs={{0,24},{4,28},{8,16},{12,20},{16,8},{20,12},{24,0},{28,4},{1,25},{... | collective-permute-start | bytes 589832 | tf_op jit(solution)/shard_map/ppermute | solution.py:140
  113.6 25.4 %collective-permute-start.20 = (f32[4,6,16,128]{3,2,1,0:T(8,128)S(1)}, f32[4,6,16,128]{3,2,1,0:T(8,128)S(1)}, u32[]{:S(2)}, u32[]{:S(2)}) collective-permute-start(f32[4,6,16,128]{3,2,1,0:T(8,128)S(1)} %get-tuple-element.52), channel_id=1, source_target_pairs={{0,28},{4,24},{8,20},{12,16},{16,12},{20,8},{24,4},{28,0},{1,29},{... | collective-permute-start | bytes 589832 | tf_op jit(solution)/shard_map/ppermute | solution.py:140
  (13 other events, 219.1 us)

commit v2 on v1

v2 whole, which is shorter than its diff:
```python
import functools

import jax
import jax.numpy as jnp
from jax import lax
from jax.experimental import pallas as pl
from jax.experimental.pallas import tpu as pltpu
from jax.sharding import PartitionSpec as P

SCALE = 0.2
LANES = 128
PAIR = 2
STEPS = 32700.0
FINE = 64.0
TINY = 1e-34
SMEM = pl.BlockSpec(memory_space=pltpu.SMEM)
VMEM = pl.BlockSpec(memory_space=pltpu.VMEM)
ANY = pl.BlockSpec(memory_space=pl.ANY)
PARAMS = pltpu.CompilerParams(vmem_limit_bytes=48 * 1024 * 1024)


def slice_of(index, tiles, parts):
    return index // (tiles * parts), (index // parts) % tiles, index % parts


def lanes_of(tile):
    return pl.ds(pl.multiple_of(tile * LANES, LANES), LANES)


def pack_kernel(groups, cells, tiles, parts, me_ref, map_ref, green_ref, screened_ref, *outs):
    me, column = me_ref[0], me_ref[1]
    comps, energies, rows, _ = outs[0].shape
    for k in range(groups):
        cell, tile, part = slice_of(me ^ k, tiles, parts)
        for comp in range(comps):
            for j in range(energies):
                if parts == 1:
                    outs[k][comp, j] = green_ref[comp, j, cell, :, lanes_of(tile)]
                else:
                    block = green_ref[comp, j, cell, :, lanes_of(tile)].astype(jnp.float32)
                    chosen = block[:rows]
                    for other in range(1, parts):
                        chosen = jnp.where(part == other, block[other * rows : (other + 1) * rows], chosen)
                    outs[k][comp, j] = chosen.astype(outs[k].dtype)
    per_cell = green_ref.shape[2]
    for k in range(cells):
        for q in range(per_cell):
            cell = map_ref[(column ^ k) * per_cell + q]
            for comp in range(comps):
                for j in range(energies):
                    outs[groups + k][comp, j, q] = screened_ref[comp, j, cell]


def pack(me, cell_map, green, screened, groups, cells, tiles, parts):
    comps, energies, per_cell, rows, width = green.shape
    block = jax.ShapeDtypeStruct((comps, energies, rows // parts, LANES), green.dtype)
    quarter = jax.ShapeDtypeStruct((comps, energies, per_cell, screened.shape[3], width), screened.dtype)
    outs = pl.pallas_call(
        functools.partial(pack_kernel, groups, cells, tiles, parts),
        out_shape=[block] * groups + [quarter] * cells,
        in_specs=[SMEM, SMEM, VMEM, VMEM],
        out_specs=[VMEM] * (groups + cells),
        compiler_params=PARAMS,
        name="pack",
    )(me, cell_map, green, screened)
    return outs[:groups], outs[groups:]


def place_kernel(groups, cells, tiles, parts, me_ref, *refs):
    quarters, outs = refs[:cells], refs[cells : cells + groups]
    held, whole, sems = refs[cells + groups :]
    me, column = me_ref[0], me_ref[1]
    comps, energies, rows, _ = outs[0].shape
    per_cell, depth = quarters[0].shape[2:4]
    copies = [pltpu.make_async_copy(quarters[k], held.at[column ^ k], sems.at[k]) for k in range(cells)]
    for copy in copies:
        copy.start()
    for copy in copies:
        copy.wait()
    for comp in range(comps):
        for j in range(energies):
            for q in range(per_cell):
                for c in range(cells):
                    whole[comp, j, q, c * depth : (c + 1) * depth, :] = held[c, comp, j, q].astype(jnp.float32)
    for k in range(groups):
        cell, tile, part = slice_of(me ^ k, tiles, parts)
        place = slice(None) if parts == 1 else pl.ds(pl.multiple_of(part * rows, rows), rows)
        for comp in range(comps):
            for j in range(energies):
                outs[k][comp, j] = whole[comp, j, cell, place, lanes_of(tile)].astype(outs[k].dtype)


def place(me, quarters, groups, tiles, parts):
    cells = len(quarters)
    comps, energies, per_cell, depth, width = quarters[0].shape
    block = jax.ShapeDtypeStruct((comps, energies, cells * depth // parts, LANES), quarters[0].dtype)
    return pl.pallas_call(
        functools.partial(place_kernel, groups, cells, tiles, parts),
        out_shape=[block] * groups,
        in_specs=[SMEM] + [ANY] * cells,
        out_specs=[VMEM] * groups,
        scratch_shapes=[
            pltpu.VMEM((cells,) + quarters[0].shape, quarters[0].dtype),
            pltpu.VMEM((comps, energies, per_cell, cells * depth, width), jnp.float32),
            pltpu.SemaphoreType.DMA((cells,)),
        ],
        compiler_params=PARAMS,
        name="place",
    )(me, *quarters)


def scale_rows(per_energy, comps):
    return comps * (per_energy // PAIR)


def sigma_kernel(groups, per_energy, slots, ks, me_ref, table_ref, count_ref, *refs):
    greens, screens = refs[:groups], refs[groups : 2 * groups]
    outs = refs[2 * groups : 2 * groups + len(ks)]
    g_held, w_all, g_all, sems = refs[2 * groups + len(ks) :]
    me = me_ref[0]
    plane = g_all.shape[2:]
    copies = []
    for k in range(groups):
        copies.append(pltpu.make_async_copy(greens[k], g_held.at[me ^ k], sems.at[0, k]))
        copies.append(pltpu.make_async_copy(screens[k], w_all.at[me ^ k], sems.at[1, k]))
    for copy in copies:
        copy.start()
    for copy in copies:
        copy.wait()
    for comp in range(4):
        for j in range(per_energy):
            g_all[comp, j] = jnp.zeros(plane, jnp.float32)
            for source in range(groups):
                g_all[comp, (source + 1) * per_energy + j] = g_held[source, comp, j].astype(jnp.float32)
    row = lax.broadcasted_iota(jnp.int32, plane, 0)
    for at, k in enumerate(ks):
        group = me ^ k
        scale_planes = -(-scale_rows(per_energy, 4) // plane[0])
        codes = [jnp.zeros(plane, jnp.float32) for _ in range(scale_planes)]
        for kind in range(2):

            def turn(source, sums):
                sums = list(sums)
                count = count_ref[group, source]
                for slot in range(slots):
                    shift = jnp.clip(table_ref[group * groups + source, slot], 0, per_energy - 1)
                    live = jnp.where(slot < count, 1.0, 0.0).astype(jnp.float32)
                    start = (group - source + 1) * per_energy - shift
                    w_real = w_all[source, 2 * kind, shift].astype(jnp.float32) * live
                    w_imag = w_all[source, 2 * kind + 1, shift].astype(jnp.float32) * live
                    for j in range(per_energy):
                        g_real = g_all[2 * kind, start + j]
                        g_imag = g_all[2 * kind + 1, start + j]
                        sums[j] = sums[j] - (g_real * w_imag + g_imag * w_real)
                        sums[per_energy + j] = sums[per_energy + j] + (g_real * w_real - g_imag * w_imag)
                return tuple(sums)

            zeros = tuple(jnp.zeros(plane, jnp.float32) for _ in range(2 * per_energy))
            sums = lax.fori_loop(0, group + 1, turn, zeros)
            sums = [total * SCALE for total in sums]
            if k == 0:
                for part in range(2):
                    for j in range(per_energy):
                        outs[at][2 * kind + part, j] = sums[part * per_energy + j]
                continue
            for first in range(0, 2 * per_energy, PAIR):
                pair = sums[first : first + PAIR]
                largest = functools.reduce(jnp.maximum, [jnp.abs(total) for total in pair])
                largest = jnp.maximum(jnp.max(largest, axis=0, keepdims=True), TINY)
                code = jnp.ceil(jnp.log2(largest) * FINE)
                inverse = jnp.exp2(code * (-1.0 / FINE)) * STEPS
                where = (kind * 2 * per_energy + first) // PAIR
                codes[where // plane[0]] = jnp.where(row == where % plane[0], code, codes[where // plane[0]])
                for j, total in enumerate(pair):
                    coded = jnp.round(total * inverse).astype(jnp.int32)
                    outs[at][kind * 2 * per_energy + first + j] = coded.astype(jnp.int16)
        if k != 0:
            for j in range(scale_planes):
                outs[at][4 * per_energy + j] = codes[j].astype(jnp.int32).astype(jnp.int16)


def sigma_of(me, table, count, greens, screens, ks):
    groups = len(greens)
    comps, per_energy, rows, lanes = greens[0].shape
    slots = table.shape[-1]
    planes = comps * per_energy + -(-scale_rows(per_energy, comps) // rows)
    own = jax.ShapeDtypeStruct(greens[0].shape, jnp.float32)
    coded = jax.ShapeDtypeStruct((planes, rows, lanes), jnp.int16)
    return pl.pallas_call(
        functools.partial(sigma_kernel, groups, per_energy, slots, ks),
        out_shape=[own if k == 0 else coded for k in ks],
        in_specs=[SMEM] * 3 + [ANY] * (2 * groups),
        out_specs=[VMEM] * len(ks),
        scratch_shapes=[
            pltpu.VMEM((groups,) + greens[0].shape, greens[0].dtype),
            pltpu.VMEM((groups,) + greens[0].shape, greens[0].dtype),
            pltpu.VMEM((comps, (groups + 1) * per_energy, rows, lanes), jnp.float32),
            pltpu.SemaphoreType.DMA((2, groups)),
        ],
        compiler_params=PARAMS,
        name="sigma",
    )(me, table.reshape(groups * groups, slots), count, *greens, *screens)


def unpack_kernel(groups, tiles, parts, me_ref, *refs):
    blocks, whole_ref = refs[:groups], refs[groups]
    me = me_ref[0]
    comps, energies, rows, _ = blocks[0].shape
    for k in range(groups):
        cell, tile, part = slice_of(me ^ k, tiles, parts)
        spot = slice(None) if parts == 1 else pl.ds(pl.multiple_of(part * rows, rows), rows)
        scales = []
        if k != 0:
            for j in range(blocks[k].shape[0] - comps * energies):
                code = blocks[k][comps * energies + j].astype(jnp.int32).astype(jnp.float32)
                scales.append(jnp.exp2(code * (1.0 / FINE)) * (1.0 / STEPS))
        for comp in range(comps):
            for j in range(energies):
                if k == 0:
                    value = blocks[0][comp, j]
                else:
                    where = (comp * energies + j) // PAIR
                    scale = scales[where // rows][where % rows : where % rows + 1]
                    value = blocks[k][comp * energies + j].astype(jnp.int32).astype(jnp.float32) * scale
                whole_ref[comp, j, cell, spot, lanes_of(tile)] = value


def unpack(me, blocks, shape, tiles, parts):
    groups = len(blocks)
    return pl.pallas_call(
        functools.partial(unpack_kernel, groups, tiles, parts),
        out_shape=jax.ShapeDtypeStruct(shape, jnp.float32),
        in_specs=[SMEM] + [VMEM] * groups,
        out_specs=VMEM,
        compiler_params=PARAMS,
        name="unpack",
    )(me, *blocks)


def swap(block, axis, count, k):
    return block if k == 0 else lax.ppermute(block, axis, [(i, i ^ k) for i in range(count)])


def per_device(green, screened, cell_map, shift_table, shift_count):
    groups = lax.axis_size("energy")
    cells = lax.axis_size("cell")
    per_energy, per_cell, rows, width = green.shape[1:]
    tiles = width // LANES
    parts = groups // (per_cell * tiles)
    me = jnp.stack([lax.axis_index("energy"), lax.axis_index("cell")]).astype(jnp.int32)
    far = list(range(groups // 2, groups))
    near = list(range(groups // 2))

    greens, quarters = pack(me, cell_map, green, screened, groups, cells, tiles, parts)
    greens = {k: swap(greens[k], "energy", groups, k) for k in far + near}
    quarters = [swap(quarters[k], "cell", cells, k) for k in range(cells)]
    screens = place(me, quarters, groups, tiles, parts)
    screens = {k: swap(screens[k], "energy", groups, k) for k in far + near}
    every = range(groups)
    parts_in = ([greens[k] for k in every], [screens[k] for k in every])
    sums = {}
    for ks in (far, near):
        for k, block in zip(ks, sigma_of(me, shift_table, shift_count, *parts_in, ks)):
            sums[k] = swap(block, "energy", groups, k)
    return unpack(me, [sums[k] for k in every], green.shape, tiles, parts)


def solution(mesh):
    placed = (
        P(None, "energy", "cell", None, None),
        P(None, "energy", None, "cell", None),
        P(),
        P(),
        P(),
    )
    return jax.shard_map(
        per_device,
        mesh=mesh,
        in_specs=placed,
        out_specs=P(None, "energy", "cell", None, None),
        check_vma=False,
    )
```

time: 189 us -> 83 us (0.44)
  the two profiles are of different devices: /device:TPU:11 before, /device:TPU:0 now
where the time goes in v2:
time: 83 us; the launch traced here: 82.9 us
  starting transfers between devices  39.4 us (47%)
  waiting for transfers between devices  23.4 us (28%)
  Pallas kernels  16.9 us (20%)
  local copies, waits for them, and re-layouts  3.05 us (4%)
    ppermute x24, starting transfers between devices, swap(): lax.ppermute(block, axis, [(i, i ^ k) for i in range(count)])  39.4 us
    ppermute x24, waiting for transfers between devices, swap(): lax.ppermute(block, axis, [(i, i ^ k) for i in range(count)])  23.4 us
    pallas_call x2, Pallas kernels, sigma_of(): pl.pallas_call(functools.partial(sigma_kernel, groups, per_energy, slots,...  12.1 us
    unnamed x11, local copies, waits for them, and re-layouts  3.05 us
    pallas_call x1, Pallas kernels, place(): pl.pallas_call(functools.partial(place_kernel, groups, cells, tiles, part...  2.01 us
    pallas_call x1, Pallas kernels, unpack(): pl.pallas_call(functools.partial(unpack_kernel, groups, tiles, parts), ou...  1.96 us
  transfers between devices with their start and end apart: 24, of which 8 were waited for; matrix products, arithmetic and copies ran while one was open for 0% of the time, Pallas kernels for 9%

profile of v2, /device:TPU:0, one launch (start us, length us, event | category | flops | bytes accessed | tf_op | source)
XLA Modules:
  0.0 82.9 jit_solution(16014001756297034466)
XLA Ops:
  0.1 1.1 %copy-done = bf16[4,6,2,16,512]{4,3,2,1,0:T(8,128)(2,1)S(1)} copy-done((bf16[4,6,2,16,512]{4,3,2,1,0:T(8,128)(2,1)S(1)}, bf16[4,6,2,16,512]{4,3,2,1,0:T(8,128)(2,1)}, u32[]{:S(2)}) %copy-start) | copy-done | bytes 786456
  1.2 1.1 %copy-done.1 = bf16[4,6,8,4,512]{4,3,2,1,0:T(4,128)(2,1)S(1)} copy-done((bf16[4,6,8,4,512]{4,3,2,1,0:T(4,128)(2,1)S(1)}, bf16[4,6,8,4,512]{4,3,2,1,0:T(4,128)(2,1)}, u32[]{:S(2)}) %copy-start.1) | copy-done | bytes 786456
  3.8 3.0 %collective-permute-start.7 = (bf16[4,6,2,4,512]{4,3,2,1,0:T(4,128)(2,1)S(1)}, bf16[4,6,2,4,512]{4,3,2,1,0:T(4,128)(2,1)S(1)}, u32[]{:S(2)}, u32[]{:S(2)}) collective-permute-start(bf16[4,6,2,4,512]{4,3,2,1,0:T(4,128)(2,1)S(1)} %get-tuple-element.42), channel_id=1, source_target_pairs={{0,1},{1,0},{2,3},{3,2},{4,5},{5,4},{6,7},{7,6},{8,9},{9,8},{10,11... | collective-permute-start | bytes 589832 | tf_op jit(solution)/shard_map/ppermute | solution.py:241
  6.8 1.5 %collective-permute-start.8 = (bf16[4,6,2,4,512]{4,3,2,1,0:T(4,128)(2,1)S(1)}, bf16[4,6,2,4,512]{4,3,2,1,0:T(4,128)(2,1)S(1)}, u32[]{:S(2)}, u32[]{:S(2)}) collective-permute-start(bf16[4,6,2,4,512]{4,3,2,1,0:T(4,128)(2,1)S(1)} %get-tuple-element.43), channel_id=1, source_target_pairs={{0,2},{1,3},{2,0},{3,1},{4,6},{5,7},{6,4},{7,5},{8,10},{9,11},{10,... | collective-permute-start | bytes 589832 | tf_op jit(solution)/shard_map/ppermute | solution.py:241
  8.4 2.0 %collective-permute-start.1 = (bf16[4,6,16,128]{3,2,1,0:T(8,128)(2,1)S(1)}, bf16[4,6,16,128]{3,2,1,0:T(8,128)(2,1)S(1)}, u32[]{:S(2)}, u32[]{:S(2)}) collective-permute-start(bf16[4,6,16,128]{3,2,1,0:T(8,128)(2,1)S(1)} %get-tuple-element.35), channel_id=1, source_target_pairs={{0,8},{4,12},{8,0},{12,4},{16,24},{20,28},{24,16},{28,20},{1,9},{5... | collective-permute-start | bytes 294920 | tf_op jit(solution)/shard_map/ppermute | solution.py:241
  10.4 2.2 %collective-permute-done.7.refs_1_ = bf16[4,6,2,4,512]{4,3,2,1,0:T(4,128)(2,1)S(1)} collective-permute-done((bf16[4,6,2,4,512]{4,3,2,1,0:T(4,128)(2,1)S(1)}, bf16[4,6,2,4,512]{4,3,2,1,0:T(4,128)(2,1)S(1)}, u32[]{:S(2)}, u32[]{:S(2)}) %collective-permute-start.7) | collective-permute-done | bytes 196640 | tf_op jit(solution)/shard_map/ppermute | solution.py:241
  12.6 4.8 %collective-permute-done.8.refs_2_ = bf16[4,6,2,4,512]{4,3,2,1,0:T(4,128)(2,1)S(1)} collective-permute-done((bf16[4,6,2,4,512]{4,3,2,1,0:T(4,128)(2,1)S(1)}, bf16[4,6,2,4,512]{4,3,2,1,0:T(4,128)(2,1)S(1)}, u32[]{:S(2)}, u32[]{:S(2)}) %collective-permute-start.8) | collective-permute-done | bytes 196640 | tf_op jit(solution)/shard_map/ppermute | solution.py:241
  17.4 2.6 %collective-permute-start.3 = (bf16[4,6,16,128]{3,2,1,0:T(8,128)(2,1)S(1)}, bf16[4,6,16,128]{3,2,1,0:T(8,128)(2,1)S(1)}, u32[]{:S(2)}, u32[]{:S(2)}) collective-permute-start(bf16[4,6,16,128]{3,2,1,0:T(8,128)(2,1)S(1)} %get-tuple-element.37), channel_id=1, source_target_pairs={{0,16},{4,20},{8,24},{12,28},{16,0},{20,4},{24,8},{28,12},{1,17},{... | collective-permute-start | bytes 294920 | tf_op jit(solution)/shard_map/ppermute | solution.py:241
  20.0 2.0 %place.1 = (bf16[4,6,16,128]{3,2,1,0:T(8,128)(2,1)S(1)}, bf16[4,6,16,128]{3,2,1,0:T(8,128)(2,1)S(1)}, bf16[4,6,16,128]{3,2,1,0:T(8,128)(2,1)S(1)}, bf16[4,6,16,1...) custom-call(s32[2]{0:T(128)S(1)} %pad_add_fusion.me_ref, ...), custom_call_target="tpu_custom_call" | custom-call | tf_op jit(solution)/shard_map/place/pallas_call | solution.py:97
  22.0 1.4 %collective-permute-start.5 = (bf16[4,6,16,128]{3,2,1,0:T(8,128)(2,1)S(1)}, bf16[4,6,16,128]{3,2,1,0:T(8,128)(2,1)S(1)}, u32[]{:S(2)}, u32[]{:S(2)}) collective-permute-start(bf16[4,6,16,128]{3,2,1,0:T(8,128)(2,1)S(1)} %get-tuple-element.39), channel_id=1, source_target_pairs={{0,24},{4,28},{8,16},{12,20},{16,8},{20,12},{24,0},{28,4},{1,25},{... | collective-permute-start | bytes 294920 | tf_op jit(solution)/shard_map/ppermute | solution.py:241
  23.5 2.4 %collective-permute-start.6 = (bf16[4,6,16,128]{3,2,1,0:T(8,128)(2,1)S(1)}, bf16[4,6,16,128]{3,2,1,0:T(8,128)(2,1)S(1)}, u32[]{:S(2)}, u32[]{:S(2)}) collective-permute-start(bf16[4,6,16,128]{3,2,1,0:T(8,128)(2,1)S(1)} %get-tuple-element.40), channel_id=1, source_target_pairs={{0,28},{4,24},{8,20},{12,16},{16,12},{20,8},{24,4},{28,0},{1,29},{... | collective-permute-start | bytes 294920 | tf_op jit(solution)/shard_map/ppermute | solution.py:241
  26.1 5.8 %collective-permute-start.11 = (bf16[4,6,16,128]{3,2,1,0:T(8,128)(2,1)S(1)}, bf16[4,6,16,128]{3,2,1,0:T(8,128)(2,1)S(1)}, u32[]{:S(2)}, u32[]{:S(2)}) collective-permute-start(bf16[4,6,16,128]{3,2,1,0:T(8,128)(2,1)S(1)} %get-tuple-element.47), channel_id=1, source_target_pairs={{0,8},{4,12},{8,0},{12,4},{16,24},{20,28},{24,16},{28,20},{1,9},{5... | collective-permute-start | bytes 294920 | tf_op jit(solution)/shard_map/ppermute | solution.py:241
  32.2 5.8 %collective-permute-start.13 = (bf16[4,6,16,128]{3,2,1,0:T(8,128)(2,1)S(1)}, bf16[4,6,16,128]{3,2,1,0:T(8,128)(2,1)S(1)}, u32[]{:S(2)}, u32[]{:S(2)}) collective-permute-start(bf16[4,6,16,128]{3,2,1,0:T(8,128)(2,1)S(1)} %get-tuple-element.49), channel_id=1, source_target_pairs={{0,16},{4,20},{8,24},{12,28},{16,0},{20,4},{24,8},{28,12},{1,17},{... | collective-permute-start | bytes 294920 | tf_op jit(solution)/shard_map/ppermute | solution.py:241
  39.2 2.1 %collective-permute-start.16 = (bf16[4,6,16,128]{3,2,1,0:T(8,128)(2,1)S(1)}, bf16[4,6,16,128]{3,2,1,0:T(8,128)(2,1)S(1)}, u32[]{:S(2)}, u32[]{:S(2)}) collective-permute-start(bf16[4,6,16,128]{3,2,1,0:T(8,128)(2,1)S(1)} %get-tuple-element.52), channel_id=1, source_target_pairs={{0,28},{4,24},{8,20},{12,16},{16,12},{20,8},{24,4},{28,0},{1,29},{... | collective-permute-start | bytes 294920 | tf_op jit(solution)/shard_map/ppermute | solution.py:241
  41.4 8.4 %collective-permute-done.13.refs_12_ = bf16[4,6,16,128]{3,2,1,0:T(8,128)(2,1)S(1)} collective-permute-done((bf16[4,6,16,128]{3,2,1,0:T(8,128)(2,1)S(1)}, bf16[4,6,16,128]{3,2,1,0:T(8,128)(2,1)S(1)}, u32[]{:S(2)}, u32[]{:S(2)}) %collective-permute-start.13) | collective-permute-done | bytes 98336 | tf_op jit(solution)/shard_map/ppermute | solution.py:241
  50.1 7.0 %sigma.3 = (s16[25,16,128]{2,1,0:T(8,128)(2,1)S(1)}, s16[25,16,128]{2,1,0:T(8,128)(2,1)S(1)}, s16[25,16,128]{2,1,0:T(8,128)(2,1)S(1)}, s16[25,16,128]{2,1,0:T(8,128)(2,1)S(1)}) custom-call(s32[2]{0:T(128)S(1)} %pad_add_fusion.me_ref, s32[64,3]{1,0:T(8,128)S(1)} %bitcast.3, s32[8,8]{1,0:T(8,128)S(1)} %copy-done.2, ...), custom_call_target="tpu_custom_call" | custom-call | tf_op jit(solution)/shard_map/sigma/pallas_call | solution.py:189
  57.1 4.1 %collective-permute-start.20 = (s16[25,16,128]{2,1,0:T(8,128)(2,1)S(1)}, s16[25,16,128]{2,1,0:T(8,128)(2,1)S(1)}, u32[]{:S(2)}, u32[]{:S(2)}) collective-permute-start(s16[25,16,128]{2,1,0:T(8,128)(2,1)S(1)} %get-tuple-element.57), channel_id=1, source_target_pairs={{0,16},{4,20},{8,24},{12,28},{16,0},{20,4},{24,8},{28,12},{1,17},{... | collective-permute-start | bytes 307208 | tf_op jit(solution)/shard_map/ppermute | solution.py:241
  61.2 3.5 %collective-permute-start.22 = (s16[25,16,128]{2,1,0:T(8,128)(2,1)S(1)}, s16[25,16,128]{2,1,0:T(8,128)(2,1)S(1)}, u32[]{:S(2)}, u32[]{:S(2)}) collective-permute-start(s16[25,16,128]{2,1,0:T(8,128)(2,1)S(1)} %get-tuple-element.59), channel_id=1, source_target_pairs={{0,24},{4,28},{8,16},{12,20},{16,8},{20,12},{24,0},{28,4},{1,25},{... | collective-permute-start | bytes 307208 | tf_op jit(solution)/shard_map/ppermute | solution.py:241
  64.7 5.1 %sigma.2 = (f32[4,6,16,128]{3,2,1,0:T(8,128)S(1)}, s16[25,16,128]{2,1,0:T(8,128)(2,1)S(1)}, s16[25,16,128]{2,1,0:T(8,128)(2,1)S(1)}, s16[25,16,128]{2,1,0:T(8,128)(2,1)S(1)}) custom-call(s32[2]{0:T(128)S(1)} %pad_add_fusion.me_ref, s32[64,3]{1,0:T(8,128)S(1)} %bitcast.4, s32[8,8]{1,0:T(8,128)S(1)} %copy-done.2, ...), custom_call_target="tpu_custom_call" | custom-call | tf_op jit(solution)/shard_map/sigma/pallas_call | solution.py:189
  70.3 3.2 %collective-permute-start.18 = (s16[25,16,128]{2,1,0:T(8,128)(2,1)S(1)}, s16[25,16,128]{2,1,0:T(8,128)(2,1)S(1)}, u32[]{:S(2)}, u32[]{:S(2)}) collective-permute-start(s16[25,16,128]{2,1,0:T(8,128)(2,1)S(1)} %get-tuple-element.55), channel_id=1, source_target_pairs={{0,8},{4,12},{8,0},{12,4},{16,24},{20,28},{24,16},{28,20},{1,9},{5... | collective-permute-start | bytes 307208 | tf_op jit(solution)/shard_map/ppermute | solution.py:241
  73.5 2.5 %collective-permute-done.21.refs_5_ = s16[25,16,128]{2,1,0:T(8,128)(2,1)S(1)} collective-permute-done((s16[25,16,128]{2,1,0:T(8,128)(2,1)S(1)}, s16[25,16,128]{2,1,0:T(8,128)(2,1)S(1)}, u32[]{:S(2)}, u32[]{:S(2)}) %collective-permute-start.21) | collective-permute-done | bytes 102432 | tf_op jit(solution)/shard_map/ppermute | solution.py:241
  76.1 1.9 %collective-permute-done.18.refs_2_ = s16[25,16,128]{2,1,0:T(8,128)(2,1)S(1)} collective-permute-done((s16[25,16,128]{2,1,0:T(8,128)(2,1)S(1)}, s16[25,16,128]{2,1,0:T(8,128)(2,1)S(1)}, u32[]{:S(2)}, u32[]{:S(2)}) %collective-permute-start.18) | collective-permute-done | bytes 102432 | tf_op jit(solution)/shard_map/ppermute | solution.py:241
  77.9 3.0 %collective-permute-done.19.refs_3_ = s16[25,16,128]{2,1,0:T(8,128)(2,1)S(1)} collective-permute-done((s16[25,16,128]{2,1,0:T(8,128)(2,1)S(1)}, s16[25,16,128]{2,1,0:T(8,128)(2,1)S(1)}, u32[]{:S(2)}, u32[]{:S(2)}) %collective-permute-start.19) | collective-permute-done | bytes 102432 | tf_op jit(solution)/shard_map/ppermute | solution.py:241
  80.9 2.0 %unpack.1 = f32[4,6,2,16,512]{4,3,2,1,0:T(8,128)} custom-call(s32[2]{0:T(128)S(1)} %pad_add_fusion.me_ref, f32[4,6,16,128]{3,2,1,0:T(8,128)S(1)} %get-tuple-element.53.refs_0_, s16[25,16,128]{2,1,0:T(8,128)(2,1)S(1)} %collective-permute-done.17.refs_1_, s16[25,16,128]{2,1,0:T(8,128)(2,1)S(1)} %collective-permute-done.18.refs_2_, ...), custom_call_target="tpu_custom_call" | custom-call | tf_op jit(solution)/shard_map/unpack/pallas_call | solution.py:230
  (41 shorter events, 4.2 us)
Async XLA Ops:
  3.8 8.7 %collective-permute-start.7 = (bf16[4,6,2,4,512]{4,3,2,1,0:T(4,128)(2,1)S(1)}, bf16[4,6,2,4,512]{4,3,2,1,0:T(4,128)(2,1)S(1)}, u32[]{:S(2)}, u32[]{:S(2)}) collective-permute-start(bf16[4,6,2,4,512]{4,3,2,1,0:T(4,128)(2,1)S(1)} %get-tuple-element.42), channel_id=1, source_target_pairs={{0,1},{1,0},{2,3},{3,2},{4,5},{5,4},{6,7},{7,6},{8,9},{9,8},{10,11... | collective-permute-start | bytes 589832 | tf_op jit(solution)/shard_map/ppermute | solution.py:241
  6.8 10.6 %collective-permute-start.8 = (bf16[4,6,2,4,512]{4,3,2,1,0:T(4,128)(2,1)S(1)}, bf16[4,6,2,4,512]{4,3,2,1,0:T(4,128)(2,1)S(1)}, u32[]{:S(2)}, u32[]{:S(2)}) collective-permute-start(bf16[4,6,2,4,512]{4,3,2,1,0:T(4,128)(2,1)S(1)} %get-tuple-element.43), channel_id=1, source_target_pairs={{0,2},{1,3},{2,0},{3,1},{4,6},{5,7},{6,4},{7,5},{8,10},{9,11},{10,... | collective-permute-start | bytes 589832 | tf_op jit(solution)/shard_map/ppermute | solution.py:241
  8.4 11.6 %collective-permute-start.9 = (bf16[4,6,2,4,512]{4,3,2,1,0:T(4,128)(2,1)S(1)}, bf16[4,6,2,4,512]{4,3,2,1,0:T(4,128)(2,1)S(1)}, u32[]{:S(2)}, u32[]{:S(2)}) collective-permute-start(bf16[4,6,2,4,512]{4,3,2,1,0:T(4,128)(2,1)S(1)} %get-tuple-element.44), channel_id=1, source_target_pairs={{0,3},{1,2},{2,1},{3,0},{4,7},{5,6},{6,5},{7,4},{8,11},{9,10},{10,... | collective-permute-start | bytes 589832 | tf_op jit(solution)/shard_map/ppermute | solution.py:241
  8.4 13.6 %collective-permute-start = (bf16[4,6,16,128]{3,2,1,0:T(8,128)(2,1)S(1)}, bf16[4,6,16,128]{3,2,1,0:T(8,128)(2,1)S(1)}, u32[]{:S(2)}, u32[]{:S(2)}) collective-permute-start(bf16[4,6,16,128]{3,2,1,0:T(8,128)(2,1)S(1)} %get-tuple-element.34), channel_id=1, source_target_pairs={{0,4},{4,0},{8,12},{12,8},{16,20},{20,16},{24,28},{28,24},{1,5},{5... | collective-permute-start | bytes 294920 | tf_op jit(solution)/shard_map/ppermute | solution.py:241
  8.4 15.1 %collective-permute-start.1 = (bf16[4,6,16,128]{3,2,1,0:T(8,128)(2,1)S(1)}, bf16[4,6,16,128]{3,2,1,0:T(8,128)(2,1)S(1)}, u32[]{:S(2)}, u32[]{:S(2)}) collective-permute-start(bf16[4,6,16,128]{3,2,1,0:T(8,128)(2,1)S(1)} %get-tuple-element.35), channel_id=1, source_target_pairs={{0,8},{4,12},{8,0},{12,4},{16,24},{20,28},{24,16},{28,20},{1,9},{5... | collective-permute-start | bytes 294920 | tf_op jit(solution)/shard_map/ppermute | solution.py:241
  12.6 13.3 %collective-permute-start.2 = (bf16[4,6,16,128]{3,2,1,0:T(8,128)(2,1)S(1)}, bf16[4,6,16,128]{3,2,1,0:T(8,128)(2,1)S(1)}, u32[]{:S(2)}, u32[]{:S(2)}) collective-permute-start(bf16[4,6,16,128]{3,2,1,0:T(8,128)(2,1)S(1)} %get-tuple-element.36), channel_id=1, source_target_pairs={{0,12},{4,8},{8,4},{12,0},{16,28},{20,24},{24,20},{28,16},{1,13},{... | collective-permute-start | bytes 294920 | tf_op jit(solution)/shard_map/ppermute | solution.py:241
  17.4 8.6 %collective-permute-start.3 = (bf16[4,6,16,128]{3,2,1,0:T(8,128)(2,1)S(1)}, bf16[4,6,16,128]{3,2,1,0:T(8,128)(2,1)S(1)}, u32[]{:S(2)}, u32[]{:S(2)}) collective-permute-start(bf16[4,6,16,128]{3,2,1,0:T(8,128)(2,1)S(1)} %get-tuple-element.37), channel_id=1, source_target_pairs={{0,16},{4,20},{8,24},{12,28},{16,0},{20,4},{24,8},{28,12},{1,17},{... | collective-permute-start | bytes 294920 | tf_op jit(solution)/shard_map/ppermute | solution.py:241
  20.0 12.2 %collective-permute-start.4 = (bf16[4,6,16,128]{3,2,1,0:T(8,128)(2,1)S(1)}, bf16[4,6,16,128]{3,2,1,0:T(8,128)(2,1)S(1)}, u32[]{:S(2)}, u32[]{:S(2)}) collective-permute-start(bf16[4,6,16,128]{3,2,1,0:T(8,128)(2,1)S(1)} %get-tuple-element.38), channel_id=1, source_target_pairs={{0,20},{4,16},{8,28},{12,24},{16,4},{20,0},{24,12},{28,8},{1,21},{... | collective-permute-start | bytes 294920 | tf_op jit(solution)/shard_map/ppermute | solution.py:241
  22.0 10.2 %collective-permute-start.5 = (bf16[4,6,16,128]{3,2,1,0:T(8,128)(2,1)S(1)}, bf16[4,6,16,128]{3,2,1,0:T(8,128)(2,1)S(1)}, u32[]{:S(2)}, u32[]{:S(2)}) collective-permute-start(bf16[4,6,16,128]{3,2,1,0:T(8,128)(2,1)S(1)} %get-tuple-element.39), channel_id=1, source_target_pairs={{0,24},{4,28},{8,16},{12,20},{16,8},{20,12},{24,0},{28,4},{1,25},{... | collective-permute-start | bytes 294920 | tf_op jit(solution)/shard_map/ppermute | solution.py:241
  23.5 14.5 %collective-permute-start.6 = (bf16[4,6,16,128]{3,2,1,0:T(8,128)(2,1)S(1)}, bf16[4,6,16,128]{3,2,1,0:T(8,128)(2,1)S(1)}, u32[]{:S(2)}, u32[]{:S(2)}) collective-permute-start(bf16[4,6,16,128]{3,2,1,0:T(8,128)(2,1)S(1)} %get-tuple-element.40), channel_id=1, source_target_pairs={{0,28},{4,24},{8,20},{12,16},{16,12},{20,8},{24,4},{28,0},{1,29},{... | collective-permute-start | bytes 294920 | tf_op jit(solution)/shard_map/ppermute | solution.py:241
  25.9 12.9 %collective-permute-start.10 = (bf16[4,6,16,128]{3,2,1,0:T(8,128)(2,1)S(1)}, bf16[4,6,16,128]{3,2,1,0:T(8,128)(2,1)S(1)}, u32[]{:S(2)}, u32[]{:S(2)}) collective-permute-start(bf16[4,6,16,128]{3,2,1,0:T(8,128)(2,1)S(1)} %get-tuple-element.46), channel_id=1, source_target_pairs={{0,4},{4,0},{8,12},{12,8},{16,20},{20,16},{24,28},{28,24},{1,5},{5... | collective-permute-start | bytes 294920 | tf_op jit(solution)/shard_map/ppermute | solution.py:241
  26.1 13.1 %collective-permute-start.11 = (bf16[4,6,16,128]{3,2,1,0:T(8,128)(2,1)S(1)}, bf16[4,6,16,128]{3,2,1,0:T(8,128)(2,1)S(1)}, u32[]{:S(2)}, u32[]{:S(2)}) collective-permute-start(bf16[4,6,16,128]{3,2,1,0:T(8,128)(2,1)S(1)} %get-tuple-element.47), channel_id=1, source_target_pairs={{0,8},{4,12},{8,0},{12,4},{16,24},{20,28},{24,16},{28,20},{1,9},{5... | collective-permute-start | bytes 294920 | tf_op jit(solution)/shard_map/ppermute | solution.py:241
  32.2 9.2 %collective-permute-start.12 = (bf16[4,6,16,128]{3,2,1,0:T(8,128)(2,1)S(1)}, bf16[4,6,16,128]{3,2,1,0:T(8,128)(2,1)S(1)}, u32[]{:S(2)}, u32[]{:S(2)}) collective-permute-start(bf16[4,6,16,128]{3,2,1,0:T(8,128)(2,1)S(1)} %get-tuple-element.48), channel_id=1, source_target_pairs={{0,12},{4,8},{8,4},{12,0},{16,28},{20,24},{24,20},{28,16},{1,13},{... | collective-permute-start | bytes 294920 | tf_op jit(solution)/shard_map/ppermute | solution.py:241
  32.2 17.6 %collective-permute-start.13 = (bf16[4,6,16,128]{3,2,1,0:T(8,128)(2,1)S(1)}, bf16[4,6,16,128]{3,2,1,0:T(8,128)(2,1)S(1)}, u32[]{:S(2)}, u32[]{:S(2)}) collective-permute-start(bf16[4,6,16,128]{3,2,1,0:T(8,128)(2,1)S(1)} %get-tuple-element.49), channel_id=1, source_target_pairs={{0,16},{4,20},{8,24},{12,28},{16,0},{20,4},{24,8},{28,12},{1,17},{... | collective-permute-start | bytes 294920 | tf_op jit(solution)/shard_map/ppermute | solution.py:241
  38.0 12.1 %collective-permute-start.14 = (bf16[4,6,16,128]{3,2,1,0:T(8,128)(2,1)S(1)}, bf16[4,6,16,128]{3,2,1,0:T(8,128)(2,1)S(1)}, u32[]{:S(2)}, u32[]{:S(2)}) collective-permute-start(bf16[4,6,16,128]{3,2,1,0:T(8,128)(2,1)S(1)} %get-tuple-element.50), channel_id=1, source_target_pairs={{0,20},{4,16},{8,28},{12,24},{16,4},{20,0},{24,12},{28,8},{1,21},{... | collective-permute-start | bytes 294920 | tf_op jit(solution)/shard_map/ppermute | solution.py:241
  38.8 11.3 %collective-permute-start.15 = (bf16[4,6,16,128]{3,2,1,0:T(8,128)(2,1)S(1)}, bf16[4,6,16,128]{3,2,1,0:T(8,128)(2,1)S(1)}, u32[]{:S(2)}, u32[]{:S(2)}) collective-permute-start(bf16[4,6,16,128]{3,2,1,0:T(8,128)(2,1)S(1)} %get-tuple-element.51), channel_id=1, source_target_pairs={{0,24},{4,28},{8,16},{12,20},{16,8},{20,12},{24,0},{28,4},{1,25},{... | collective-permute-start | bytes 294920 | tf_op jit(solution)/shard_map/ppermute | solution.py:241
  39.2 10.9 %collective-permute-start.16 = (bf16[4,6,16,128]{3,2,1,0:T(8,128)(2,1)S(1)}, bf16[4,6,16,128]{3,2,1,0:T(8,128)(2,1)S(1)}, u32[]{:S(2)}, u32[]{:S(2)}) collective-permute-start(bf16[4,6,16,128]{3,2,1,0:T(8,128)(2,1)S(1)} %get-tuple-element.52), channel_id=1, source_target_pairs={{0,28},{4,24},{8,20},{12,16},{16,12},{20,8},{24,4},{28,0},{1,29},{... | collective-permute-start | bytes 294920 | tf_op jit(solution)/shard_map/ppermute | solution.py:241
  57.1 13.2 %collective-permute-start.20 = (s16[25,16,128]{2,1,0:T(8,128)(2,1)S(1)}, s16[25,16,128]{2,1,0:T(8,128)(2,1)S(1)}, u32[]{:S(2)}, u32[]{:S(2)}) collective-permute-start(s16[25,16,128]{2,1,0:T(8,128)(2,1)S(1)} %get-tuple-element.57), channel_id=1, source_target_pairs={{0,16},{4,20},{8,24},{12,28},{16,0},{20,4},{24,8},{28,12},{1,17},{... | collective-permute-start | bytes 307208 | tf_op jit(solution)/shard_map/ppermute | solution.py:241
  61.2 14.9 %collective-permute-start.21 = (s16[25,16,128]{2,1,0:T(8,128)(2,1)S(1)}, s16[25,16,128]{2,1,0:T(8,128)(2,1)S(1)}, u32[]{:S(2)}, u32[]{:S(2)}) collective-permute-start(s16[25,16,128]{2,1,0:T(8,128)(2,1)S(1)} %get-tuple-element.58), channel_id=1, source_target_pairs={{0,20},{4,16},{8,28},{12,24},{16,4},{20,0},{24,12},{28,8},{1,21},{... | collective-permute-start | bytes 307208 | tf_op jit(solution)/shard_map/ppermute | solution.py:241
  61.2 14.9 %collective-permute-start.22 = (s16[25,16,128]{2,1,0:T(8,128)(2,1)S(1)}, s16[25,16,128]{2,1,0:T(8,128)(2,1)S(1)}, u32[]{:S(2)}, u32[]{:S(2)}) collective-permute-start(s16[25,16,128]{2,1,0:T(8,128)(2,1)S(1)} %get-tuple-element.59), channel_id=1, source_target_pairs={{0,24},{4,28},{8,16},{12,20},{16,8},{20,12},{24,0},{28,4},{1,25},{... | collective-permute-start | bytes 307208 | tf_op jit(solution)/shard_map/ppermute | solution.py:241
  64.7 11.3 %collective-permute-start.23 = (s16[25,16,128]{2,1,0:T(8,128)(2,1)S(1)}, s16[25,16,128]{2,1,0:T(8,128)(2,1)S(1)}, u32[]{:S(2)}, u32[]{:S(2)}) collective-permute-start(s16[25,16,128]{2,1,0:T(8,128)(2,1)S(1)} %get-tuple-element.60), channel_id=1, source_target_pairs={{0,28},{4,24},{8,20},{12,16},{16,12},{20,8},{24,4},{28,0},{1,29},{... | collective-permute-start | bytes 307208 | tf_op jit(solution)/shard_map/ppermute | solution.py:241
  69.8 6.2 %collective-permute-start.17 = (s16[25,16,128]{2,1,0:T(8,128)(2,1)S(1)}, s16[25,16,128]{2,1,0:T(8,128)(2,1)S(1)}, u32[]{:S(2)}, u32[]{:S(2)}) collective-permute-start(s16[25,16,128]{2,1,0:T(8,128)(2,1)S(1)} %get-tuple-element.54), channel_id=1, source_target_pairs={{0,4},{4,0},{8,12},{12,8},{16,20},{20,16},{24,28},{28,24},{1,5},{5... | collective-permute-start | bytes 307208 | tf_op jit(solution)/shard_map/ppermute | solution.py:241
  70.3 7.6 %collective-permute-start.18 = (s16[25,16,128]{2,1,0:T(8,128)(2,1)S(1)}, s16[25,16,128]{2,1,0:T(8,128)(2,1)S(1)}, u32[]{:S(2)}, u32[]{:S(2)}) collective-permute-start(s16[25,16,128]{2,1,0:T(8,128)(2,1)S(1)} %get-tuple-element.55), channel_id=1, source_target_pairs={{0,8},{4,12},{8,0},{12,4},{16,24},{20,28},{24,16},{28,20},{1,9},{5... | collective-permute-start | bytes 307208 | tf_op jit(solution)/shard_map/ppermute | solution.py:241
  76.1 4.8 %collective-permute-start.19 = (s16[25,16,128]{2,1,0:T(8,128)(2,1)S(1)}, s16[25,16,128]{2,1,0:T(8,128)(2,1)S(1)}, u32[]{:S(2)}, u32[]{:S(2)}) collective-permute-start(s16[25,16,128]{2,1,0:T(8,128)(2,1)S(1)} %get-tuple-element.56), channel_id=1, source_target_pairs={{0,12},{4,8},{8,4},{12,0},{16,28},{20,24},{24,20},{28,16},{1,13},{... | collective-permute-start | bytes 307208 | tf_op jit(solution)/shard_map/ppermute | solution.py:241
  (5 other events, 94.3 us)

commit v3 on v0

v3 whole, which is shorter than its diff:
```python
import functools

import jax
import jax.numpy as jnp
from jax import lax
from jax.experimental import pallas as pl
from jax.experimental.pallas import tpu as pltpu
from jax.sharding import PartitionSpec as P

SCALE = 0.2
LANES = 128
PAIR = 2
STEPS = 32700.0
FINE = 64.0
TINY = 1e-34
SMEM = pl.BlockSpec(memory_space=pltpu.SMEM)
VMEM = pl.BlockSpec(memory_space=pltpu.VMEM)
HBM = pl.BlockSpec(memory_space=pltpu.HBM)
PARAMS = pltpu.CompilerParams(vmem_limit_bytes=32 * 1024 * 1024)


class Sizes:
    def __init__(self, green, screened, groups, cells):
        self.comps, self.energies, self.per_cell, self.rows, self.width = green.shape
        self.groups, self.cells = groups, cells
        self.tiles = self.width // LANES
        self.slices = groups // self.per_cell
        self.parts = self.slices // self.tiles
        self.held = screened.shape[3]
        self.plane = (self.rows // self.parts, LANES)
        self.planes = self.comps * self.energies
        self.scales = self.planes // PAIR
        self.scale_planes = -(-self.scales // self.plane[0])

    def where(self, index):
        cell, tile, part = index // self.slices, (index // self.parts) % self.tiles, index % self.parts
        return cell, part, pl.ds(pl.multiple_of(tile * LANES, LANES), LANES)


def part_of(s, value, part):
    count = value.shape[0] // s.parts
    chosen = value[:count]
    for other in range(1, s.parts):
        chosen = jnp.where(part == other, value[other * count : (other + 1) * count], chosen)
    return chosen


def pick_kernel(s, map_ref, screened_ref, out_ref):
    for column in range(s.cells):
        for q in range(s.per_cell):
            cell = map_ref[column * s.per_cell + q]
            for t in range(s.tiles):
                target = (q * s.slices + t) * s.cells + column
                for comp in range(s.comps):
                    for j in range(s.energies):
                        part = screened_ref[comp, j, cell, :, t * LANES : (t + 1) * LANES]
                        out_ref[target, comp * s.energies + j] = part


def pick_screened(s, cell_map, screened):
    shape = (s.groups * s.cells, s.planes, s.held, LANES)
    return pl.pallas_call(
        functools.partial(pick_kernel, s),
        out_shape=jax.ShapeDtypeStruct(shape, screened.dtype),
        in_specs=[SMEM, VMEM],
        out_specs=VMEM,
        compiler_params=PARAMS,
        name="pick_screened",
    )(cell_map, screened)


def cut_kernel(s, me_ref, green_ref, *greens):
    me = me_ref[0]
    for k in range(s.groups):
        cell, part, lanes = s.where(me ^ k)
        for comp in range(s.comps):
            for j in range(s.energies):
                if s.parts == 1:
                    greens[k][comp * s.energies + j] = green_ref[comp, j, cell, :, lanes]
                else:
                    value = green_ref[comp, j, cell, :, lanes].astype(jnp.float32)
                    greens[k][comp * s.energies + j] = part_of(s, value, part).astype(greens[k].dtype)


def cut_green(s, me, green):
    return pl.pallas_call(
        functools.partial(cut_kernel, s),
        out_shape=[jax.ShapeDtypeStruct((s.planes,) + s.plane, green.dtype)] * s.groups,
        in_specs=[SMEM, VMEM],
        out_specs=[VMEM] * s.groups,
        compiler_params=PARAMS,
        name="cut_green",
    )(me, green)


def stage_kernel(s, me_ref, screens_ref, *refs):
    greens = refs[: s.groups]
    g_all, w_all = refs[s.groups :]
    me = me_ref[0]
    zero = jnp.zeros(s.plane, jnp.float32)
    for comp in range(s.comps):
        for j in range(s.energies):
            plane = comp * s.energies + j
            g_all[comp, j] = zero
            for k in range(s.groups):
                g_all[comp, ((me ^ k) + 1) * s.energies + j] = greens[k][plane].astype(jnp.float32)
            for source in range(s.groups):
                if s.parts > 1:
                    w_all[source, comp, j] = screens_ref[source, plane].astype(jnp.float32)
                    continue
                for c in range(s.cells):
                    piece = screens_ref[source * s.cells + c, plane].astype(jnp.float32)
                    w_all[source, comp, j, c * s.held : (c + 1) * s.held, :] = piece


def stage(s, me, greens, screens):
    return pl.pallas_call(
        functools.partial(stage_kernel, s),
        out_shape=[
            jax.ShapeDtypeStruct((s.comps, (s.groups + 1) * s.energies) + s.plane, jnp.float32),
            jax.ShapeDtypeStruct((s.groups, s.comps, s.energies) + s.plane, jnp.float32),
        ],
        in_specs=[SMEM] + [VMEM] * (s.groups + 1),
        out_specs=[VMEM] * 2,
        compiler_params=PARAMS,
        name="stage",
    )(me, screens, *greens)


def sigma_kernel(s, slots, ks, me_ref, table_ref, count_ref, g_all, w_all, *outs):
    me = me_ref[0]
    row = lax.broadcasted_iota(jnp.int32, s.plane, 0)
    for at, k in enumerate(ks):
        group = me ^ k
        codes = [jnp.zeros(s.plane, jnp.float32) for _ in range(s.scale_planes)]
        for kind in range(2):

            def turn(source, sums):
                sums = list(sums)
                count = count_ref[group, source]
                for slot in range(slots):
                    shift = jnp.clip(table_ref[group * s.groups + source, slot], 0, s.energies - 1)
                    live = jnp.where(slot < count, 1.0, 0.0).astype(jnp.float32)
                    start = (group - source + 1) * s.energies - shift
                    w_real = w_all[source, 2 * kind, shift] * live
                    w_imag = w_all[source, 2 * kind + 1, shift] * live
                    for j in range(s.energies):
                        g_real = g_all[2 * kind, start + j]
                        g_imag = g_all[2 * kind + 1, start + j]
                        sums[j] = sums[j] - (g_real * w_imag + g_imag * w_real)
                        sums[s.energies + j] = sums[s.energies + j] + (g_real * w_real - g_imag * w_imag)
                return tuple(sums)

            zeros = tuple(jnp.zeros(s.plane, jnp.float32) for _ in range(2 * s.energies))
            sums = lax.fori_loop(0, group + 1, turn, zeros)
            sums = [total * SCALE for total in sums]
            first = kind * 2 * s.energies
            if k == 0:
                for j, total in enumerate(sums):
                    outs[at][first + j] = total
                continue
            for low in range(0, 2 * s.energies, PAIR):
                pair = sums[low : low + PAIR]
                largest = functools.reduce(jnp.maximum, [jnp.abs(total) for total in pair])
                largest = jnp.maximum(jnp.max(largest, axis=0, keepdims=True), TINY)
                code = jnp.ceil(jnp.log2(largest) * FINE)
                inverse = jnp.exp2(code * (-1.0 / FINE)) * STEPS
                where = (first + low) // PAIR
                spot = where // s.plane[0]
                codes[spot] = jnp.where(row == where % s.plane[0], code, codes[spot])
                for j, total in enumerate(pair):
                    coded = jnp.round(total * inverse).astype(jnp.int32)
                    outs[at][first + low + j] = coded.astype(jnp.int16)
        if k != 0:
            for j in range(s.scale_planes):
                outs[at][s.comps * s.energies + j] = codes[j].astype(jnp.int32).astype(jnp.int16)


def sigma_of(s, me, table, count, g_all, w_all, ks):
    slots = table.shape[-1]
    planes = s.comps * s.energies
    own = jax.ShapeDtypeStruct((planes,) + s.plane, jnp.float32)
    coded = jax.ShapeDtypeStruct((planes + s.scale_planes,) + s.plane, jnp.int16)
    return pl.pallas_call(
        functools.partial(sigma_kernel, s, slots, ks),
        out_shape=[own if k == 0 else coded for k in ks],
        in_specs=[SMEM] * 3 + [VMEM] * 2,
        out_specs=[VMEM] * len(ks),
        compiler_params=PARAMS,
        name="sigma",
    )(me, table.reshape(s.groups * s.groups, slots), count, g_all, w_all)


def unpack_kernel(s, me_ref, *refs):
    blocks, whole_ref = refs[: s.groups], refs[s.groups]
    me = me_ref[0]
    for k, block in enumerate(blocks):
        cell, part, lanes = s.where(me ^ k)
        rows = slice(None) if s.parts == 1 else pl.ds(pl.multiple_of(part * s.plane[0], s.plane[0]), s.plane[0])
        scales = []
        if k != 0:
            for j in range(s.scale_planes):
                code = block[s.planes + j].astype(jnp.int32).astype(jnp.float32)
                scales.append(jnp.exp2(code * (1.0 / FINE)) * (1.0 / STEPS))
        for comp in range(s.comps):
            for j in range(s.energies):
                plane = comp * s.energies + j
                value = block[plane]
                if k != 0:
                    where = plane // PAIR
                    scale = scales[where // s.plane[0]][where % s.plane[0] : where % s.plane[0] + 1]
                    value = value.astype(jnp.int32).astype(jnp.float32) * scale
                whole_ref[comp, j, cell, rows, lanes] = value


def unpack(s, me, blocks):
    return pl.pallas_call(
        functools.partial(unpack_kernel, s),
        out_shape=jax.ShapeDtypeStruct((s.comps, s.energies, s.per_cell, s.rows, s.width), jnp.float32),
        in_specs=[SMEM] + [VMEM] * s.groups,
        out_specs=VMEM,
        compiler_params=PARAMS,
        name="unpack",
    )(me, *blocks)


def swap(s, block, k):
    return block if k == 0 else lax.ppermute(block, "energy", [(i, i ^ k) for i in range(s.groups)])


def send_screened(s, cell_map, screened):
    if s.parts == 1:
        return lax.all_to_all(pick_screened(s, cell_map, screened), ("energy", "cell"), 0, 0, tiled=True)
    chosen = jnp.take(screened, cell_map, axis=2).reshape(s.planes, s.cells, s.per_cell, s.held, s.width)
    whole = lax.all_to_all(chosen, "cell", 1, 3, tiled=True)
    cut = whole.reshape(s.planes, s.per_cell, s.parts, s.plane[0], s.tiles, LANES)
    cut = jnp.transpose(cut, (1, 4, 2, 0, 3, 5)).reshape((s.groups, s.planes) + s.plane)
    return lax.all_to_all(cut, "energy", 0, 0, tiled=True)


def per_device(green, screened, cell_map, shift_table, shift_count):
    s = Sizes(green, screened, lax.axis_size("energy"), lax.axis_size("cell"))
    me = jnp.stack([lax.axis_index("energy"), lax.axis_index("cell")]).astype(jnp.int32)
    half = s.groups // 2
    far, near = list(range(half, s.groups)), list(range(half))

    screens = send_screened(s, cell_map, screened)
    greens = [swap(s, block, k) for k, block in enumerate(cut_green(s, me, green))]
    g_all, w_all = stage(s, me, greens, screens)
    sums = {}
    for ks in (far, near):
        for k, block in zip(ks, sigma_of(s, me, shift_table, shift_count, g_all, w_all, ks)):
            sums[k] = swap(s, block, k)
    return unpack(s, me, [sums[k] for k in range(s.groups)])


def solution(mesh):
    placed = (
        P(None, "energy", "cell", None, None),
        P(None, "energy", None, "cell", None),
        P(),
        P(),
        P(),
    )
    return jax.shard_map(
        per_device,
        mesh=mesh,
        in_specs=placed,
        out_specs=P(None, "energy", "cell", None, None),
        check_vma=False,
    )
```

time: 262 us -> 73.7 us (0.28)
  waiting for transfers between devices: 105 us -> 31.5 us
  loops' own time: 51.6 us -> 0 us
  other arithmetic: 38.7 us -> 0.08 us
  local copies, waits for them, and re-layouts: 35 us -> 1.92 us
  starting transfers between devices: 0.04 us -> 27.6 us
  blocking collectives: 16.3 us -> 0 us
  between operations: 13.5 us -> 0.08 us
  Pallas kernels: 0 us -> 12.2 us
    all_gather x2 -> x0, waiting for transfers between devices: 104 us -> none  [the longest x1 57.9 us: per_device(): every = lax.all_gather(owned, 'energy', axis=1, tiled=True)]
    another operation x1 -> x0, loops' own time: 51.6 us -> none  [per_device(): lax.scan(turn, (zeros, zeros, zeros, zeros), jnp.arange(groups, dtype=jnp...]
    ppermute x0 -> x14, waiting for transfers between devices: none -> 31.5 us  [swap(): lax.ppermute(block, 'energy', [(i, i ^ k) for i in range(s.groups)])]
    add x16 -> x0, other arithmetic: 28.3 us -> none  [turn(): sums[2 * kind + 1] + (g_real * w_real - g_imag * w_imag)]
    ppermute x0 -> x14, starting transfers between devices: none -> 20.3 us  [swap(): lax.ppermute(block, 'energy', [(i, i ^ k) for i in range(s.groups)])]
    all_to_all x1 -> x0, blocking collectives: 16.3 us -> none  [per_device(): lax.all_to_all(outgoing, 'cell', split_axis=3, concat_axis=3, tiled=True)]
    dynamic_slice x25 -> x0, local copies, waits for them, and re-layouts: 15 us -> none  [the longest x8 4.9 us: turn(): energy = source * per_energy + table_row[source, slot]]
    pallas_call x0 -> x6, Pallas kernels: none -> 12.2 us  [the longest x2 6.98 us: sigma_of(): pl.pallas_call(functools.partial(sigma_kernel, s, slots, ks), out_shape=[...]
  transfers between devices with their start and end apart: 2 -> 15, of which waited for: 2 -> 7; matrix products, arithmetic and copies ran while one was open for 5% -> 0% of each run, Pallas kernels for 0% -> 4%
where the time goes in v3:
time: 73.7 us; the launch traced here: 73.4 us
  waiting for transfers between devices  31.5 us (43%)
  starting transfers between devices  27.6 us (37%)
  Pallas kernels  12.2 us (17%)
  local copies, waits for them, and re-layouts  1.92 us (3%)
    ppermute x14, waiting for transfers between devices, swap(): lax.ppermute(block, 'energy', [(i, i ^ k) for i in range(s.groups)])  31.5 us
    ppermute x14, starting transfers between devices, swap(): lax.ppermute(block, 'energy', [(i, i ^ k) for i in range(s.groups)])  20.3 us
    all_to_all x1, starting transfers between devices, send_screened(): lax.all_to_all(pick_screened(s, cell_map, screened), ('energy', 'cell'),...  7.3 us
    pallas_call x2, Pallas kernels, sigma_of(): pl.pallas_call(functools.partial(sigma_kernel, s, slots, ks), out_shape=[...  6.98 us
    pallas_call x1, Pallas kernels, unpack(): pl.pallas_call(functools.partial(unpack_kernel, s), out_shape=jax.ShapeDt...  1.96 us
    unnamed x11, local copies, waits for them, and re-layouts  1.92 us
    pallas_call x1, Pallas kernels, pick_screened(): pl.pallas_call(functools.partial(pick_kernel, s), out_shape=jax.ShapeDtyp...  1.7 us
  transfers between devices with their start and end apart: 15, of which 7 were waited for; matrix products, arithmetic and copies ran while one was open for 0% of the time, Pallas kernels for 4%

profile of v3, /device:TPU:0, one launch (start us, length us, event | category | flops | bytes accessed | tf_op | source)
XLA Modules:
  0.0 73.4 jit_solution(16131677571064800395)
XLA Ops:
  0.0 1.1 %copy-done = bf16[4,6,8,4,512]{4,3,2,1,0:T(4,128)(2,1)S(1)} copy-done((bf16[4,6,8,4,512]{4,3,2,1,0:T(4,128)(2,1)S(1)}, bf16[4,6,8,4,512]{4,3,2,1,0:T(4,128)(2,1)}, u32[]{:S(2)}) %copy-start) | copy-done | bytes 786456
  1.1 0.7 copy-done.3
  1.8 1.7 %pick_screened.1 = bf16[32,24,4,128]{3,2,1,0:T(4,128)(2,1)} custom-call(s32[8]{0:T(128)S(1)} %copy-done.3, bf16[4,6,8,4,512]{4,3,2,1,0:T(4,128)(2,1)S(1)} %copy-done), custom_call_target="tpu_custom_call" | custom-call | tf_op jit(solution)/shard_map/pick_screened/pallas_call | solution.py:62
  3.5 7.3 %all-to-all-start = ((bf16[32,24,4,128]{3,2,1,0:T(4,128)(2,1)}), bf16[32,24,4,128]{3,2,1,0:T(4,128)(2,1)S(1)}, u32[]{:S(2)}, u32[]{:S(2)}) async-start(bf16[32,24,4,128]{3,2,1,0:T(4,128)(2,1)} %pick_screened.1), calls=%async_computation | async-start | bytes 1572864 | tf_op jit(solution)/shard_map/all_to_all | solution.py:233
  10.9 0.7 cut_green.1
  11.6 0.3 collective-permute-start
  11.9 1.7 %collective-permute-start.1 = (bf16[24,16,128]{2,1,0:T(8,128)(2,1)S(1)}, bf16[24,16,128]{2,1,0:T(8,128)(2,1)S(1)}, u32[]{:S(2)}, u32[]{:S(2)}) collective-permute-start(bf16[24,16,128]{2,1,0:T(8,128)(2,1)S(1)} %get-tuple-element.25), channel_id=1, source_target_pairs={{0,8},{4,12},{8,0},{12,4},{16,24},{20,28},{24,16},{28,20},{1,9},{5... | collective-permute-start | bytes 294920 | tf_op jit(solution)/shard_map/ppermute | solution.py:228
  13.6 2.6 %collective-permute-start.3 = (bf16[24,16,128]{2,1,0:T(8,128)(2,1)S(1)}, bf16[24,16,128]{2,1,0:T(8,128)(2,1)S(1)}, u32[]{:S(2)}, u32[]{:S(2)}) collective-permute-start(bf16[24,16,128]{2,1,0:T(8,128)(2,1)S(1)} %get-tuple-element.27), channel_id=1, source_target_pairs={{0,16},{4,20},{8,24},{12,28},{16,0},{20,4},{24,8},{28,12},{1,17},{... | collective-permute-start | bytes 294920 | tf_op jit(solution)/shard_map/ppermute | solution.py:228
  16.3 3.5 %collective-permute-start.5 = (bf16[24,16,128]{2,1,0:T(8,128)(2,1)S(1)}, bf16[24,16,128]{2,1,0:T(8,128)(2,1)S(1)}, u32[]{:S(2)}, u32[]{:S(2)}) collective-permute-start(bf16[24,16,128]{2,1,0:T(8,128)(2,1)S(1)} %get-tuple-element.29), channel_id=1, source_target_pairs={{0,24},{4,28},{8,16},{12,20},{16,8},{20,12},{24,0},{28,4},{1,25},{... | collective-permute-start | bytes 294920 | tf_op jit(solution)/shard_map/ppermute | solution.py:228
  19.9 6.7 %collective-permute-done.1.refs_2_ = bf16[24,16,128]{2,1,0:T(8,128)(2,1)S(1)} collective-permute-done((bf16[24,16,128]{2,1,0:T(8,128)(2,1)S(1)}, bf16[24,16,128]{2,1,0:T(8,128)(2,1)S(1)}, u32[]{:S(2)}, u32[]{:S(2)}) %collective-permute-start.1) | collective-permute-done | bytes 98336 | tf_op jit(solution)/shard_map/ppermute | solution.py:228
  26.6 2.5 %collective-permute-start.6 = (bf16[24,16,128]{2,1,0:T(8,128)(2,1)S(1)}, bf16[24,16,128]{2,1,0:T(8,128)(2,1)S(1)}, u32[]{:S(2)}, u32[]{:S(2)}) collective-permute-start(bf16[24,16,128]{2,1,0:T(8,128)(2,1)S(1)} %get-tuple-element.30), channel_id=1, source_target_pairs={{0,28},{4,24},{8,20},{12,16},{16,12},{20,8},{24,4},{28,0},{1,29},{... | collective-permute-start | bytes 294920 | tf_op jit(solution)/shard_map/ppermute | solution.py:228
  29.2 13.3 %collective-permute-done.3.refs_4_ = bf16[24,16,128]{2,1,0:T(8,128)(2,1)S(1)} collective-permute-done((bf16[24,16,128]{2,1,0:T(8,128)(2,1)S(1)}, bf16[24,16,128]{2,1,0:T(8,128)(2,1)S(1)}, u32[]{:S(2)}, u32[]{:S(2)}) %collective-permute-start.3) | collective-permute-done | bytes 98336 | tf_op jit(solution)/shard_map/ppermute | solution.py:228
  42.5 1.2 %collective-permute-done.4.refs_5_ = bf16[24,16,128]{2,1,0:T(8,128)(2,1)S(1)} collective-permute-done((bf16[24,16,128]{2,1,0:T(8,128)(2,1)S(1)}, bf16[24,16,128]{2,1,0:T(8,128)(2,1)S(1)}, u32[]{:S(2)}, u32[]{:S(2)}) %collective-permute-start.4) | collective-permute-done | bytes 98336 | tf_op jit(solution)/shard_map/ppermute | solution.py:228
  43.6 0.8 %stage.1 = (f32[4,54,16,128]{3,2,1,0:T(8,128)S(1)}, f32[8,4,6,16,128]{4,3,2,1,0:T(8,128)S(1)}) custom-call(s32[2]{0:T(128)S(1)} %pad_add_fusion.me_ref, bf16[32,24,4,128]{3,2,1,0:T(4,128)(2,1)S(1)} %all-to-all-done.screens_ref, bf16[24,16,128]{2,1,0:T(8,128)(2,1)S(1)} %get-tuple-element.23.refs_0_, bf16[24,16,128]{2,1,0:T(8,128)(2,1)S(1)} %collective-permute-done.refs_1_, ...), custom_call_target="tpu_custom_call" | custom-call | tf_op jit(solution)/shard_map/stage/pallas_call | solution.py:117
  44.5 4.4 %sigma.3 = (s16[25,16,128]{2,1,0:T(8,128)(2,1)S(1)}, s16[25,16,128]{2,1,0:T(8,128)(2,1)S(1)}, s16[25,16,128]{2,1,0:T(8,128)(2,1)S(1)}, s16[25,16,128]{2,1,0:T(8,128)(2,1)S(1)}) custom-call(s32[2]{0:T(128)S(1)} %pad_add_fusion.me_ref, s32[64,3]{1,0:T(8,128)S(1)} %bitcast.3, s32[8,8]{1,0:T(8,128)S(1)} %copy-done.2, ...), custom_call_target="tpu_custom_call" | custom-call | tf_op jit(solution)/shard_map/sigma/pallas_call | solution.py:184
  48.9 3.3 %collective-permute-start.10 = (s16[25,16,128]{2,1,0:T(8,128)(2,1)S(1)}, s16[25,16,128]{2,1,0:T(8,128)(2,1)S(1)}, u32[]{:S(2)}, u32[]{:S(2)}) collective-permute-start(s16[25,16,128]{2,1,0:T(8,128)(2,1)S(1)} %get-tuple-element.37), channel_id=1, source_target_pairs={{0,16},{4,20},{8,24},{12,28},{16,0},{20,4},{24,8},{28,12},{1,17},{... | collective-permute-start | bytes 307208 | tf_op jit(solution)/shard_map/ppermute | solution.py:228
  52.2 2.6 %sigma.2 = (f32[24,16,128]{2,1,0:T(8,128)S(1)}, s16[25,16,128]{2,1,0:T(8,128)(2,1)S(1)}, s16[25,16,128]{2,1,0:T(8,128)(2,1)S(1)}, s16[25,16,128]{2,1,0:T(8,128)(2,1)S(1)}) custom-call(s32[2]{0:T(128)S(1)} %pad_add_fusion.me_ref, s32[64,3]{1,0:T(8,128)S(1)} %bitcast.4, s32[8,8]{1,0:T(8,128)S(1)} %copy-done.2, f32[4,54,16,128]{3,2,1,0:T(8,128)S(1)} %get-tuple-element.31.g_all, ...), custom_call_target="tpu_custom_call" | custom-call | tf_op jit(solution)/shard_map/sigma/pallas_call | solution.py:184
  54.8 5.7 %collective-permute-start.12 = (s16[25,16,128]{2,1,0:T(8,128)(2,1)S(1)}, s16[25,16,128]{2,1,0:T(8,128)(2,1)S(1)}, u32[]{:S(2)}, u32[]{:S(2)}) collective-permute-start(s16[25,16,128]{2,1,0:T(8,128)(2,1)S(1)} %get-tuple-element.39), channel_id=1, source_target_pairs={{0,24},{4,28},{8,16},{12,20},{16,8},{20,12},{24,0},{28,4},{1,25},{... | collective-permute-start | bytes 307208 | tf_op jit(solution)/shard_map/ppermute | solution.py:228
  60.7 0.3 collective-permute-start.8
  61.1 3.9 %collective-permute-done.11.refs_5_ = s16[25,16,128]{2,1,0:T(8,128)(2,1)S(1)} collective-permute-done((s16[25,16,128]{2,1,0:T(8,128)(2,1)S(1)}, s16[25,16,128]{2,1,0:T(8,128)(2,1)S(1)}, u32[]{:S(2)}, u32[]{:S(2)}) %collective-permute-start.11) | collective-permute-done | bytes 102432 | tf_op jit(solution)/shard_map/ppermute | solution.py:228
  65.0 2.6 %collective-permute-done.13.refs_7_ = s16[25,16,128]{2,1,0:T(8,128)(2,1)S(1)} collective-permute-done((s16[25,16,128]{2,1,0:T(8,128)(2,1)S(1)}, s16[25,16,128]{2,1,0:T(8,128)(2,1)S(1)}, u32[]{:S(2)}, u32[]{:S(2)}) %collective-permute-start.13) | collective-permute-done | bytes 102432 | tf_op jit(solution)/shard_map/ppermute | solution.py:228
  67.6 1.8 %collective-permute-done.8.refs_2_ = s16[25,16,128]{2,1,0:T(8,128)(2,1)S(1)} collective-permute-done((s16[25,16,128]{2,1,0:T(8,128)(2,1)S(1)}, s16[25,16,128]{2,1,0:T(8,128)(2,1)S(1)}, u32[]{:S(2)}, u32[]{:S(2)}) %collective-permute-start.8) | collective-permute-done | bytes 102432 | tf_op jit(solution)/shard_map/ppermute | solution.py:228
  69.3 2.1 %collective-permute-done.9.refs_3_ = s16[25,16,128]{2,1,0:T(8,128)(2,1)S(1)} collective-permute-done((s16[25,16,128]{2,1,0:T(8,128)(2,1)S(1)}, s16[25,16,128]{2,1,0:T(8,128)(2,1)S(1)}, u32[]{:S(2)}, u32[]{:S(2)}) %collective-permute-start.9) | collective-permute-done | bytes 102432 | tf_op jit(solution)/shard_map/ppermute | solution.py:228
  71.4 2.0 %unpack.1 = f32[4,6,2,16,512]{4,3,2,1,0:T(8,128)} custom-call(s32[2]{0:T(128)S(1)} %pad_add_fusion.me_ref, f32[24,16,128]{2,1,0:T(8,128)S(1)} %get-tuple-element.33.refs_0_, s16[25,16,128]{2,1,0:T(8,128)(2,1)S(1)} %collective-permute-done.7.refs_1_, s16[25,16,128]{2,1,0:T(8,128)(2,1)S(1)} %collective-permute-done.8.refs_2_, ...), custom_call_target="tpu_custom_call" | custom-call | tf_op jit(solution)/shard_map/unpack/pallas_call | solution.py:217
  (24 shorter events, 0.5 us)
Async XLA Ops:
  0.0 1.1 %copy-start = (bf16[4,6,8,4,512]{4,3,2,1,0:T(4,128)(2,1)S(1)}, bf16[4,6,8,4,512]{4,3,2,1,0:T(4,128)(2,1)}, u32[]{:S(2)}) copy-start(bf16[4,6,8,4,512]{4,3,2,1,0:T(4,128)(2,1)} %screened_ref.1) | copy-start | bytes 2359300
  1.1 0.7 copy-start.3
  1.8 9.1 %copy-start.1 = (bf16[4,6,2,16,512]{4,3,2,1,0:T(8,128)(2,1)S(1)}, bf16[4,6,2,16,512]{4,3,2,1,0:T(8,128)(2,1)}, u32[]{:S(2)}) copy-start(bf16[4,6,2,16,512]{4,3,2,1,0:T(8,128)(2,1)} %green_ref.1) | copy-start | bytes 2359300
  3.5 25.6 %copy-start.4 = (s32[8,8,3]{1,0,2:T(8,128)S(1)}, s32[8,8,3]{1,0,2:T(8,128)}, u32[]{:S(2)}) copy-start(s32[8,8,3]{1,0,2:T(8,128)} %param.8) | copy-start | bytes 2308
  3.5 40.1 %all-to-all-start = ((bf16[32,24,4,128]{3,2,1,0:T(4,128)(2,1)}), bf16[32,24,4,128]{3,2,1,0:T(4,128)(2,1)S(1)}, u32[]{:S(2)}, u32[]{:S(2)}) async-start(bf16[32,24,4,128]{3,2,1,0:T(4,128)(2,1)} %pick_screened.1), calls=%async_computation | async-start | bytes 1572864 | tf_op jit(solution)/shard_map/all_to_all | solution.py:233
  10.8 33.7 %copy-start.2 = (s32[8,8]{1,0:T(8,128)S(1)}, s32[8,8]{1,0:T(8,128)}, u32[]{:S(2)}) copy-start(s32[8,8]{1,0:T(8,128)} %count_ref.3) | copy-start | bytes 772
  11.6 4.7 %collective-permute-start = (bf16[24,16,128]{2,1,0:T(8,128)(2,1)S(1)}, bf16[24,16,128]{2,1,0:T(8,128)(2,1)S(1)}, u32[]{:S(2)}, u32[]{:S(2)}) collective-permute-start(bf16[24,16,128]{2,1,0:T(8,128)(2,1)S(1)} %get-tuple-element.24), channel_id=1, source_target_pairs={{0,4},{4,0},{8,12},{12,8},{16,20},{20,16},{24,28},{28,24},{1,5},{5... | collective-permute-start | bytes 294920 | tf_op jit(solution)/shard_map/ppermute | solution.py:228
  11.9 14.6 %collective-permute-start.1 = (bf16[24,16,128]{2,1,0:T(8,128)(2,1)S(1)}, bf16[24,16,128]{2,1,0:T(8,128)(2,1)S(1)}, u32[]{:S(2)}, u32[]{:S(2)}) collective-permute-start(bf16[24,16,128]{2,1,0:T(8,128)(2,1)S(1)} %get-tuple-element.25), channel_id=1, source_target_pairs={{0,8},{4,12},{8,0},{12,4},{16,24},{20,28},{24,16},{28,20},{1,9},{5... | collective-permute-start | bytes 294920 | tf_op jit(solution)/shard_map/ppermute | solution.py:228
  13.6 15.5 %collective-permute-start.2 = (bf16[24,16,128]{2,1,0:T(8,128)(2,1)S(1)}, bf16[24,16,128]{2,1,0:T(8,128)(2,1)S(1)}, u32[]{:S(2)}, u32[]{:S(2)}) collective-permute-start(bf16[24,16,128]{2,1,0:T(8,128)(2,1)S(1)} %get-tuple-element.26), channel_id=1, source_target_pairs={{0,12},{4,8},{8,4},{12,0},{16,28},{20,24},{24,20},{28,16},{1,13},{... | collective-permute-start | bytes 294920 | tf_op jit(solution)/shard_map/ppermute | solution.py:228
  13.6 28.8 %collective-permute-start.3 = (bf16[24,16,128]{2,1,0:T(8,128)(2,1)S(1)}, bf16[24,16,128]{2,1,0:T(8,128)(2,1)S(1)}, u32[]{:S(2)}, u32[]{:S(2)}) collective-permute-start(bf16[24,16,128]{2,1,0:T(8,128)(2,1)S(1)} %get-tuple-element.27), channel_id=1, source_target_pairs={{0,16},{4,20},{8,24},{12,28},{16,0},{20,4},{24,8},{28,12},{1,17},{... | collective-permute-start | bytes 294920 | tf_op jit(solution)/shard_map/ppermute | solution.py:228
  16.2 27.4 %collective-permute-start.4 = (bf16[24,16,128]{2,1,0:T(8,128)(2,1)S(1)}, bf16[24,16,128]{2,1,0:T(8,128)(2,1)S(1)}, u32[]{:S(2)}, u32[]{:S(2)}) collective-permute-start(bf16[24,16,128]{2,1,0:T(8,128)(2,1)S(1)} %get-tuple-element.28), channel_id=1, source_target_pairs={{0,20},{4,16},{8,28},{12,24},{16,4},{20,0},{24,12},{28,8},{1,21},{... | collective-permute-start | bytes 294920 | tf_op jit(solution)/shard_map/ppermute | solution.py:228
  16.3 27.3 %collective-permute-start.5 = (bf16[24,16,128]{2,1,0:T(8,128)(2,1)S(1)}, bf16[24,16,128]{2,1,0:T(8,128)(2,1)S(1)}, u32[]{:S(2)}, u32[]{:S(2)}) collective-permute-start(bf16[24,16,128]{2,1,0:T(8,128)(2,1)S(1)} %get-tuple-element.29), channel_id=1, source_target_pairs={{0,24},{4,28},{8,16},{12,20},{16,8},{20,12},{24,0},{28,4},{1,25},{... | collective-permute-start | bytes 294920 | tf_op jit(solution)/shard_map/ppermute | solution.py:228
  26.6 17.0 %collective-permute-start.6 = (bf16[24,16,128]{2,1,0:T(8,128)(2,1)S(1)}, bf16[24,16,128]{2,1,0:T(8,128)(2,1)S(1)}, u32[]{:S(2)}, u32[]{:S(2)}) collective-permute-start(bf16[24,16,128]{2,1,0:T(8,128)(2,1)S(1)} %get-tuple-element.30), channel_id=1, source_target_pairs={{0,28},{4,24},{8,20},{12,16},{16,12},{20,8},{24,4},{28,0},{1,29},{... | collective-permute-start | bytes 294920 | tf_op jit(solution)/shard_map/ppermute | solution.py:228
  48.9 11.8 %collective-permute-start.10 = (s16[25,16,128]{2,1,0:T(8,128)(2,1)S(1)}, s16[25,16,128]{2,1,0:T(8,128)(2,1)S(1)}, u32[]{:S(2)}, u32[]{:S(2)}) collective-permute-start(s16[25,16,128]{2,1,0:T(8,128)(2,1)S(1)} %get-tuple-element.37), channel_id=1, source_target_pairs={{0,16},{4,20},{8,24},{12,28},{16,0},{20,4},{24,8},{28,12},{1,17},{... | collective-permute-start | bytes 307208 | tf_op jit(solution)/shard_map/ppermute | solution.py:228
  52.2 12.7 %collective-permute-start.11 = (s16[25,16,128]{2,1,0:T(8,128)(2,1)S(1)}, s16[25,16,128]{2,1,0:T(8,128)(2,1)S(1)}, u32[]{:S(2)}, u32[]{:S(2)}) collective-permute-start(s16[25,16,128]{2,1,0:T(8,128)(2,1)S(1)} %get-tuple-element.38), channel_id=1, source_target_pairs={{0,20},{4,16},{8,28},{12,24},{16,4},{20,0},{24,12},{28,8},{1,21},{... | collective-permute-start | bytes 307208 | tf_op jit(solution)/shard_map/ppermute | solution.py:228
  54.8 10.2 %collective-permute-start.12 = (s16[25,16,128]{2,1,0:T(8,128)(2,1)S(1)}, s16[25,16,128]{2,1,0:T(8,128)(2,1)S(1)}, u32[]{:S(2)}, u32[]{:S(2)}) collective-permute-start(s16[25,16,128]{2,1,0:T(8,128)(2,1)S(1)} %get-tuple-element.39), channel_id=1, source_target_pairs={{0,24},{4,28},{8,16},{12,20},{16,8},{20,12},{24,0},{28,4},{1,25},{... | collective-permute-start | bytes 307208 | tf_op jit(solution)/shard_map/ppermute | solution.py:228
  60.5 7.1 %collective-permute-start.13 = (s16[25,16,128]{2,1,0:T(8,128)(2,1)S(1)}, s16[25,16,128]{2,1,0:T(8,128)(2,1)S(1)}, u32[]{:S(2)}, u32[]{:S(2)}) collective-permute-start(s16[25,16,128]{2,1,0:T(8,128)(2,1)S(1)} %get-tuple-element.40), channel_id=1, source_target_pairs={{0,28},{4,24},{8,20},{12,16},{16,12},{20,8},{24,4},{28,0},{1,29},{... | collective-permute-start | bytes 307208 | tf_op jit(solution)/shard_map/ppermute | solution.py:228
  60.5 7.1 %collective-permute-start.7 = (s16[25,16,128]{2,1,0:T(8,128)(2,1)S(1)}, s16[25,16,128]{2,1,0:T(8,128)(2,1)S(1)}, u32[]{:S(2)}, u32[]{:S(2)}) collective-permute-start(s16[25,16,128]{2,1,0:T(8,128)(2,1)S(1)} %get-tuple-element.34), channel_id=1, source_target_pairs={{0,4},{4,0},{8,12},{12,8},{16,20},{20,16},{24,28},{28,24},{1,5},{5... | collective-permute-start | bytes 307208 | tf_op jit(solution)/shard_map/ppermute | solution.py:228
  60.7 8.6 %collective-permute-start.8 = (s16[25,16,128]{2,1,0:T(8,128)(2,1)S(1)}, s16[25,16,128]{2,1,0:T(8,128)(2,1)S(1)}, u32[]{:S(2)}, u32[]{:S(2)}) collective-permute-start(s16[25,16,128]{2,1,0:T(8,128)(2,1)S(1)} %get-tuple-element.35), channel_id=1, source_target_pairs={{0,8},{4,12},{8,0},{12,4},{16,24},{20,28},{24,16},{28,20},{1,9},{5... | collective-permute-start | bytes 307208 | tf_op jit(solution)/shard_map/ppermute | solution.py:228
  65.0 6.4 %collective-permute-start.9 = (s16[25,16,128]{2,1,0:T(8,128)(2,1)S(1)}, s16[25,16,128]{2,1,0:T(8,128)(2,1)S(1)}, u32[]{:S(2)}, u32[]{:S(2)}) collective-permute-start(s16[25,16,128]{2,1,0:T(8,128)(2,1)S(1)} %get-tuple-element.36), channel_id=1, source_target_pairs={{0,12},{4,8},{8,4},{12,0},{16,28},{20,24},{24,20},{28,16},{1,13},{... | collective-permute-start | bytes 307208 | tf_op jit(solution)/shard_map/ppermute | solution.py:228

commit v4 on v3

--- a/solution.py
+++ b/solution.py
@@ -10,12 +10,12 @@
 SCALE = 0.2
 LANES = 128
 PAIR = 2
-STEPS = 32700.0
+halfS = 32700.0
 FINE = 64.0
 TINY = 1e-34
 SMEM = pl.BlockSpec(memory_space=pltpu.SMEM)
 VMEM = pl.BlockSpec(memory_space=pltpu.VMEM)
-HBM = pl.BlockSpec(memory_space=pltpu.HBM)
+ANY = pl.BlockSpec(memory_space=pl.ANY)
 PARAMS = pltpu.CompilerParams(vmem_limit_bytes=32 * 1024 * 1024)
 
 
@@ -93,17 +93,28 @@
     )(me, green)
 
 
-def stage_kernel(s, me_ref, screens_ref, *refs):
-    greens = refs[: s.groups]
-    g_all, w_all = refs[s.groups :]
-    me = me_ref[0]
+def held(s):
+    return jax.ShapeDtypeStruct((s.comps, (s.groups // 2 + 2) * s.energies) + s.plane, jnp.float32)
+
+
+def stage_green(s, me, first, blocks, g_half):
+    half = s.groups // 2
     zero = jnp.zeros(s.plane, jnp.float32)
     for comp in range(s.comps):
         for j in range(s.energies):
+            g_half[comp, j] = zero
+            g_half[comp, (half + 1) * s.energies + j] = zero
+            for k, block in enumerate(blocks):
+                group = (me ^ (first + k)) % half
+                g_half[comp, (group + 1) * s.energies + j] = block[comp * s.energies + j].astype(jnp.float32)
+
+
+def stage_near_kernel(s, me_ref, screens_ref, *refs):
+    g_half, w_all = refs[-2:]
+    stage_green(s, me_ref[0], 0, refs[:-2], g_half)
+    for comp in range(s.comps):
+        for j in range(s.energies):
             plane = comp * s.energies + j
-            g_all[comp, j] = zero
-            for k in range(s.groups):
-                g_all[comp, ((me ^ k) + 1) * s.energies + j] = greens[k][plane].astype(jnp.float32)
             for source in range(s.groups):
                 if s.parts > 1:
                     w_all[source, comp, j] = screens_ref[source, plane].astype(jnp.float32)
@@ -113,48 +124,95 @@
                     w_all[source, comp, j, c * s.held : (c + 1) * s.held, :] = piece
 
 
-def stage(s, me, greens, screens):
-    return pl.pallas_call(
-        functools.partial(stage_kernel, s),
-        out_shape=[
-            jax.ShapeDtypeStruct((s.comps, (s.groups + 1) * s.energies) + s.plane, jnp.float32),
-            jax.ShapeDtypeStruct((s.groups, s.comps, s.energies) + s.plane, jnp.float32),
-        ],
-        in_specs=[SMEM] + [VMEM] * (s.groups + 1),
+def stage_near(s, me, screens, greens):
+    return pl.pallas_call(
+        functools.partial(stage_near_kernel, s),
+        out_shape=[held(s), jax.ShapeDtypeStruct((s.groups, s.comps, s.energies) + s.plane, jnp.float32)],
+        in_specs=[SMEM] + [VMEM] * (len(greens) + 1),
         out_specs=[VMEM] * 2,
         compiler_params=PARAMS,
-        name="stage",
+        name="stage_near",
     )(me, screens, *greens)
 
 
-def sigma_kernel(s, slots, ks, me_ref, table_ref, count_ref, g_all, w_all, *outs):
+def stage_far_kernel(s, me_ref, after_ref, *refs):
+    stage_green(s, me_ref[0], s.groups // 2, refs[:-1], refs[-1])
+
+
+def stage_far(s, me, greens, after):
+    return pl.pallas_call(
+        functools.partial(stage_far_kernel, s),
+        out_shape=held(s),
+        in_specs=[SMEM, ANY] + [VMEM] * len(greens),
+        out_specs=VMEM,
+        compiler_params=PARAMS,
+        name="stage_far",
+    )(me, after, *greens)
+
+
+def add_terms(s, slots, side, group, kind, table_ref, count_ref, g_half, w_all, sums):
+    low = side * (s.groups // 2)
+
+    def turn(source, sums):
+        sums = list(sums)
+        count = count_ref[group, source]
+        for slot in range(slots):
+            shift = jnp.clip(table_ref[group * s.groups + source, slot], 0, s.energies - 1)
+            live = jnp.where(slot < count, 1.0, 0.0).astype(jnp.float32)
+            start = (group - source - low + 1) * s.energies - shift
+            w_real = w_all[source, 2 * kind, shift] * live
+            w_imag = w_all[source, 2 * kind + 1, shift] * live
+            for j in range(s.energies):
+                g_real = g_half[2 * kind, start + j]
+                g_imag = g_half[2 * kind + 1, start + j]
+                sums[j] = sums[j] - (g_real * w_imag + g_imag * w_real)
+                sums[s.energies + j] = sums[s.energies + j] + (g_real * w_real - g_imag * w_imag)
+        return tuple(sums)
+
+    first = jnp.maximum(group - low - s.groups // 2, 0)
+    return lax.fori_loop(first, jnp.maximum(group - low + 1, first), turn, tuple(sums))
+
+
+def partial_kernel(s, slots, ks, me_ref, table_ref, count_ref, g_half, w_all, out_ref):
     me = me_ref[0]
+    side = me // (s.groups // 2)
+    for at, k in enumerate(ks):
+        for kind in range(2):
+            zeros = [jnp.zeros(s.plane, jnp.float32) for _ in range(2 * s.energies)]
+            sums = add_terms(s, slots, side, me ^ k, kind, table_ref, count_ref, g_half, w_all, zeros)
+            for j, total in enumerate(sums):
+                out_ref[at, kind * 2 * s.energies + j] = total
+
+
+def partial_of(s, me, table, count, g_half, w_all, ks):
+    return pl.pallas_call(
+        functools.partial(partial_kernel, s, table.shape[1], ks),
+        out_shape=jax.ShapeDtypeStruct((len(ks), s.planes) + s.plane, jnp.float32),
+        in_specs=[SMEM] * 3 + [VMEM] * 2,
+        out_specs=VMEM,
+        compiler_params=PARAMS,
+        name="partial",
+    )(me, table, count, g_half, w_all)
+
+
+def sigma_kernel(s, slots, ks, begun, me_ref, table_ref, count_ref, *refs):
+    outs = refs[-len(ks) :]
+    other, w_all, g_far = refs[: -len(ks)]
+    me = me_ref[0]
+    side = me // (s.groups // 2)
     row = lax.broadcasted_iota(jnp.int32, s.plane, 0)
     for at, k in enumerate(ks):
         group = me ^ k
         codes = [jnp.zeros(s.plane, jnp.float32) for _ in range(s.scale_planes)]
         for kind in range(2):
-
-            def turn(source, sums):
-                sums = list(sums)
-                count = count_ref[group, source]
-                for slot in range(slots):
-                    shift = jnp.clip(table_ref[group * s.groups + source, slot], 0, s.energies - 1)
-                    live = jnp.where(slot < count, 1.0, 0.0).astype(jnp.float32)
-                    start = (group - source + 1) * s.energies - shift
-                    w_real = w_all[source, 2 * kind, shift] * live
-                    w_imag = w_all[source, 2 * kind + 1, shift] * live
-                    for j in range(s.energies):
-                        g_real = g_all[2 * kind, start + j]
-                        g_imag = g_all[2 * kind + 1, start + j]
-                        sums[j] = sums[j] - (g_real * w_imag + g_imag * w_real)
-                        sums[s.energies + j] = sums[s.energies + j] + (g_real * w_real - g_imag * w_imag)
-                return tuple(sums)
-
-            zeros = tuple(jnp.zeros(s.plane, jnp.float32) for _ in range(2 * s.energies))
-            sums = lax.fori_loop(0, group + 1, turn, zeros)
+            first = kind * 2 * s.energies
+            if begun is None:
+                sums = [jnp.zeros(s.plane, jnp.float32) for _ in range(2 * s.energies)]
+                sums = add_terms(s, slots, side, group, kind, table_ref, count_ref, other, w_all, sums)
+            else:
+                sums = [other[begun + at, first + j] for j in range(2 * s.energies)]
+            sums = add_terms(s, slots, 1 - side, group, kind, table_ref, count_ref, g_far, w_all, sums)
             sums = [total * SCALE for total in sums]
-            first = kind * 2 * s.energies
             if k == 0:
                 for j, total in enumerate(sums):
                     outs[at][first + j] = total
@@ -164,7 +222,7 @@
                 largest = functools.reduce(jnp.maximum, [jnp.abs(total) for total in pair])
                 largest = jnp.maximum(jnp.max(largest, axis=0, keepdims=True), TINY)
                 code = jnp.ceil(jnp.log2(largest) * FINE)
-                inverse = jnp.exp2(code * (-1.0 / FINE)) * STEPS
+                inverse = jnp.exp2(code * (-1.0 / FINE)) * halfS
                 where = (first + low) // PAIR
                 spot = where // s.plane[0]
                 codes[spot] = jnp.where(row == where % s.plane[0], code, codes[spot])
@@ -173,22 +231,20 @@
                     outs[at][first + low + j] = coded.astype(jnp.int16)
         if k != 0:
             for j in range(s.scale_planes):
-                outs[at][s.comps * s.energies + j] = codes[j].astype(jnp.int32).astype(jnp.int16)
-
-
-def sigma_of(s, me, table, count, g_all, w_all, ks):
-    slots = table.shape[-1]
-    planes = s.comps * s.energies
-    own = jax.ShapeDtypeStruct((planes,) + s.plane, jnp.float32)
-    coded = jax.ShapeDtypeStruct((planes + s.scale_planes,) + s.plane, jnp.int16)
-    return pl.pallas_call(
-        functools.partial(sigma_kernel, s, slots, ks),
+                outs[at][s.planes + j] = codes[j].astype(jnp.int32).astype(jnp.int16)
+
+
+def sigma_of(s, me, table, count, g_far, w_all, other, ks, begun):
+    own = jax.ShapeDtypeStruct((s.planes,) + s.plane, jnp.float32)
+    coded = jax.ShapeDtypeStruct((s.planes + s.scale_planes,) + s.plane, jnp.int16)
+    return pl.pallas_call(
+        functools.partial(sigma_kernel, s, table.shape[1], ks, begun),
         out_shape=[own if k == 0 else coded for k in ks],
-        in_specs=[SMEM] * 3 + [VMEM] * 2,
+        in_specs=[SMEM] * 3 + [VMEM] * 3,
         out_specs=[VMEM] * len(ks),
         compiler_params=PARAMS,
         name="sigma",
-    )(me, table.reshape(s.groups * s.groups, slots), count, g_all, w_all)
+    )(me, table, count, other, w_all, g_far)
 
 
 def unpack_kernel(s, me_ref, *refs):
@@ -201,7 +257,7 @@
         if k != 0:
             for j in range(s.scale_planes):
                 code = block[s.planes + j].astype(jnp.int32).astype(jnp.float32)
-                scales.append(jnp.exp2(code * (1.0 / FINE)) * (1.0 / STEPS))
+                scales.append(jnp.exp2(code * (1.0 / FINE)) * (1.0 / halfS))
         for comp in range(s.comps):
             for j in range(s.energies):
                 plane = comp * s.energies + j
@@ -246,11 +302,17 @@
 
     screens = send_screened(s, cell_map, screened)
     greens = [swap(s, block, k) for k, block in enumerate(cut_green(s, me, green))]
-    g_all, w_all = stage(s, me, greens, screens)
+    table = shift_table.reshape(s.groups * s.groups, shift_table.shape[2])
+    g_near, w_all = stage_near(s, me, screens, greens[:half])
+    begun = partial_of(s, me, table, shift_count, g_near, w_all, far)
+    g_far = stage_far(s, me, greens[half:], begun)
     sums = {}
-    for ks in (far, near):
-        for k, block in zip(ks, sigma_of(s, me, shift_table, shift_count, g_all, w_all, ks)):
+    for first in range(0, half, half):
+        ks = far[first : first + half]
+        for k, block in zip(ks, sigma_of(s, me, table, shift_count, g_far, w_all, begun, ks, first)):
             sums[k] = swap(s, block, k)
+    for k, block in zip(near, sigma_of(s, me, table, shift_count, g_far, w_all, g_near, near, None)):
+        sums[k] = swap(s, block, k)
     return unpack(s, me, [sums[k] for k in range(s.groups)])
 
 

time: 73.7 us -> 72.2 us (0.980)
  waiting for transfers between devices: 31.5 us -> 26.5 us
  Pallas kernels: 12.2 us -> 14.5 us
  starting transfers between devices: 27.6 us -> 28.4 us
    ppermute x14, waiting for transfers between devices: 31.5 us -> 23.5 us  [swap(): lax.ppermute(block, 'energy', [(i, i ^ k) for i in range(s.groups)])]
    all_to_all x1, waiting for transfers between devices: 0.01 us -> 3.01 us  [send_screened(): lax.all_to_all(pick_screened(s, cell_map, screened), ('energy', 'cell'),...]
    pallas_call x3 -> x5, Pallas kernels: 7.81 us -> 10.1 us  [the longest x2 5.27 us: sigma_of(): pl.pallas_call(functools.partial(sigma_kernel, s, table.shape[1], ks, beg...]
    ppermute x14, starting transfers between devices: 20.3 us -> 21.1 us  [swap(): lax.ppermute(block, 'energy', [(i, i ^ k) for i in range(s.groups)])]
  transfers between devices with their start and end apart: 15 -> 15, of which waited for: 7 -> 9; matrix products, arithmetic and copies ran while one was open for 0% -> 0% of each run, Pallas kernels for 4% -> 11%
where the time goes in v4:
time: 72.2 us; the launch traced here: 71.5 us
  starting transfers between devices  28.4 us (39%)
  waiting for transfers between devices  26.5 us (37%)
  Pallas kernels  14.5 us (20%)
  local copies, waits for them, and re-layouts  1.92 us (3%)
    ppermute x14, waiting for transfers between devices, swap(): lax.ppermute(block, 'energy', [(i, i ^ k) for i in range(s.groups)])  23.5 us
    ppermute x14, starting transfers between devices, swap(): lax.ppermute(block, 'energy', [(i, i ^ k) for i in range(s.groups)])  21.1 us
    all_to_all x1, starting transfers between devices, send_screened(): lax.all_to_all(pick_screened(s, cell_map, screened), ('energy', 'cell'),...  7.3 us
    pallas_call x2, Pallas kernels, sigma_of(): pl.pallas_call(functools.partial(sigma_kernel, s, table.shape[1], ks, beg...  5.27 us
    pallas_call x1, Pallas kernels, partial_of(): pl.pallas_call(functools.partial(partial_kernel, s, table.shape[1], ks),...  3.46 us
    all_to_all x1, waiting for transfers between devices, send_screened(): lax.all_to_all(pick_screened(s, cell_map, screened), ('energy', 'cell'),...  3.01 us
    pallas_call x1, Pallas kernels, unpack(): pl.pallas_call(functools.partial(unpack_kernel, s), out_shape=jax.ShapeDt...  1.96 us
    unnamed x11, local copies, waits for them, and re-layouts  1.92 us
  transfers between devices with their start and end apart: 15, of which 9 were waited for; matrix products, arithmetic and copies ran while one was open for 0% of the time, Pallas kernels for 11%

profile of v4, /device:TPU:0, one launch (start us, length us, event | category | flops | bytes accessed | tf_op | source)
XLA Modules:
  0.0 71.5 jit_solution(14819430105522571973)
XLA Ops:
  0.0 1.1 %copy-done = bf16[4,6,8,4,512]{4,3,2,1,0:T(4,128)(2,1)S(1)} copy-done((bf16[4,6,8,4,512]{4,3,2,1,0:T(4,128)(2,1)S(1)}, bf16[4,6,8,4,512]{4,3,2,1,0:T(4,128)(2,1)}, u32[]{:S(2)}) %copy-start) | copy-done | bytes 786456
  1.8 1.7 %pick_screened.1 = bf16[32,24,4,128]{3,2,1,0:T(4,128)(2,1)} custom-call(s32[8]{0:T(128)S(1)} %copy-done.3, bf16[4,6,8,4,512]{4,3,2,1,0:T(4,128)(2,1)S(1)} %copy-done), custom_call_target="tpu_custom_call" | custom-call | tf_op jit(solution)/shard_map/pick_screened/pallas_call | solution.py:62
  3.5 7.3 %all-to-all-start = ((bf16[32,24,4,128]{3,2,1,0:T(4,128)(2,1)}), bf16[32,24,4,128]{3,2,1,0:T(4,128)(2,1)S(1)}, u32[]{:S(2)}, u32[]{:S(2)}) async-start(bf16[32,24,4,128]{3,2,1,0:T(4,128)(2,1)} %pick_screened.1), calls=%async_computation | async-start | bytes 1572864 | tf_op jit(solution)/shard_map/all_to_all | solution.py:289
  10.9 0.7 %cut_green.1 = (bf16[24,16,128]{2,1,0:T(8,128)(2,1)S(1)}, bf16[24,16,128]{2,1,0:T(8,128)(2,1)S(1)}, bf16[24,16,128]{2,1,0:T(8,128)(2,1)S(1)}, bf16[24,16,128]{2,...) custom-call(s32[2]{0:T(128)S(1)} %pad_add_fusion.me_ref, ...), custom_call_target="tpu_custom_call" | custom-call | tf_op jit(solution)/shard_map/cut_green/pallas_call | solution.py:86
  11.9 1.7 %collective-permute-start.1 = (bf16[24,16,128]{2,1,0:T(8,128)(2,1)S(1)}, bf16[24,16,128]{2,1,0:T(8,128)(2,1)S(1)}, u32[]{:S(2)}, u32[]{:S(2)}) collective-permute-start(bf16[24,16,128]{2,1,0:T(8,128)(2,1)S(1)} %get-tuple-element.25), channel_id=1, source_target_pairs={{0,8},{4,12},{8,0},{12,4},{16,24},{20,28},{24,16},{28,20},{1,9},{5... | collective-permute-start | bytes 294920 | tf_op jit(solution)/shard_map/ppermute | solution.py:284
  13.6 2.6 %collective-permute-start.3 = (bf16[24,16,128]{2,1,0:T(8,128)(2,1)S(1)}, bf16[24,16,128]{2,1,0:T(8,128)(2,1)S(1)}, u32[]{:S(2)}, u32[]{:S(2)}) collective-permute-start(bf16[24,16,128]{2,1,0:T(8,128)(2,1)S(1)} %get-tuple-element.29), channel_id=1, source_target_pairs={{0,16},{4,20},{8,24},{12,28},{16,0},{20,4},{24,8},{28,12},{1,17},{... | collective-permute-start | bytes 294920 | tf_op jit(solution)/shard_map/ppermute | solution.py:284
  16.3 3.5 %collective-permute-start.5 = (bf16[24,16,128]{2,1,0:T(8,128)(2,1)S(1)}, bf16[24,16,128]{2,1,0:T(8,128)(2,1)S(1)}, u32[]{:S(2)}, u32[]{:S(2)}) collective-permute-start(bf16[24,16,128]{2,1,0:T(8,128)(2,1)S(1)} %get-tuple-element.31), channel_id=1, source_target_pairs={{0,24},{4,28},{8,16},{12,20},{16,8},{20,12},{24,0},{28,4},{1,25},{... | collective-permute-start | bytes 294920 | tf_op jit(solution)/shard_map/ppermute | solution.py:284
  19.9 6.7 %collective-permute-done.1.refs_2_ = bf16[24,16,128]{2,1,0:T(8,128)(2,1)S(1)} collective-permute-done((bf16[24,16,128]{2,1,0:T(8,128)(2,1)S(1)}, bf16[24,16,128]{2,1,0:T(8,128)(2,1)S(1)}, u32[]{:S(2)}, u32[]{:S(2)}) %collective-permute-start.1) | collective-permute-done | bytes 98336 | tf_op jit(solution)/shard_map/ppermute | solution.py:284
  26.6 2.5 %collective-permute-start.6 = (bf16[24,16,128]{2,1,0:T(8,128)(2,1)S(1)}, bf16[24,16,128]{2,1,0:T(8,128)(2,1)S(1)}, u32[]{:S(2)}, u32[]{:S(2)}) collective-permute-start(bf16[24,16,128]{2,1,0:T(8,128)(2,1)S(1)} %get-tuple-element.32), channel_id=1, source_target_pairs={{0,28},{4,24},{8,20},{12,16},{16,12},{20,8},{24,4},{28,0},{1,29},{... | collective-permute-start | bytes 294920 | tf_op jit(solution)/shard_map/ppermute | solution.py:284
  29.2 3.0 %all-to-all-done.screens_ref = bf16[32,24,4,128]{3,2,1,0:T(4,128)(2,1)S(1)} async-done(((bf16[32,24,4,128]{3,2,1,0:T(4,128)(2,1)}), bf16[32,24,4,128]{3,2,1,0:T(4,128)(2,1)S(1)}, u32[]{:S(2)}, u32[]{:S(2)}) %all-to-all-start) | async-done | bytes 786464 | tf_op jit(solution)/shard_map/all_to_all | solution.py:289
  32.2 0.8 %stage_near.1 = (f32[4,36,16,128]{3,2,1,0:T(8,128)S(1)}, f32[8,4,6,16,128]{4,3,2,1,0:T(8,128)S(1)}) custom-call(s32[2]{0:T(128)S(1)} %pad_add_fusion.me_ref, bf16[32,24,4,128]{3,2,1,0:T(4,128)(2,1)S(1)} %all-to-all-done.screens_ref, bf16[24,16,128]{2,1,0:T(8,128)(2,1)S(1)} %get-tuple-element.23.refs_0_, ...), custom_call_target="tpu_custom_call" | custom-call | tf_op jit(solution)/shard_map/stage_near/pallas_call | solution.py:128
  33.0 3.5 %partial.1.after_ref.refs_0_ = f32[4,24,16,128]{3,2,1,0:T(8,128)S(1)} custom-call(s32[2]{0:T(128)S(1)} %pad_add_fusion.me_ref, s32[64,3]{1,0:T(8,128)S(1)} %bitcast.3, s32[8,8]{1,0:T(8,128)S(1)} %copy-done.2, f32[4,36,16,128]{3,2,1,0:T(8,128)S(1)} %get-tuple-element.27.g_half.refs_0_, f32[8,4,6,16,128]{4,3,2,1,0:T(8,128)S(1)} %get-tuple-element.28.w_all.refs_1_), custom_call_target="tpu_custom_call" | custom-call | tf_op jit(solution)/shard_map/partial/pallas_call | solution.py:188
  36.5 6.0 %collective-permute-done.3.refs_0_ = bf16[24,16,128]{2,1,0:T(8,128)(2,1)S(1)} collective-permute-done((bf16[24,16,128]{2,1,0:T(8,128)(2,1)S(1)}, bf16[24,16,128]{2,1,0:T(8,128)(2,1)S(1)}, u32[]{:S(2)}, u32[]{:S(2)}) %collective-permute-start.3) | collective-permute-done | bytes 98336 | tf_op jit(solution)/shard_map/ppermute | solution.py:284
  42.5 1.2 %collective-permute-done.4.refs_1_ = bf16[24,16,128]{2,1,0:T(8,128)(2,1)S(1)} collective-permute-done((bf16[24,16,128]{2,1,0:T(8,128)(2,1)S(1)}, bf16[24,16,128]{2,1,0:T(8,128)(2,1)S(1)}, u32[]{:S(2)}, u32[]{:S(2)}) %collective-permute-start.4) | collective-permute-done | bytes 98336 | tf_op jit(solution)/shard_map/ppermute | solution.py:284
  44.3 2.6 %sigma.3 = (s16[25,16,128]{2,1,0:T(8,128)(2,1)S(1)}, s16[25,16,128]{2,1,0:T(8,128)(2,1)S(1)}, s16[25,16,128]{2,1,0:T(8,128)(2,1)S(1)}, s16[25,16,128]{2,1,0:T(8,128)(2,1)S(1)}) custom-call(s32[2]{0:T(128)S(1)} %pad_add_fusion.me_ref, s32[64,3]{1,0:T(8,128)S(1)} %bitcast.4, s32[8,8]{1,0:T(8,128)S(1)} %copy-done.2, ...), custom_call_target="tpu_custom_call" | custom-call | tf_op jit(solution)/shard_map/sigma/pallas_call | solution.py:240
  46.9 5.1 %collective-permute-start.10 = (s16[25,16,128]{2,1,0:T(8,128)(2,1)S(1)}, s16[25,16,128]{2,1,0:T(8,128)(2,1)S(1)}, u32[]{:S(2)}, u32[]{:S(2)}) collective-permute-start(s16[25,16,128]{2,1,0:T(8,128)(2,1)S(1)} %get-tuple-element.37), channel_id=1, source_target_pairs={{0,16},{4,20},{8,24},{12,28},{16,0},{20,4},{24,8},{28,12},{1,17},{... | collective-permute-start | bytes 307208 | tf_op jit(solution)/shard_map/ppermute | solution.py:284
  52.0 2.6 %sigma.2 = (f32[24,16,128]{2,1,0:T(8,128)S(1)}, s16[25,16,128]{2,1,0:T(8,128)(2,1)S(1)}, s16[25,16,128]{2,1,0:T(8,128)(2,1)S(1)}, s16[25,16,128]{2,1,0:T(8,128)(2,1)S(1)}) custom-call(s32[2]{0:T(128)S(1)} %pad_add_fusion.me_ref, s32[64,3]{1,0:T(8,128)S(1)} %bitcast.5, s32[8,8]{1,0:T(8,128)S(1)} %copy-done.2, ...), custom_call_target="tpu_custom_call" | custom-call | tf_op jit(solution)/shard_map/sigma/pallas_call | solution.py:240
  54.7 4.4 %collective-permute-start.12 = (s16[25,16,128]{2,1,0:T(8,128)(2,1)S(1)}, s16[25,16,128]{2,1,0:T(8,128)(2,1)S(1)}, u32[]{:S(2)}, u32[]{:S(2)}) collective-permute-start(s16[25,16,128]{2,1,0:T(8,128)(2,1)S(1)} %get-tuple-element.39), channel_id=1, source_target_pairs={{0,24},{4,28},{8,16},{12,20},{16,8},{20,12},{24,0},{28,4},{1,25},{... | collective-permute-start | bytes 307208 | tf_op jit(solution)/shard_map/ppermute | solution.py:284
  59.6 0.7 collective-permute-start.8
  60.3 3.7 %collective-permute-done.11.refs_5_ = s16[25,16,128]{2,1,0:T(8,128)(2,1)S(1)} collective-permute-done((s16[25,16,128]{2,1,0:T(8,128)(2,1)S(1)}, s16[25,16,128]{2,1,0:T(8,128)(2,1)S(1)}, u32[]{:S(2)}, u32[]{:S(2)}) %collective-permute-start.11) | collective-permute-done | bytes 102432 | tf_op jit(solution)/shard_map/ppermute | solution.py:284
  64.0 2.1 %collective-permute-done.13.refs_7_ = s16[25,16,128]{2,1,0:T(8,128)(2,1)S(1)} collective-permute-done((s16[25,16,128]{2,1,0:T(8,128)(2,1)S(1)}, s16[25,16,128]{2,1,0:T(8,128)(2,1)S(1)}, u32[]{:S(2)}, u32[]{:S(2)}) %collective-permute-start.13) | collective-permute-done | bytes 102432 | tf_op jit(solution)/shard_map/ppermute | solution.py:284
  66.1 2.3 %collective-permute-done.8.refs_2_ = s16[25,16,128]{2,1,0:T(8,128)(2,1)S(1)} collective-permute-done((s16[25,16,128]{2,1,0:T(8,128)(2,1)S(1)}, s16[25,16,128]{2,1,0:T(8,128)(2,1)S(1)}, u32[]{:S(2)}, u32[]{:S(2)}) %collective-permute-start.8) | collective-permute-done | bytes 102432 | tf_op jit(solution)/shard_map/ppermute | solution.py:284
  68.4 1.1 %collective-permute-done.9.refs_3_ = s16[25,16,128]{2,1,0:T(8,128)(2,1)S(1)} collective-permute-done((s16[25,16,128]{2,1,0:T(8,128)(2,1)S(1)}, s16[25,16,128]{2,1,0:T(8,128)(2,1)S(1)}, u32[]{:S(2)}, u32[]{:S(2)}) %collective-permute-start.9) | collective-permute-done | bytes 102432 | tf_op jit(solution)/shard_map/ppermute | solution.py:284
  69.5 2.0 %unpack.1 = f32[4,6,2,16,512]{4,3,2,1,0:T(8,128)} custom-call(s32[2]{0:T(128)S(1)} %pad_add_fusion.me_ref, f32[24,16,128]{2,1,0:T(8,128)S(1)} %get-tuple-element.33.refs_0_, s16[25,16,128]{2,1,0:T(8,128)(2,1)S(1)} %collective-permute-done.7.refs_1_, s16[25,16,128]{2,1,0:T(8,128)(2,1)S(1)} %collective-permute-done.8.refs_2_, ...), custom_call_target="tpu_custom_call" | custom-call | tf_op jit(solution)/shard_map/unpack/pallas_call | solution.py:273
  (26 shorter events, 2.5 us)
Async XLA Ops:
  0.0 1.1 %copy-start = (bf16[4,6,8,4,512]{4,3,2,1,0:T(4,128)(2,1)S(1)}, bf16[4,6,8,4,512]{4,3,2,1,0:T(4,128)(2,1)}, u32[]{:S(2)}) copy-start(bf16[4,6,8,4,512]{4,3,2,1,0:T(4,128)(2,1)} %screened_ref.1) | copy-start | bytes 2359300
  1.1 0.7 copy-start.3
  1.8 9.1 %copy-start.1 = (bf16[4,6,2,16,512]{4,3,2,1,0:T(8,128)(2,1)S(1)}, bf16[4,6,2,16,512]{4,3,2,1,0:T(8,128)(2,1)}, u32[]{:S(2)}) copy-start(bf16[4,6,2,16,512]{4,3,2,1,0:T(8,128)(2,1)} %green_ref.1) | copy-start | bytes 2359300
  3.5 25.6 %copy-start.4 = (s32[8,8,3]{1,0,2:T(8,128)S(1)}, s32[8,8,3]{1,0,2:T(8,128)}, u32[]{:S(2)}) copy-start(s32[8,8,3]{1,0,2:T(8,128)} %param.8) | copy-start | bytes 2308
  3.5 29.5 %copy-start.2 = (s32[8,8]{1,0:T(8,128)S(1)}, s32[8,8]{1,0:T(8,128)}, u32[]{:S(2)}) copy-start(s32[8,8]{1,0:T(8,128)} %count_ref.5) | copy-start | bytes 772
  3.5 28.7 %all-to-all-start = ((bf16[32,24,4,128]{3,2,1,0:T(4,128)(2,1)}), bf16[32,24,4,128]{3,2,1,0:T(4,128)(2,1)S(1)}, u32[]{:S(2)}, u32[]{:S(2)}) async-start(bf16[32,24,4,128]{3,2,1,0:T(4,128)(2,1)} %pick_screened.1), calls=%async_computation | async-start | bytes 1572864 | tf_op jit(solution)/shard_map/all_to_all | solution.py:289
  11.6 4.7 %collective-permute-start = (bf16[24,16,128]{2,1,0:T(8,128)(2,1)S(1)}, bf16[24,16,128]{2,1,0:T(8,128)(2,1)S(1)}, u32[]{:S(2)}, u32[]{:S(2)}) collective-permute-start(bf16[24,16,128]{2,1,0:T(8,128)(2,1)S(1)} %get-tuple-element.24), channel_id=1, source_target_pairs={{0,4},{4,0},{8,12},{12,8},{16,20},{20,16},{24,28},{28,24},{1,5},{5... | collective-permute-start | bytes 294920 | tf_op jit(solution)/shard_map/ppermute | solution.py:284
  11.9 14.7 %collective-permute-start.1 = (bf16[24,16,128]{2,1,0:T(8,128)(2,1)S(1)}, bf16[24,16,128]{2,1,0:T(8,128)(2,1)S(1)}, u32[]{:S(2)}, u32[]{:S(2)}) collective-permute-start(bf16[24,16,128]{2,1,0:T(8,128)(2,1)S(1)} %get-tuple-element.25), channel_id=1, source_target_pairs={{0,8},{4,12},{8,0},{12,4},{16,24},{20,28},{24,16},{28,20},{1,9},{5... | collective-permute-start | bytes 294920 | tf_op jit(solution)/shard_map/ppermute | solution.py:284
  13.6 15.6 %collective-permute-start.2 = (bf16[24,16,128]{2,1,0:T(8,128)(2,1)S(1)}, bf16[24,16,128]{2,1,0:T(8,128)(2,1)S(1)}, u32[]{:S(2)}, u32[]{:S(2)}) collective-permute-start(bf16[24,16,128]{2,1,0:T(8,128)(2,1)S(1)} %get-tuple-element.26), channel_id=1, source_target_pairs={{0,12},{4,8},{8,4},{12,0},{16,28},{20,24},{24,20},{28,16},{1,13},{... | collective-permute-start | bytes 294920 | tf_op jit(solution)/shard_map/ppermute | solution.py:284
  13.6 28.8 %collective-permute-start.3 = (bf16[24,16,128]{2,1,0:T(8,128)(2,1)S(1)}, bf16[24,16,128]{2,1,0:T(8,128)(2,1)S(1)}, u32[]{:S(2)}, u32[]{:S(2)}) collective-permute-start(bf16[24,16,128]{2,1,0:T(8,128)(2,1)S(1)} %get-tuple-element.29), channel_id=1, source_target_pairs={{0,16},{4,20},{8,24},{12,28},{16,0},{20,4},{24,8},{28,12},{1,17},{... | collective-permute-start | bytes 294920 | tf_op jit(solution)/shard_map/ppermute | solution.py:284
  16.2 27.4 %collective-permute-start.4 = (bf16[24,16,128]{2,1,0:T(8,128)(2,1)S(1)}, bf16[24,16,128]{2,1,0:T(8,128)(2,1)S(1)}, u32[]{:S(2)}, u32[]{:S(2)}) collective-permute-start(bf16[24,16,128]{2,1,0:T(8,128)(2,1)S(1)} %get-tuple-element.30), channel_id=1, source_target_pairs={{0,20},{4,16},{8,28},{12,24},{16,4},{20,0},{24,12},{28,8},{1,21},{... | collective-permute-start | bytes 294920 | tf_op jit(solution)/shard_map/ppermute | solution.py:284
  16.3 27.3 %collective-permute-start.5 = (bf16[24,16,128]{2,1,0:T(8,128)(2,1)S(1)}, bf16[24,16,128]{2,1,0:T(8,128)(2,1)S(1)}, u32[]{:S(2)}, u32[]{:S(2)}) collective-permute-start(bf16[24,16,128]{2,1,0:T(8,128)(2,1)S(1)} %get-tuple-element.31), channel_id=1, source_target_pairs={{0,24},{4,28},{8,16},{12,20},{16,8},{20,12},{24,0},{28,4},{1,25},{... | collective-permute-start | bytes 294920 | tf_op jit(solution)/shard_map/ppermute | solution.py:284
  26.6 17.0 %collective-permute-start.6 = (bf16[24,16,128]{2,1,0:T(8,128)(2,1)S(1)}, bf16[24,16,128]{2,1,0:T(8,128)(2,1)S(1)}, u32[]{:S(2)}, u32[]{:S(2)}) collective-permute-start(bf16[24,16,128]{2,1,0:T(8,128)(2,1)S(1)} %get-tuple-element.32), channel_id=1, source_target_pairs={{0,28},{4,24},{8,20},{12,16},{16,12},{20,8},{24,4},{28,0},{1,29},{... | collective-permute-start | bytes 294920 | tf_op jit(solution)/shard_map/ppermute | solution.py:284
  46.9 12.7 %collective-permute-start.10 = (s16[25,16,128]{2,1,0:T(8,128)(2,1)S(1)}, s16[25,16,128]{2,1,0:T(8,128)(2,1)S(1)}, u32[]{:S(2)}, u32[]{:S(2)}) collective-permute-start(s16[25,16,128]{2,1,0:T(8,128)(2,1)S(1)} %get-tuple-element.37), channel_id=1, source_target_pairs={{0,16},{4,20},{8,24},{12,28},{16,0},{20,4},{24,8},{28,12},{1,17},{... | collective-permute-start | bytes 307208 | tf_op jit(solution)/shard_map/ppermute | solution.py:284
  52.0 12.0 %collective-permute-start.11 = (s16[25,16,128]{2,1,0:T(8,128)(2,1)S(1)}, s16[25,16,128]{2,1,0:T(8,128)(2,1)S(1)}, u32[]{:S(2)}, u32[]{:S(2)}) collective-permute-start(s16[25,16,128]{2,1,0:T(8,128)(2,1)S(1)} %get-tuple-element.38), channel_id=1, source_target_pairs={{0,20},{4,16},{8,28},{12,24},{16,4},{20,0},{24,12},{28,8},{1,21},{... | collective-permute-start | bytes 307208 | tf_op jit(solution)/shard_map/ppermute | solution.py:284
  54.7 9.4 %collective-permute-start.12 = (s16[25,16,128]{2,1,0:T(8,128)(2,1)S(1)}, s16[25,16,128]{2,1,0:T(8,128)(2,1)S(1)}, u32[]{:S(2)}, u32[]{:S(2)}) collective-permute-start(s16[25,16,128]{2,1,0:T(8,128)(2,1)S(1)} %get-tuple-element.39), channel_id=1, source_target_pairs={{0,24},{4,28},{8,16},{12,20},{16,8},{20,12},{24,0},{28,4},{1,25},{... | collective-permute-start | bytes 307208 | tf_op jit(solution)/shard_map/ppermute | solution.py:284
  59.1 7.1 %collective-permute-start.13 = (s16[25,16,128]{2,1,0:T(8,128)(2,1)S(1)}, s16[25,16,128]{2,1,0:T(8,128)(2,1)S(1)}, u32[]{:S(2)}, u32[]{:S(2)}) collective-permute-start(s16[25,16,128]{2,1,0:T(8,128)(2,1)S(1)} %get-tuple-element.40), channel_id=1, source_target_pairs={{0,28},{4,24},{8,20},{12,16},{16,12},{20,8},{24,4},{28,0},{1,29},{... | collective-permute-start | bytes 307208 | tf_op jit(solution)/shard_map/ppermute | solution.py:284
  59.1 7.1 %collective-permute-start.7 = (s16[25,16,128]{2,1,0:T(8,128)(2,1)S(1)}, s16[25,16,128]{2,1,0:T(8,128)(2,1)S(1)}, u32[]{:S(2)}, u32[]{:S(2)}) collective-permute-start(s16[25,16,128]{2,1,0:T(8,128)(2,1)S(1)} %get-tuple-element.34), channel_id=1, source_target_pairs={{0,4},{4,0},{8,12},{12,8},{16,20},{20,16},{24,28},{28,24},{1,5},{5... | collective-permute-start | bytes 307208 | tf_op jit(solution)/shard_map/ppermute | solution.py:284
  59.6 8.8 %collective-permute-start.8 = (s16[25,16,128]{2,1,0:T(8,128)(2,1)S(1)}, s16[25,16,128]{2,1,0:T(8,128)(2,1)S(1)}, u32[]{:S(2)}, u32[]{:S(2)}) collective-permute-start(s16[25,16,128]{2,1,0:T(8,128)(2,1)S(1)} %get-tuple-element.35), channel_id=1, source_target_pairs={{0,8},{4,12},{8,0},{12,4},{16,24},{20,28},{24,16},{28,20},{1,9},{5... | collective-permute-start | bytes 307208 | tf_op jit(solution)/shard_map/ppermute | solution.py:284
  64.0 5.5 %collective-permute-start.9 = (s16[25,16,128]{2,1,0:T(8,128)(2,1)S(1)}, s16[25,16,128]{2,1,0:T(8,128)(2,1)S(1)}, u32[]{:S(2)}, u32[]{:S(2)}) collective-permute-start(s16[25,16,128]{2,1,0:T(8,128)(2,1)S(1)} %get-tuple-element.36), channel_id=1, source_target_pairs={{0,12},{4,8},{8,4},{12,0},{16,28},{20,24},{24,20},{28,16},{1,13},{... | collective-permute-start | bytes 307208 | tf_op jit(solution)/shard_map/ppermute | solution.py:284

commit v5 on v4

v5 whole, which is shorter than its diff:
```python
import functools

import jax
import jax.numpy as jnp
from jax import lax
from jax.experimental import pallas as pl
from jax.experimental.pallas import tpu as pltpu
from jax.sharding import PartitionSpec as P

SCALE = 0.2
LANES = 128
PAIR = 2
STEPS = 32700.0
FINE = 64.0
TINY = 1e-34
SMEM = pl.BlockSpec(memory_space=pltpu.SMEM)
VMEM = pl.BlockSpec(memory_space=pltpu.VMEM)
ANY = pl.BlockSpec(memory_space=pl.ANY)
PARAMS = pltpu.CompilerParams(vmem_limit_bytes=32 * 1024 * 1024)


class Sizes:
    def __init__(self, green, screened, groups, cells):
        self.comps, self.energies, self.per_cell, self.rows, self.width = green.shape
        self.groups, self.cells = groups, cells
        self.tiles = self.width // LANES
        self.slices = groups // self.per_cell
        self.parts = self.slices // self.tiles
        self.held = screened.shape[3]
        self.plane = (self.rows // self.parts, LANES)
        self.planes = self.comps * self.energies
        self.half = groups // 2
        self.held_planes = (self.half + 2) * self.energies
        self.scales = self.planes // PAIR
        self.scale_planes = -(-self.scales // self.plane[0])

    def where(self, index):
        cell, tile, part = index // self.slices, (index // self.parts) % self.tiles, index % self.parts
        return cell, part, pl.ds(pl.multiple_of(tile * LANES, LANES), LANES)


def part_of(s, value, part):
    count = value.shape[0] // s.parts
    chosen = value[:count]
    for other in range(1, s.parts):
        chosen = jnp.where(part == other, value[other * count : (other + 1) * count], chosen)
    return chosen


def pick_kernel(s, map_hbm, screened_hbm, out_hbm, map_ref, screened_ref, out_ref, in_sems, out_sems, map_sem):
    chunks = [pl.ds(comp * s.energies, s.energies) for comp in range(s.comps)]
    arriving = [
        pltpu.make_async_copy(screened_hbm.at[chunk], screened_ref.at[chunk], in_sems.at[i])
        for i, chunk in enumerate(chunks)
    ]
    leaving = [
        pltpu.make_async_copy(out_ref.at[:, chunk], out_hbm.at[:, chunk], out_sems.at[i])
        for i, chunk in enumerate(chunks)
    ]
    mapped = pltpu.make_async_copy(map_hbm, map_ref, map_sem)
    mapped.start()
    for copy in arriving:
        copy.start()
    mapped.wait()
    picked = [map_ref[i] for i in range(s.cells * s.per_cell)]
    for comp in range(s.comps):
        arriving[comp].wait()
        for plane in range(comp * s.energies, (comp + 1) * s.energies):
            for i, cell in enumerate(picked):
                for t in range(s.tiles):
                    target = (i % s.per_cell * s.slices + t) * s.cells + i // s.per_cell
                    out_ref[target, plane] = screened_ref[plane, cell, :, t * LANES : (t + 1) * LANES]
        leaving[comp].start()
    for copy in leaving:
        copy.wait()


def pick_screened(s, cell_map, screened):
    out = jax.ShapeDtypeStruct((s.groups * s.cells, s.planes, s.held, LANES), screened.dtype)
    flat = screened.reshape((s.planes,) + screened.shape[2:])
    return pl.pallas_call(
        functools.partial(pick_kernel, s),
        out_shape=out,
        in_specs=[ANY, ANY],
        out_specs=ANY,
        scratch_shapes=[
            pltpu.SMEM(cell_map.shape, jnp.int32),
            pltpu.VMEM(flat.shape, flat.dtype),
            pltpu.VMEM(out.shape, out.dtype),
            pltpu.SemaphoreType.DMA((s.comps,)),
            pltpu.SemaphoreType.DMA((s.comps,)),
            pltpu.SemaphoreType.DMA(()),
        ],
        compiler_params=pltpu.CompilerParams(vmem_limit_bytes=60 * 1024 * 1024),
        name="pick_screened",
    )(cell_map, flat)


def cut_kernel(s, me_ref, green_ref, *greens):
    me = me_ref[0]
    places = [s.where(me ^ k) for k in range(s.groups)]

    for plane in range(s.planes):
        for k, (cell, part, lanes) in enumerate(places):
            value = green_ref[plane, cell, :, lanes]
            if s.parts > 1:
                value = part_of(s, value.astype(jnp.float32), part).astype(greens[k].dtype)
            greens[k][plane] = value


def cut_green(s, me, green):
    return pl.pallas_call(
        functools.partial(cut_kernel, s),
        out_shape=[jax.ShapeDtypeStruct((s.planes,) + s.plane, green.dtype)] * s.groups,
        in_specs=[SMEM, VMEM],
        out_specs=[VMEM] * s.groups,
        compiler_params=PARAMS,
        name="cut_green",
    )(me, green.reshape((s.planes,) + green.shape[2:]))


def held(s):
    return jax.ShapeDtypeStruct((s.comps * s.held_planes,) + s.plane, jnp.float32)


def stage_green(s, me, first, blocks, g_half):
    zero = jnp.zeros(s.plane, jnp.float32)
    spots = [((me ^ (first + k)) % s.half + 1) * s.energies for k in range(s.half)]

    @pl.loop(0, s.energies)
    def _(j):
        for comp in range(s.comps):
            base = comp * s.held_planes + j
            g_half[base] = zero
            g_half[base + (s.half + 1) * s.energies] = zero
            for spot, block in zip(spots, blocks):
                g_half[base + spot] = block[comp * s.energies + j].astype(jnp.float32)


def stage_near_kernel(s, me_ref, screens_ref, *refs):
    g_half, w_all = refs[-2:]
    stage_green(s, me_ref[0], 0, refs[:-2], g_half)

    @pl.loop(0, s.planes)
    def _(plane):
        for source in range(s.groups):
            if s.parts > 1:
                w_all[source, plane] = screens_ref[source, plane].astype(jnp.float32)
                continue
            for c in range(s.cells):
                piece = screens_ref[source * s.cells + c, plane].astype(jnp.float32)
                w_all[source, plane, c * s.held : (c + 1) * s.held, :] = piece


def stage_near(s, me, screens, greens):
    return pl.pallas_call(
        functools.partial(stage_near_kernel, s),
        out_shape=[held(s), jax.ShapeDtypeStruct((s.groups, s.planes) + s.plane, jnp.float32)],
        in_specs=[SMEM] + [VMEM] * (len(greens) + 1),
        out_specs=[VMEM] * 2,
        compiler_params=PARAMS,
        name="stage_near",
    )(me, screens, *greens)


def stage_far_kernel(s, me_ref, after_ref, *refs):
    stage_green(s, me_ref[0], s.groups // 2, refs[:-1], refs[-1])


def stage_far(s, me, greens, after):
    return pl.pallas_call(
        functools.partial(stage_far_kernel, s),
        out_shape=held(s),
        in_specs=[SMEM, ANY] + [VMEM] * len(greens),
        out_specs=VMEM,
        compiler_params=PARAMS,
        name="stage_far",
    )(me, after, *greens)


def add_terms(s, slots, side, group, kind, table_ref, count_ref, g_half, w_all, sums):
    low = side * s.half
    real, imag = 2 * kind, 2 * kind + 1

    def turn(source, sums):
        sums = list(sums)
        count = count_ref[group, source]
        for slot in range(slots):
            shift = jnp.clip(table_ref[group * s.groups + source, slot], 0, s.energies - 1)
            live = jnp.where(slot < count, 1.0, 0.0).astype(jnp.float32)
            start = (group - source - low + 1) * s.energies - shift
            w_real = w_all[source, real * s.energies + shift] * live
            w_imag = w_all[source, imag * s.energies + shift] * live
            for j in range(s.energies):
                g_real = g_half[real * s.held_planes + start + j]
                g_imag = g_half[imag * s.held_planes + start + j]
                sums[j] = sums[j] - (g_real * w_imag + g_imag * w_real)
                sums[s.energies + j] = sums[s.energies + j] + (g_real * w_real - g_imag * w_imag)
        return tuple(sums)

    first = jnp.maximum(group - low - s.half, 0)
    return lax.fori_loop(first, jnp.maximum(group - low + 1, first), turn, tuple(sums))


def partial_kernel(s, slots, me_ref, table_ref, count_ref, g_half, w_all, out_ref):
    me = me_ref[0]

    @pl.loop(0, 2 * s.groups)
    def _(at):
        k, kind = at // 2, at % 2
        zeros = [jnp.zeros(s.plane, jnp.float32) for _ in range(2 * s.energies)]
        sums = add_terms(s, slots, me // s.half, me ^ k, kind, table_ref, count_ref, g_half, w_all, zeros)
        for j, total in enumerate(sums):
            out_ref[k, kind * 2 * s.energies + j] = total


def partial_of(s, me, table, count, g_half, w_all):
    return pl.pallas_call(
        functools.partial(partial_kernel, s, table.shape[1]),
        out_shape=jax.ShapeDtypeStruct((s.groups, s.planes) + s.plane, jnp.float32),
        in_specs=[SMEM] * 3 + [VMEM] * 2,
        out_specs=VMEM,
        compiler_params=PARAMS,
        name="partial",
    )(me, table, count, g_half, w_all)


def sigma_kernel(s, slots, ks, me_ref, table_ref, count_ref, begun, w_all, g_far, *outs):
    me = me_ref[0]
    side = me // s.half
    row = lax.broadcasted_iota(jnp.int32, s.plane, 0)
    for at, k in enumerate(ks):

        def turn(kind, codes):
            codes = list(codes)
            first = kind * 2 * s.energies
            sums = [begun[k, first + j] for j in range(2 * s.energies)]
            sums = add_terms(s, slots, 1 - side, me ^ k, kind, table_ref, count_ref, g_far, w_all, sums)
            sums = [total * SCALE for total in sums]
            if k == 0:
                for j, total in enumerate(sums):
                    outs[at][first + j] = total
                return tuple(codes)
            for low in range(0, 2 * s.energies, PAIR):
                pair = sums[low : low + PAIR]
                largest = functools.reduce(jnp.maximum, [jnp.abs(total) for total in pair])
                largest = jnp.maximum(jnp.max(largest, axis=0, keepdims=True), TINY)
                code = jnp.ceil(jnp.log2(largest) * FINE)
                inverse = jnp.exp2(code * (-1.0 / FINE)) * STEPS
                where = (first + low) // PAIR
                for i in range(s.scale_planes):
                    codes[i] = jnp.where(row + i * s.plane[0] == where, code, codes[i])
                for j, total in enumerate(pair):
                    coded = jnp.round(total * inverse).astype(jnp.int32)
                    outs[at][first + low + j] = coded.astype(jnp.int16)
            return tuple(codes)

        codes = lax.fori_loop(0, 2, turn, tuple(jnp.zeros(s.plane, jnp.float32) for _ in range(s.scale_planes)))
        if k != 0:
            for j in range(s.scale_planes):
                outs[at][s.planes + j] = codes[j].astype(jnp.int32).astype(jnp.int16)


def sigma_of(s, me, table, count, begun, w_all, g_far, ks):
    own = jax.ShapeDtypeStruct((s.planes,) + s.plane, jnp.float32)
    coded = jax.ShapeDtypeStruct((s.planes + s.scale_planes,) + s.plane, jnp.int16)
    return pl.pallas_call(
        functools.partial(sigma_kernel, s, table.shape[1], ks),
        out_shape=[own if k == 0 else coded for k in ks],
        in_specs=[SMEM] * 3 + [VMEM] * 3,
        out_specs=[VMEM] * len(ks),
        compiler_params=PARAMS,
        name="sigma",
    )(me, table, count, begun, w_all, g_far)


def unpack_kernel(s, order, me_ref, *refs):
    at = dict(zip(order, refs))
    blocks, whole_ref, scales = [at[k] for k in range(s.groups)], refs[s.groups], refs[s.groups + 1]
    me = me_ref[0]
    places = []
    for k, block in enumerate(blocks):
        cell, part, lanes = s.where(me ^ k)
        places.append((cell, slice(None) if s.parts == 1 else pl.ds(pl.multiple_of(part * s.plane[0], s.plane[0]), s.plane[0]), lanes))
        if k != 0:
            for j in range(s.scale_planes):
                code = block[s.planes + j].astype(jnp.int32).astype(jnp.float32)
                scales[k, j * s.plane[0] : (j + 1) * s.plane[0]] = jnp.exp2(code * (1.0 / FINE)) * (1.0 / STEPS)

    @pl.loop(0, s.scales)
    def _(pair):
        for k, (cell, rows, lanes) in enumerate(places):
            for i in range(PAIR):
                value = blocks[k][pair * PAIR + i]
                if k != 0:
                    value = value.astype(jnp.int32).astype(jnp.float32) * scales[k, pl.ds(pair, 1)]
                whole_ref[pair * PAIR + i, cell, rows, lanes] = value


def unpack(s, me, blocks, order):
    return pl.pallas_call(
        functools.partial(unpack_kernel, s, order),
        out_shape=jax.ShapeDtypeStruct((s.planes, s.per_cell, s.rows, s.width), jnp.float32),
        in_specs=[SMEM] + [VMEM] * s.groups,
        out_specs=VMEM,
        scratch_shapes=[pltpu.VMEM((s.groups, s.scale_planes * s.plane[0], LANES), jnp.float32)],
        compiler_params=PARAMS,
        name="unpack",
    )(me, *[blocks[k] for k in order])


def swap(s, block, k):
    return block if k == 0 else lax.ppermute(block, "energy", [(i, i ^ k) for i in range(s.groups)])


def send_screened(s, cell_map, screened):
    if s.parts == 1:
        return lax.all_to_all(pick_screened(s, cell_map, screened), ("energy", "cell"), 0, 0, tiled=True)
    chosen = jnp.take(screened, cell_map, axis=2).reshape(s.planes, s.cells, s.per_cell, s.held, s.width)
    whole = lax.all_to_all(chosen, "cell", 1, 3, tiled=True)
    cut = whole.reshape(s.planes, s.per_cell, s.parts, s.plane[0], s.tiles, LANES)
    cut = jnp.transpose(cut, (1, 4, 2, 0, 3, 5)).reshape((s.groups, s.planes) + s.plane)
    return lax.all_to_all(cut, "energy", 0, 0, tiled=True)


def per_device(green, screened, cell_map, shift_table, shift_count):
    s = Sizes(green, screened, lax.axis_size("energy"), lax.axis_size("cell"))
    me = lax.axis_index("energy").astype(jnp.int32).reshape(1)
    half = s.groups // 2
    far, near = list(range(half, s.groups)), list(range(half))

    screens = send_screened(s, cell_map, screened)
    greens = [swap(s, block, k) for k, block in enumerate(cut_green(s, me, green))]
    table = shift_table.reshape(s.groups * s.groups, shift_table.shape[2])
    g_near, w_all = stage_near(s, me, screens, greens[:half])
    begun = partial_of(s, me, table, shift_count, g_near, w_all)
    g_far = stage_far(s, me, greens[half:], begun)
    first, later = far[:2], [0] + far[2:] + near[1:]
    sums = {}
    for ks in (first, later):
        for k, block in zip(ks, sigma_of(s, me, table, shift_count, begun, w_all, g_far, ks)):
            sums[k] = swap(s, block, k)
    return unpack(s, me, sums, later + first).reshape(green.shape)


def solution(mesh):
    placed = (
        P(None, "energy", "cell", None, None),
        P(None, "energy", None, "cell", None),
        P(),
        P(),
        P(),
    )
    return jax.shard_map(
        per_device,
        mesh=mesh,
        in_specs=placed,
        out_specs=P(None, "energy", "cell", None, None),
        check_vma=False,
    )
```

time: 72.2 us -> 69.6 us (0.964)
  starting transfers between devices: 28.4 us -> 30.9 us
  waiting for transfers between devices: 26.5 us -> 24.6 us
  local copies, waits for them, and re-layouts: 1.92 us -> 0.14 us
  Pallas kernels: 14.5 us -> 13.6 us
    ppermute x14, starting transfers between devices: 21.1 us -> 23.6 us  [swap(): lax.ppermute(block, 'energy', [(i, i ^ k) for i in range(s.groups)])]
    ppermute x14, waiting for transfers between devices: 23.5 us -> 21.6 us  [swap(): lax.ppermute(block, 'energy', [(i, i ^ k) for i in range(s.groups)])]
    unnamed x11 -> x7, local copies, waits for them, and re-layouts: 1.92 us -> 0.14 us
  transfers between devices with their start and end apart: 15 -> 15, of which waited for: 9 -> 8; matrix products, arithmetic and copies ran while one was open for 0% -> 0% of each run, Pallas kernels for 11% -> 12%
where the time goes in v5:
time: 69.6 us; the launch traced here: 69.4 us
  starting transfers between devices  30.9 us (44%)
  waiting for transfers between devices  24.6 us (35%)
  Pallas kernels  13.6 us (20%)
    ppermute x14, starting transfers between devices, swap(): lax.ppermute(block, 'energy', [(i, i ^ k) for i in range(s.groups)])  23.6 us
    ppermute x14, waiting for transfers between devices, swap(): lax.ppermute(block, 'energy', [(i, i ^ k) for i in range(s.groups)])  21.6 us
    all_to_all x1, starting transfers between devices, send_screened(): lax.all_to_all(pick_screened(s, cell_map, screened), ('energy', 'cell'),...  7.3 us
    pallas_call x1, Pallas kernels, partial_of(): pl.pallas_call(functools.partial(partial_kernel, s, table.shape[1]), out_...  5.05 us
    pallas_call x2, Pallas kernels, sigma_of(): pl.pallas_call(functools.partial(sigma_kernel, s, table.shape[1], ks), ou...  4.27 us
    all_to_all x1, waiting for transfers between devices, send_screened(): lax.all_to_all(pick_screened(s, cell_map, screened), ('energy', 'cell'),...  3.01 us
    pallas_call x1, Pallas kernels, pick_screened(): pl.pallas_call(functools.partial(pick_kernel, s), out_shape=out, in_specs...  2.11 us
    pallas_call x1, Pallas kernels, unpack(): pl.pallas_call(functools.partial(unpack_kernel, s, order), out_shape=jax....  1.54 us
  transfers between devices with their start and end apart: 15, of which 8 were waited for; matrix products, arithmetic and copies ran while one was open for 0% of the time, Pallas kernels for 12%

profile of v5, /device:TPU:0, one launch (start us, length us, event | category | flops | bytes accessed | tf_op | source)
XLA Modules:
  0.0 69.4 jit_solution(1632368620453241959)
XLA Ops:
  0.0 2.1 %pick_screened.1 = bf16[32,24,4,128]{3,2,1,0:T(4,128)(2,1)} custom-call(s32[8]{0:T(128)} %map_hbm.1, bf16[24,8,4,512]{3,2,1,0:T(4,128)(2,1)} %bitcast.9), custom_call_target="tpu_custom_call" | custom-call | tf_op jit(solution)/shard_map/pick_screened/pallas_call | solution.py:81
  2.1 7.3 %all-to-all-start = ((bf16[32,24,4,128]{3,2,1,0:T(4,128)(2,1)}), bf16[32,24,4,128]{3,2,1,0:T(4,128)(2,1)S(1)}, u32[]{:S(2)}, u32[]{:S(2)}) async-start(bf16[32,24,4,128]{3,2,1,0:T(4,128)(2,1)} %pick_screened.1), calls=%async_computation | async-start | bytes 1572864 | tf_op jit(solution)/shard_map/all_to_all | solution.py:318
  10.0 1.7 %collective-permute-start.1 = (bf16[24,16,128]{2,1,0:T(8,128)(2,1)S(1)}, bf16[24,16,128]{2,1,0:T(8,128)(2,1)S(1)}, u32[]{:S(2)}, u32[]{:S(2)}) collective-permute-start(bf16[24,16,128]{2,1,0:T(8,128)(2,1)S(1)} %get-tuple-element.25), channel_id=1, source_target_pairs={{0,8},{4,12},{8,0},{12,4},{16,24},{20,28},{24,16},{28,20},{1,9},{5... | collective-permute-start | bytes 294920 | tf_op jit(solution)/shard_map/ppermute | solution.py:313
  11.6 2.6 %collective-permute-start.3 = (bf16[24,16,128]{2,1,0:T(8,128)(2,1)S(1)}, bf16[24,16,128]{2,1,0:T(8,128)(2,1)S(1)}, u32[]{:S(2)}, u32[]{:S(2)}) collective-permute-start(bf16[24,16,128]{2,1,0:T(8,128)(2,1)S(1)} %get-tuple-element.29), channel_id=1, source_target_pairs={{0,16},{4,20},{8,24},{12,28},{16,0},{20,4},{24,8},{28,12},{1,17},{... | collective-permute-start | bytes 294920 | tf_op jit(solution)/shard_map/ppermute | solution.py:313
  14.3 3.5 %collective-permute-start.5 = (bf16[24,16,128]{2,1,0:T(8,128)(2,1)S(1)}, bf16[24,16,128]{2,1,0:T(8,128)(2,1)S(1)}, u32[]{:S(2)}, u32[]{:S(2)}) collective-permute-start(bf16[24,16,128]{2,1,0:T(8,128)(2,1)S(1)} %get-tuple-element.31), channel_id=1, source_target_pairs={{0,24},{4,28},{8,16},{12,20},{16,8},{20,12},{24,0},{28,4},{1,25},{... | collective-permute-start | bytes 294920 | tf_op jit(solution)/shard_map/ppermute | solution.py:313
  17.9 7.4 %collective-permute-done.1.refs_2_ = bf16[24,16,128]{2,1,0:T(8,128)(2,1)S(1)} collective-permute-done((bf16[24,16,128]{2,1,0:T(8,128)(2,1)S(1)}, bf16[24,16,128]{2,1,0:T(8,128)(2,1)S(1)}, u32[]{:S(2)}, u32[]{:S(2)}) %collective-permute-start.1) | collective-permute-done | bytes 98336 | tf_op jit(solution)/shard_map/ppermute | solution.py:313
  25.2 2.5 %collective-permute-start.6 = (bf16[24,16,128]{2,1,0:T(8,128)(2,1)S(1)}, bf16[24,16,128]{2,1,0:T(8,128)(2,1)S(1)}, u32[]{:S(2)}, u32[]{:S(2)}) collective-permute-start(bf16[24,16,128]{2,1,0:T(8,128)(2,1)S(1)} %get-tuple-element.32), channel_id=1, source_target_pairs={{0,28},{4,24},{8,20},{12,16},{16,12},{20,8},{24,4},{28,0},{1,29},{... | collective-permute-start | bytes 294920 | tf_op jit(solution)/shard_map/ppermute | solution.py:313
  27.8 3.0 %all-to-all-done.screens_ref = bf16[32,24,4,128]{3,2,1,0:T(4,128)(2,1)S(1)} async-done(((bf16[32,24,4,128]{3,2,1,0:T(4,128)(2,1)}), bf16[32,24,4,128]{3,2,1,0:T(4,128)(2,1)S(1)}, u32[]{:S(2)}, u32[]{:S(2)}) %all-to-all-start) | async-done | bytes 786464 | tf_op jit(solution)/shard_map/all_to_all | solution.py:318
  30.8 0.4 stage_near.1
  31.2 5.1 %partial.1.after_ref.begun = f32[8,24,16,128]{3,2,1,0:T(8,128)S(1)} custom-call(s32[1]{0:T(128)} %bitcast.me_ref, s32[64,3]{1,0:T(8,128)S(1)} %bitcast.6, s32[8,8]{1,0:T(8,128)S(1)} %copy-done.1, f32[144,16,128]{2,1,0:T(8,128)S(1)} %get-tuple-element.27.g_half, f32[8,24,16,128]{3,2,1,0:T(8,128)S(1)} %get-tuple-element.28.w_all), custom_call_target="tpu_custom_call" | custom-call | tf_op jit(solution)/shard_map/partial/pallas_call | solution.py:218
  36.3 4.8 %collective-permute-done.3.refs_0_ = bf16[24,16,128]{2,1,0:T(8,128)(2,1)S(1)} collective-permute-done((bf16[24,16,128]{2,1,0:T(8,128)(2,1)S(1)}, bf16[24,16,128]{2,1,0:T(8,128)(2,1)S(1)}, u32[]{:S(2)}, u32[]{:S(2)}) %collective-permute-start.3) | collective-permute-done | bytes 98336 | tf_op jit(solution)/shard_map/ppermute | solution.py:313
  41.1 1.2 %collective-permute-done.4.refs_1_ = bf16[24,16,128]{2,1,0:T(8,128)(2,1)S(1)} collective-permute-done((bf16[24,16,128]{2,1,0:T(8,128)(2,1)S(1)}, bf16[24,16,128]{2,1,0:T(8,128)(2,1)S(1)}, u32[]{:S(2)}, u32[]{:S(2)}) %collective-permute-start.4) | collective-permute-done | bytes 98336 | tf_op jit(solution)/shard_map/ppermute | solution.py:313
  42.4 1.7 %sigma.3 = (s16[25,16,128]{2,1,0:T(8,128)(2,1)S(1)}, s16[25,16,128]{2,1,0:T(8,128)(2,1)S(1)}) custom-call(s32[1]{0:T(128)} %bitcast.me_ref, s32[64,3]{1,0:T(8,128)S(1)} %bitcast.7, s32[8,8]{1,0:T(8,128)S(1)} %copy-done.1, f32[8,24,16,128]{3,2,1,0:T(8,128)S(1)} %partial.1.after_ref.begun, f32[8,24,16,128]{3,2,1,0:T(8,128)S(1)} %get-tuple-element.28.w_all, ...), custom_call_target="tpu_custom_call" | custom-call | tf_op jit(solution)/shard_map/sigma/pallas_call | solution.py:267
  44.1 5.1 %collective-permute-start.12 = (s16[25,16,128]{2,1,0:T(8,128)(2,1)S(1)}, s16[25,16,128]{2,1,0:T(8,128)(2,1)S(1)}, u32[]{:S(2)}, u32[]{:S(2)}) collective-permute-start(s16[25,16,128]{2,1,0:T(8,128)(2,1)S(1)} %get-tuple-element.39), channel_id=1, source_target_pairs={{0,16},{4,20},{8,24},{12,28},{16,0},{20,4},{24,8},{28,12},{1,17},{... | collective-permute-start | bytes 307208 | tf_op jit(solution)/shard_map/ppermute | solution.py:313
  49.2 2.6 %sigma.2 = (f32[24,16,128]{2,1,0:T(8,128)S(1)}, s16[25,16,128]{2,1,0:T(8,128)(2,1)S(1)}, s16[25,16,128]{2,1,0:T(8,128)(2,1)S(1)}, s16[25,16,128]{2,1,0:T(8,128)(...) custom-call(s32[1]{0:T(128)} %bitcast.me_ref, s32[64,3]{1,0:T(8,128)S(1)} %bitcast.8, ...), custom_call_target="tpu_custom_call" | custom-call | tf_op jit(solution)/shard_map/sigma/pallas_call | solution.py:267
  51.8 2.3 %collective-permute-start.10 = (s16[25,16,128]{2,1,0:T(8,128)(2,1)S(1)}, s16[25,16,128]{2,1,0:T(8,128)(2,1)S(1)}, u32[]{:S(2)}, u32[]{:S(2)}) collective-permute-start(s16[25,16,128]{2,1,0:T(8,128)(2,1)S(1)} %get-tuple-element.37), channel_id=1, source_target_pairs={{0,8},{4,12},{8,0},{12,4},{16,24},{20,28},{24,16},{28,20},{1,9},{5... | collective-permute-start | bytes 307208 | tf_op jit(solution)/shard_map/ppermute | solution.py:313
  54.3 4.0 %collective-permute-start.7 = (s16[25,16,128]{2,1,0:T(8,128)(2,1)S(1)}, s16[25,16,128]{2,1,0:T(8,128)(2,1)S(1)}, u32[]{:S(2)}, u32[]{:S(2)}) collective-permute-start(s16[25,16,128]{2,1,0:T(8,128)(2,1)S(1)} %get-tuple-element.34), channel_id=1, source_target_pairs={{0,24},{4,28},{8,16},{12,20},{16,8},{20,12},{24,0},{28,4},{1,25},{... | collective-permute-start | bytes 307208 | tf_op jit(solution)/shard_map/ppermute | solution.py:313
  58.4 0.6 collective-permute-start.8
  58.9 0.4 collective-permute-done.13.refs_7_
  59.3 0.6 collective-permute-start.9
  60.0 1.8 %collective-permute-done.11.refs_5_ = s16[25,16,128]{2,1,0:T(8,128)(2,1)S(1)} collective-permute-done((s16[25,16,128]{2,1,0:T(8,128)(2,1)S(1)}, s16[25,16,128]{2,1,0:T(8,128)(2,1)S(1)}, u32[]{:S(2)}, u32[]{:S(2)}) %collective-permute-start.11) | collective-permute-done | bytes 102432 | tf_op jit(solution)/shard_map/ppermute | solution.py:313
  61.8 4.4 %collective-permute-done.7.refs_1_ = s16[25,16,128]{2,1,0:T(8,128)(2,1)S(1)} collective-permute-done((s16[25,16,128]{2,1,0:T(8,128)(2,1)S(1)}, s16[25,16,128]{2,1,0:T(8,128)(2,1)S(1)}, u32[]{:S(2)}, u32[]{:S(2)}) %collective-permute-start.7) | collective-permute-done | bytes 102432 | tf_op jit(solution)/shard_map/ppermute | solution.py:313
  66.2 1.6 %collective-permute-done.8.refs_2_ = s16[25,16,128]{2,1,0:T(8,128)(2,1)S(1)} collective-permute-done((s16[25,16,128]{2,1,0:T(8,128)(2,1)S(1)}, s16[25,16,128]{2,1,0:T(8,128)(2,1)S(1)}, u32[]{:S(2)}, u32[]{:S(2)}) %collective-permute-start.8) | collective-permute-done | bytes 102432 | tf_op jit(solution)/shard_map/ppermute | solution.py:313
  67.8 1.5 %unpack.1 = f32[24,2,16,512]{3,2,1,0:T(8,128)} custom-call(s32[1]{0:T(128)} %bitcast.me_ref, f32[24,16,128]{2,1,0:T(8,128)S(1)} %get-tuple-element.33.refs_0_, s16[25,16,128]{2,1,0:T(8,128)(2,1)S(1)} %collective-permute-done.7.refs_1_, s16[25,16,128]{2,1,0:T(8,128)(2,1)S(1)} %collective-permute-done.8.refs_2_, ...), custom_call_target="tpu_custom_call" | custom-call | tf_op jit(solution)/shard_map/unpack/pallas_call | solution.py:301
  (21 shorter events, 1.0 us)
Async XLA Ops:
  0.0 9.5 %copy-start = (bf16[4,6,2,16,512]{4,3,2,1,0:T(8,128)(2,1)S(1)}, bf16[4,6,2,16,512]{4,3,2,1,0:T(8,128)(2,1)}, u32[]{:S(2)}) copy-start(bf16[4,6,2,16,512]{4,3,2,1,0:T(8,128)(2,1)} %param.5) | copy-start | bytes 2359300
  2.1 25.6 %copy-start.2 = (s32[8,8,3]{1,0,2:T(8,128)S(1)}, s32[8,8,3]{1,0,2:T(8,128)}, u32[]{:S(2)}) copy-start(s32[8,8,3]{1,0,2:T(8,128)} %param.8) | copy-start | bytes 2308
  2.1 29.1 %copy-start.1 = (s32[8,8]{1,0:T(8,128)S(1)}, s32[8,8]{1,0:T(8,128)}, u32[]{:S(2)}) copy-start(s32[8,8]{1,0:T(8,128)} %count_ref.5) | copy-start | bytes 772
  2.1 28.7 %all-to-all-start = ((bf16[32,24,4,128]{3,2,1,0:T(4,128)(2,1)}), bf16[32,24,4,128]{3,2,1,0:T(4,128)(2,1)S(1)}, u32[]{:S(2)}, u32[]{:S(2)}) async-start(bf16[32,24,4,128]{3,2,1,0:T(4,128)(2,1)} %pick_screened.1), calls=%async_computation | async-start | bytes 1572864 | tf_op jit(solution)/shard_map/all_to_all | solution.py:318
  9.6 4.7 %collective-permute-start = (bf16[24,16,128]{2,1,0:T(8,128)(2,1)S(1)}, bf16[24,16,128]{2,1,0:T(8,128)(2,1)S(1)}, u32[]{:S(2)}, u32[]{:S(2)}) collective-permute-start(bf16[24,16,128]{2,1,0:T(8,128)(2,1)S(1)} %get-tuple-element.24), channel_id=1, source_target_pairs={{0,4},{4,0},{8,12},{12,8},{16,20},{20,16},{24,28},{28,24},{1,5},{5... | collective-permute-start | bytes 294920 | tf_op jit(solution)/shard_map/ppermute | solution.py:313
  10.0 15.3 %collective-permute-start.1 = (bf16[24,16,128]{2,1,0:T(8,128)(2,1)S(1)}, bf16[24,16,128]{2,1,0:T(8,128)(2,1)S(1)}, u32[]{:S(2)}, u32[]{:S(2)}) collective-permute-start(bf16[24,16,128]{2,1,0:T(8,128)(2,1)S(1)} %get-tuple-element.25), channel_id=1, source_target_pairs={{0,8},{4,12},{8,0},{12,4},{16,24},{20,28},{24,16},{28,20},{1,9},{5... | collective-permute-start | bytes 294920 | tf_op jit(solution)/shard_map/ppermute | solution.py:313
  11.6 16.2 %collective-permute-start.2 = (bf16[24,16,128]{2,1,0:T(8,128)(2,1)S(1)}, bf16[24,16,128]{2,1,0:T(8,128)(2,1)S(1)}, u32[]{:S(2)}, u32[]{:S(2)}) collective-permute-start(bf16[24,16,128]{2,1,0:T(8,128)(2,1)S(1)} %get-tuple-element.26), channel_id=1, source_target_pairs={{0,12},{4,8},{8,4},{12,0},{16,28},{20,24},{24,20},{28,16},{1,13},{... | collective-permute-start | bytes 294920 | tf_op jit(solution)/shard_map/ppermute | solution.py:313
  11.6 29.5 %collective-permute-start.3 = (bf16[24,16,128]{2,1,0:T(8,128)(2,1)S(1)}, bf16[24,16,128]{2,1,0:T(8,128)(2,1)S(1)}, u32[]{:S(2)}, u32[]{:S(2)}) collective-permute-start(bf16[24,16,128]{2,1,0:T(8,128)(2,1)S(1)} %get-tuple-element.29), channel_id=1, source_target_pairs={{0,16},{4,20},{8,24},{12,28},{16,0},{20,4},{24,8},{28,12},{1,17},{... | collective-permute-start | bytes 294920 | tf_op jit(solution)/shard_map/ppermute | solution.py:313
  14.2 28.0 %collective-permute-start.4 = (bf16[24,16,128]{2,1,0:T(8,128)(2,1)S(1)}, bf16[24,16,128]{2,1,0:T(8,128)(2,1)S(1)}, u32[]{:S(2)}, u32[]{:S(2)}) collective-permute-start(bf16[24,16,128]{2,1,0:T(8,128)(2,1)S(1)} %get-tuple-element.30), channel_id=1, source_target_pairs={{0,20},{4,16},{8,28},{12,24},{16,4},{20,0},{24,12},{28,8},{1,21},{... | collective-permute-start | bytes 294920 | tf_op jit(solution)/shard_map/ppermute | solution.py:313
  14.3 27.9 %collective-permute-start.5 = (bf16[24,16,128]{2,1,0:T(8,128)(2,1)S(1)}, bf16[24,16,128]{2,1,0:T(8,128)(2,1)S(1)}, u32[]{:S(2)}, u32[]{:S(2)}) collective-permute-start(bf16[24,16,128]{2,1,0:T(8,128)(2,1)S(1)} %get-tuple-element.31), channel_id=1, source_target_pairs={{0,24},{4,28},{8,16},{12,20},{16,8},{20,12},{24,0},{28,4},{1,25},{... | collective-permute-start | bytes 294920 | tf_op jit(solution)/shard_map/ppermute | solution.py:313
  25.2 17.0 %collective-permute-start.6 = (bf16[24,16,128]{2,1,0:T(8,128)(2,1)S(1)}, bf16[24,16,128]{2,1,0:T(8,128)(2,1)S(1)}, u32[]{:S(2)}, u32[]{:S(2)}) collective-permute-start(bf16[24,16,128]{2,1,0:T(8,128)(2,1)S(1)} %get-tuple-element.32), channel_id=1, source_target_pairs={{0,28},{4,24},{8,20},{12,16},{16,12},{20,8},{24,4},{28,0},{1,29},{... | collective-permute-start | bytes 294920 | tf_op jit(solution)/shard_map/ppermute | solution.py:313
  44.1 14.2 %collective-permute-start.12 = (s16[25,16,128]{2,1,0:T(8,128)(2,1)S(1)}, s16[25,16,128]{2,1,0:T(8,128)(2,1)S(1)}, u32[]{:S(2)}, u32[]{:S(2)}) collective-permute-start(s16[25,16,128]{2,1,0:T(8,128)(2,1)S(1)} %get-tuple-element.39), channel_id=1, source_target_pairs={{0,16},{4,20},{8,24},{12,28},{16,0},{20,4},{24,8},{28,12},{1,17},{... | collective-permute-start | bytes 307208 | tf_op jit(solution)/shard_map/ppermute | solution.py:313
  49.2 10.1 %collective-permute-start.13 = (s16[25,16,128]{2,1,0:T(8,128)(2,1)S(1)}, s16[25,16,128]{2,1,0:T(8,128)(2,1)S(1)}, u32[]{:S(2)}, u32[]{:S(2)}) collective-permute-start(s16[25,16,128]{2,1,0:T(8,128)(2,1)S(1)} %get-tuple-element.40), channel_id=1, source_target_pairs={{0,20},{4,16},{8,28},{12,24},{16,4},{20,0},{24,12},{28,8},{1,21},{... | collective-permute-start | bytes 307208 | tf_op jit(solution)/shard_map/ppermute | solution.py:313
  51.8 8.2 %collective-permute-start.10 = (s16[25,16,128]{2,1,0:T(8,128)(2,1)S(1)}, s16[25,16,128]{2,1,0:T(8,128)(2,1)S(1)}, u32[]{:S(2)}, u32[]{:S(2)}) collective-permute-start(s16[25,16,128]{2,1,0:T(8,128)(2,1)S(1)} %get-tuple-element.37), channel_id=1, source_target_pairs={{0,8},{4,12},{8,0},{12,4},{16,24},{20,28},{24,16},{28,20},{1,9},{5... | collective-permute-start | bytes 307208 | tf_op jit(solution)/shard_map/ppermute | solution.py:313
  54.1 7.7 %collective-permute-start.11 = (s16[25,16,128]{2,1,0:T(8,128)(2,1)S(1)}, s16[25,16,128]{2,1,0:T(8,128)(2,1)S(1)}, u32[]{:S(2)}, u32[]{:S(2)}) collective-permute-start(s16[25,16,128]{2,1,0:T(8,128)(2,1)S(1)} %get-tuple-element.38), channel_id=1, source_target_pairs={{0,12},{4,8},{8,4},{12,0},{16,28},{20,24},{24,20},{28,16},{1,13},{... | collective-permute-start | bytes 307208 | tf_op jit(solution)/shard_map/ppermute | solution.py:313
  54.3 11.9 %collective-permute-start.7 = (s16[25,16,128]{2,1,0:T(8,128)(2,1)S(1)}, s16[25,16,128]{2,1,0:T(8,128)(2,1)S(1)}, u32[]{:S(2)}, u32[]{:S(2)}) collective-permute-start(s16[25,16,128]{2,1,0:T(8,128)(2,1)S(1)} %get-tuple-element.34), channel_id=1, source_target_pairs={{0,24},{4,28},{8,16},{12,20},{16,8},{20,12},{24,0},{28,4},{1,25},{... | collective-permute-start | bytes 307208 | tf_op jit(solution)/shard_map/ppermute | solution.py:313
  58.4 9.5 %collective-permute-start.8 = (s16[25,16,128]{2,1,0:T(8,128)(2,1)S(1)}, s16[25,16,128]{2,1,0:T(8,128)(2,1)S(1)}, u32[]{:S(2)}, u32[]{:S(2)}) collective-permute-start(s16[25,16,128]{2,1,0:T(8,128)(2,1)S(1)} %get-tuple-element.35), channel_id=1, source_target_pairs={{0,28},{4,24},{8,20},{12,16},{16,12},{20,8},{24,4},{28,0},{1,29},{... | collective-permute-start | bytes 307208 | tf_op jit(solution)/shard_map/ppermute | solution.py:313
  59.3 8.5 %collective-permute-start.9 = (s16[25,16,128]{2,1,0:T(8,128)(2,1)S(1)}, s16[25,16,128]{2,1,0:T(8,128)(2,1)S(1)}, u32[]{:S(2)}, u32[]{:S(2)}) collective-permute-start(s16[25,16,128]{2,1,0:T(8,128)(2,1)S(1)} %get-tuple-element.36), channel_id=1, source_target_pairs={{0,4},{4,0},{8,12},{12,8},{16,20},{20,16},{24,28},{28,24},{1,5},{5... | collective-permute-start | bytes 307208 | tf_op jit(solution)/shard_map/ppermute | solution.py:313

commit v6 on v5

--- a/solution.py
+++ b/solution.py
@@ -13,6 +13,7 @@
 STEPS = 32700.0
 FINE = 64.0
 TINY = 1e-34
+PICKS = 8
 SMEM = pl.BlockSpec(memory_space=pltpu.SMEM)
 VMEM = pl.BlockSpec(memory_space=pltpu.VMEM)
 ANY = pl.BlockSpec(memory_space=pl.ANY)
@@ -48,7 +49,8 @@
 
 
 def pick_kernel(s, map_hbm, screened_hbm, out_hbm, map_ref, screened_ref, out_ref, in_sems, out_sems, map_sem):
-    chunks = [pl.ds(comp * s.energies, s.energies) for comp in range(s.comps)]
+    size = s.planes // PICKS
+    chunks = [pl.ds(i * size, size) for i in range(PICKS)]
     arriving = [
         pltpu.make_async_copy(screened_hbm.at[chunk], screened_ref.at[chunk], in_sems.at[i])
         for i, chunk in enumerate(chunks)
@@ -63,14 +65,14 @@
         copy.start()
     mapped.wait()
     picked = [map_ref[i] for i in range(s.cells * s.per_cell)]
-    for comp in range(s.comps):
-        arriving[comp].wait()
-        for plane in range(comp * s.energies, (comp + 1) * s.energies):
+    for chunk in range(PICKS):
+        arriving[chunk].wait()
+        for plane in range(chunk * size, (chunk + 1) * size):
             for i, cell in enumerate(picked):
                 for t in range(s.tiles):
                     target = (i % s.per_cell * s.slices + t) * s.cells + i // s.per_cell
                     out_ref[target, plane] = screened_ref[plane, cell, :, t * LANES : (t + 1) * LANES]
-        leaving[comp].start()
+        leaving[chunk].start()
     for copy in leaving:
         copy.wait()
 
@@ -87,8 +89,8 @@
             pltpu.SMEM(cell_map.shape, jnp.int32),
             pltpu.VMEM(flat.shape, flat.dtype),
             pltpu.VMEM(out.shape, out.dtype),
-            pltpu.SemaphoreType.DMA((s.comps,)),
-            pltpu.SemaphoreType.DMA((s.comps,)),
+            pltpu.SemaphoreType.DMA((PICKS,)),
+            pltpu.SemaphoreType.DMA((PICKS,)),
             pltpu.SemaphoreType.DMA(()),
         ],
         compiler_params=pltpu.CompilerParams(vmem_limit_bytes=60 * 1024 * 1024),
@@ -276,34 +278,46 @@
 
 def unpack_kernel(s, order, me_ref, *refs):
     at = dict(zip(order, refs))
-    blocks, whole_ref, scales = [at[k] for k in range(s.groups)], refs[s.groups], refs[s.groups + 1]
+    blocks = [at[k] for k in range(s.groups)]
+    whole_hbm, whole_ref, scales, sems = refs[s.groups :]
     me = me_ref[0]
     places = []
     for k, block in enumerate(blocks):
         cell, part, lanes = s.where(me ^ k)
-        places.append((cell, slice(None) if s.parts == 1 else pl.ds(pl.multiple_of(part * s.plane[0], s.plane[0]), s.plane[0]), lanes))
+        rows = slice(None) if s.parts == 1 else pl.ds(pl.multiple_of(part * s.plane[0], s.plane[0]), s.plane[0])
+        places.append((cell, rows, lanes))
         if k != 0:
             for j in range(s.scale_planes):
                 code = block[s.planes + j].astype(jnp.int32).astype(jnp.float32)
                 scales[k, j * s.plane[0] : (j + 1) * s.plane[0]] = jnp.exp2(code * (1.0 / FINE)) * (1.0 / STEPS)
-
-    @pl.loop(0, s.scales)
-    def _(pair):
-        for k, (cell, rows, lanes) in enumerate(places):
-            for i in range(PAIR):
-                value = blocks[k][pair * PAIR + i]
+    leaving = []
+    for comp in range(s.comps):
+        chunk = pl.ds(comp * s.energies, s.energies)
+        for plane in range(comp * s.energies, (comp + 1) * s.energies):
+            pair = plane // PAIR
+            for k, (cell, rows, lanes) in enumerate(places):
+                value = blocks[k][plane]
                 if k != 0:
-                    value = value.astype(jnp.int32).astype(jnp.float32) * scales[k, pl.ds(pair, 1)]
-                whole_ref[pair * PAIR + i, cell, rows, lanes] = value
+                    value = value.astype(jnp.int32).astype(jnp.float32) * scales[k, pair : pair + 1]
+                whole_ref[plane, cell, rows, lanes] = value
+        leaving.append(pltpu.make_async_copy(whole_ref.at[chunk], whole_hbm.at[chunk], sems.at[comp]))
+        leaving[-1].start()
+    for copy in leaving:
+        copy.wait()
 
 
 def unpack(s, me, blocks, order):
+    shape = (s.planes, s.per_cell, s.rows, s.width)
     return pl.pallas_call(
         functools.partial(unpack_kernel, s, order),
-        out_shape=jax.ShapeDtypeStruct((s.planes, s.per_cell, s.rows, s.width), jnp.float32),
+        out_shape=jax.ShapeDtypeStruct(shape, jnp.float32),
         in_specs=[SMEM] + [VMEM] * s.groups,
-        out_specs=VMEM,
-        scratch_shapes=[pltpu.VMEM((s.groups, s.scale_planes * s.plane[0], LANES), jnp.float32)],
+        out_specs=ANY,
+        scratch_shapes=[
+            pltpu.VMEM(shape, jnp.float32),
+            pltpu.VMEM((s.groups, s.scale_planes * s.plane[0], LANES), jnp.float32),
+            pltpu.SemaphoreType.DMA((s.comps,)),
+        ],
         compiler_params=PARAMS,
         name="unpack",
     )(me, *[blocks[k] for k in order])
@@ -335,7 +349,7 @@
     g_near, w_all = stage_near(s, me, screens, greens[:half])
     begun = partial_of(s, me, table, shift_count, g_near, w_all)
     g_far = stage_far(s, me, greens[half:], begun)
-    first, later = far[:2], [0] + far[2:] + near[1:]
+    first, later = far[2:], [0] + near[3:] + far[1:2] + near[1:2] + far[:1] + near[2:3]
     sums = {}
     for ks in (first, later):
         for k, block in zip(ks, sigma_of(s, me, table, shift_count, begun, w_all, g_far, ks)):

time: 69.6 us -> 68.9 us (0.990)
  starting transfers between devices: 30.9 us -> 29.2 us
  waiting for transfers between devices: 24.6 us -> 25.9 us
    ppermute x14, starting transfers between devices: 23.6 us -> 21.9 us  [swap(): lax.ppermute(block, 'energy', [(i, i ^ k) for i in range(s.groups)])]
    ppermute x14, waiting for transfers between devices: 21.6 us -> 22.9 us  [swap(): lax.ppermute(block, 'energy', [(i, i ^ k) for i in range(s.groups)])]
  transfers between devices with their start and end apart: 15 -> 15, of which waited for: 8 -> 8; matrix products, arithmetic and copies ran while one was open for 0% -> 0% of each run, Pallas kernels for 12% -> 11%
where the time goes in v6:
time: 68.9 us; the launch traced here: 68.6 us
  starting transfers between devices  29.2 us (42%)
  waiting for transfers between devices  25.9 us (38%)
  Pallas kernels  13.3 us (19%)
    ppermute x14, waiting for transfers between devices, swap(): lax.ppermute(block, 'energy', [(i, i ^ k) for i in range(s.groups)])  22.9 us
    ppermute x14, starting transfers between devices, swap(): lax.ppermute(block, 'energy', [(i, i ^ k) for i in range(s.groups)])  21.9 us
    all_to_all x1, starting transfers between devices, send_screened(): lax.all_to_all(pick_screened(s, cell_map, screened), ('energy', 'cell'),...  7.3 us
    pallas_call x1, Pallas kernels, partial_of(): pl.pallas_call(functools.partial(partial_kernel, s, table.shape[1]), out_...  5.05 us
    pallas_call x2, Pallas kernels, sigma_of(): pl.pallas_call(functools.partial(sigma_kernel, s, table.shape[1], ks), ou...  4.27 us
    all_to_all x1, waiting for transfers between devices, send_screened(): lax.all_to_all(pick_screened(s, cell_map, screened), ('energy', 'cell'),...  3.01 us
    pallas_call x1, Pallas kernels, pick_screened(): pl.pallas_call(functools.partial(pick_kernel, s), out_shape=out, in_specs...  2.11 us
  transfers between devices with their start and end apart: 15, of which 8 were waited for; matrix products, arithmetic and copies ran while one was open for 0% of the time, Pallas kernels for 11%

profile of v6, /device:TPU:0, one launch (start us, length us, event | category | flops | bytes accessed | tf_op | source)
XLA Modules:
  0.0 68.6 jit_solution(2401401077648848563)
XLA Ops:
  0.0 2.1 %pick_screened.1 = bf16[32,24,4,128]{3,2,1,0:T(4,128)(2,1)} custom-call(s32[8]{0:T(128)} %map_hbm.1, bf16[24,8,4,512]{3,2,1,0:T(4,128)(2,1)} %bitcast.9), custom_call_target="tpu_custom_call" | custom-call | tf_op jit(solution)/shard_map/pick_screened/pallas_call | solution.py:83
  2.1 7.3 %all-to-all-start = ((bf16[32,24,4,128]{3,2,1,0:T(4,128)(2,1)}), bf16[32,24,4,128]{3,2,1,0:T(4,128)(2,1)S(1)}, u32[]{:S(2)}, u32[]{:S(2)}) async-start(bf16[32,24,4,128]{3,2,1,0:T(4,128)(2,1)} %pick_screened.1), calls=%async_computation | async-start | bytes 1572864 | tf_op jit(solution)/shard_map/all_to_all | solution.py:332
  10.0 1.7 %collective-permute-start.1 = (bf16[24,16,128]{2,1,0:T(8,128)(2,1)S(1)}, bf16[24,16,128]{2,1,0:T(8,128)(2,1)S(1)}, u32[]{:S(2)}, u32[]{:S(2)}) collective-permute-start(bf16[24,16,128]{2,1,0:T(8,128)(2,1)S(1)} %get-tuple-element.25), channel_id=1, source_target_pairs={{0,8},{4,12},{8,0},{12,4},{16,24},{20,28},{24,16},{28,20},{1,9},{5... | collective-permute-start | bytes 294920 | tf_op jit(solution)/shard_map/ppermute | solution.py:327
  11.6 2.6 %collective-permute-start.3 = (bf16[24,16,128]{2,1,0:T(8,128)(2,1)S(1)}, bf16[24,16,128]{2,1,0:T(8,128)(2,1)S(1)}, u32[]{:S(2)}, u32[]{:S(2)}) collective-permute-start(bf16[24,16,128]{2,1,0:T(8,128)(2,1)S(1)} %get-tuple-element.29), channel_id=1, source_target_pairs={{0,16},{4,20},{8,24},{12,28},{16,0},{20,4},{24,8},{28,12},{1,17},{... | collective-permute-start | bytes 294920 | tf_op jit(solution)/shard_map/ppermute | solution.py:327
  14.3 3.5 %collective-permute-start.5 = (bf16[24,16,128]{2,1,0:T(8,128)(2,1)S(1)}, bf16[24,16,128]{2,1,0:T(8,128)(2,1)S(1)}, u32[]{:S(2)}, u32[]{:S(2)}) collective-permute-start(bf16[24,16,128]{2,1,0:T(8,128)(2,1)S(1)} %get-tuple-element.31), channel_id=1, source_target_pairs={{0,24},{4,28},{8,16},{12,20},{16,8},{20,12},{24,0},{28,4},{1,25},{... | collective-permute-start | bytes 294920 | tf_op jit(solution)/shard_map/ppermute | solution.py:327
  17.9 7.4 %collective-permute-done.1.refs_2_ = bf16[24,16,128]{2,1,0:T(8,128)(2,1)S(1)} collective-permute-done((bf16[24,16,128]{2,1,0:T(8,128)(2,1)S(1)}, bf16[24,16,128]{2,1,0:T(8,128)(2,1)S(1)}, u32[]{:S(2)}, u32[]{:S(2)}) %collective-permute-start.1) | collective-permute-done | bytes 98336 | tf_op jit(solution)/shard_map/ppermute | solution.py:327
  25.3 2.5 %collective-permute-start.6 = (bf16[24,16,128]{2,1,0:T(8,128)(2,1)S(1)}, bf16[24,16,128]{2,1,0:T(8,128)(2,1)S(1)}, u32[]{:S(2)}, u32[]{:S(2)}) collective-permute-start(bf16[24,16,128]{2,1,0:T(8,128)(2,1)S(1)} %get-tuple-element.32), channel_id=1, source_target_pairs={{0,28},{4,24},{8,20},{12,16},{16,12},{20,8},{24,4},{28,0},{1,29},{... | collective-permute-start | bytes 294920 | tf_op jit(solution)/shard_map/ppermute | solution.py:327
  27.8 3.0 %all-to-all-done.screens_ref = bf16[32,24,4,128]{3,2,1,0:T(4,128)(2,1)S(1)} async-done(((bf16[32,24,4,128]{3,2,1,0:T(4,128)(2,1)}), bf16[32,24,4,128]{3,2,1,0:T(4,128)(2,1)S(1)}, u32[]{:S(2)}, u32[]{:S(2)}) %all-to-all-start) | async-done | bytes 786464 | tf_op jit(solution)/shard_map/all_to_all | solution.py:332
  30.8 0.4 stage_near.1
  31.2 5.1 %partial.1.after_ref.begun = f32[8,24,16,128]{3,2,1,0:T(8,128)S(1)} custom-call(s32[1]{0:T(128)} %bitcast.me_ref, s32[64,3]{1,0:T(8,128)S(1)} %bitcast.6, s32[8,8]{1,0:T(8,128)S(1)} %copy-done.1, f32[144,16,128]{2,1,0:T(8,128)S(1)} %get-tuple-element.27.g_half, f32[8,24,16,128]{3,2,1,0:T(8,128)S(1)} %get-tuple-element.28.w_all), custom_call_target="tpu_custom_call" | custom-call | tf_op jit(solution)/shard_map/partial/pallas_call | solution.py:220
  36.3 4.8 %collective-permute-done.3.refs_0_ = bf16[24,16,128]{2,1,0:T(8,128)(2,1)S(1)} collective-permute-done((bf16[24,16,128]{2,1,0:T(8,128)(2,1)S(1)}, bf16[24,16,128]{2,1,0:T(8,128)(2,1)S(1)}, u32[]{:S(2)}, u32[]{:S(2)}) %collective-permute-start.3) | collective-permute-done | bytes 98336 | tf_op jit(solution)/shard_map/ppermute | solution.py:327
  41.1 1.2 %collective-permute-done.4.refs_1_ = bf16[24,16,128]{2,1,0:T(8,128)(2,1)S(1)} collective-permute-done((bf16[24,16,128]{2,1,0:T(8,128)(2,1)S(1)}, bf16[24,16,128]{2,1,0:T(8,128)(2,1)S(1)}, u32[]{:S(2)}, u32[]{:S(2)}) %collective-permute-start.4) | collective-permute-done | bytes 98336 | tf_op jit(solution)/shard_map/ppermute | solution.py:327
  42.4 2.2 %sigma.3 = (s16[25,16,128]{2,1,0:T(8,128)(2,1)S(1)}, s16[25,16,128]{2,1,0:T(8,128)(2,1)S(1)}) custom-call(s32[1]{0:T(128)} %bitcast.me_ref, s32[64,3]{1,0:T(8,128)S(1)} %bitcast.7, s32[8,8]{1,0:T(8,128)S(1)} %copy-done.1, f32[8,24,16,128]{3,2,1,0:T(8,128)S(1)} %partial.1.after_ref.begun, f32[8,24,16,128]{3,2,1,0:T(8,128)S(1)} %get-tuple-element.28.w_all, ...), custom_call_target="tpu_custom_call" | custom-call | tf_op jit(solution)/shard_map/sigma/pallas_call | solution.py:269
  44.6 1.3 %collective-permute-start.12 = (s16[25,16,128]{2,1,0:T(8,128)(2,1)S(1)}, s16[25,16,128]{2,1,0:T(8,128)(2,1)S(1)}, u32[]{:S(2)}, u32[]{:S(2)}) collective-permute-start(s16[25,16,128]{2,1,0:T(8,128)(2,1)S(1)} %get-tuple-element.39), channel_id=1, source_target_pairs={{0,24},{4,28},{8,16},{12,20},{16,8},{20,12},{24,0},{28,4},{1,25},{... | collective-permute-start | bytes 307208 | tf_op jit(solution)/shard_map/ppermute | solution.py:327
  45.9 2.7 %collective-permute-start.13 = (s16[25,16,128]{2,1,0:T(8,128)(2,1)S(1)}, s16[25,16,128]{2,1,0:T(8,128)(2,1)S(1)}, u32[]{:S(2)}, u32[]{:S(2)}) collective-permute-start(s16[25,16,128]{2,1,0:T(8,128)(2,1)S(1)} %get-tuple-element.40), channel_id=1, source_target_pairs={{0,28},{4,24},{8,20},{12,16},{16,12},{20,8},{24,4},{28,0},{1,29},{... | collective-permute-start | bytes 307208 | tf_op jit(solution)/shard_map/ppermute | solution.py:327
  48.6 2.1 %sigma.2 = (f32[24,16,128]{2,1,0:T(8,128)S(1)}, s16[25,16,128]{2,1,0:T(8,128)(2,1)S(1)}, s16[25,16,128]{2,1,0:T(8,128)(2,1)S(1)}, s16[25,16,128]{2,1,0:T(8,128)(...) custom-call(s32[1]{0:T(128)} %bitcast.me_ref, s32[64,3]{1,0:T(8,128)S(1)} %bitcast.8, ...), custom_call_target="tpu_custom_call" | custom-call | tf_op jit(solution)/shard_map/sigma/pallas_call | solution.py:269
  50.7 5.0 %collective-permute-start.10 = (s16[25,16,128]{2,1,0:T(8,128)(2,1)S(1)}, s16[25,16,128]{2,1,0:T(8,128)(2,1)S(1)}, u32[]{:S(2)}, u32[]{:S(2)}) collective-permute-start(s16[25,16,128]{2,1,0:T(8,128)(2,1)S(1)} %get-tuple-element.37), channel_id=1, source_target_pairs={{0,16},{4,20},{8,24},{12,28},{16,0},{20,4},{24,8},{28,12},{1,17},{... | collective-permute-start | bytes 307208 | tf_op jit(solution)/shard_map/ppermute | solution.py:327
  55.6 1.8 %collective-permute-start.7 = (s16[25,16,128]{2,1,0:T(8,128)(2,1)S(1)}, s16[25,16,128]{2,1,0:T(8,128)(2,1)S(1)}, u32[]{:S(2)}, u32[]{:S(2)}) collective-permute-start(s16[25,16,128]{2,1,0:T(8,128)(2,1)S(1)} %get-tuple-element.34), channel_id=1, source_target_pairs={{0,12},{4,8},{8,4},{12,0},{16,28},{20,24},{24,20},{28,16},{1,13},{... | collective-permute-start | bytes 307208 | tf_op jit(solution)/shard_map/ppermute | solution.py:327
  57.5 0.4 collective-permute-start.9
  57.9 5.4 %collective-permute-done.10.refs_4_ = s16[25,16,128]{2,1,0:T(8,128)(2,1)S(1)} collective-permute-done((s16[25,16,128]{2,1,0:T(8,128)(2,1)S(1)}, s16[25,16,128]{2,1,0:T(8,128)(2,1)S(1)}, u32[]{:S(2)}, u32[]{:S(2)}) %collective-permute-start.10) | collective-permute-done | bytes 102432 | tf_op jit(solution)/shard_map/ppermute | solution.py:327
  63.3 0.6 collective-permute-done.11.refs_5_
  63.9 1.2 %collective-permute-done.7.refs_1_ = s16[25,16,128]{2,1,0:T(8,128)(2,1)S(1)} collective-permute-done((s16[25,16,128]{2,1,0:T(8,128)(2,1)S(1)}, s16[25,16,128]{2,1,0:T(8,128)(2,1)S(1)}, u32[]{:S(2)}, u32[]{:S(2)}) %collective-permute-start.7) | collective-permute-done | bytes 102432 | tf_op jit(solution)/shard_map/ppermute | solution.py:327
  65.1 2.2 %collective-permute-done.8.refs_2_ = s16[25,16,128]{2,1,0:T(8,128)(2,1)S(1)} collective-permute-done((s16[25,16,128]{2,1,0:T(8,128)(2,1)S(1)}, s16[25,16,128]{2,1,0:T(8,128)(2,1)S(1)}, u32[]{:S(2)}, u32[]{:S(2)}) %collective-permute-start.8) | collective-permute-done | bytes 102432 | tf_op jit(solution)/shard_map/ppermute | solution.py:327
  67.4 1.3 %unpack.1 = f32[24,2,16,512]{3,2,1,0:T(8,128)} custom-call(s32[1]{0:T(128)} %bitcast.me_ref, f32[24,16,128]{2,1,0:T(8,128)S(1)} %get-tuple-element.33.refs_0_, s16[25,16,128]{2,1,0:T(8,128)(2,1)S(1)} %collective-permute-done.7.refs_1_, s16[25,16,128]{2,1,0:T(8,128)(2,1)S(1)} %collective-permute-done.8.refs_2_, ...), custom_call_target="tpu_custom_call" | custom-call | tf_op jit(solution)/shard_map/unpack/pallas_call | solution.py:311
  (21 shorter events, 0.9 us)
Async XLA Ops:
  0.0 9.5 %copy-start = (bf16[4,6,2,16,512]{4,3,2,1,0:T(8,128)(2,1)S(1)}, bf16[4,6,2,16,512]{4,3,2,1,0:T(8,128)(2,1)}, u32[]{:S(2)}) copy-start(bf16[4,6,2,16,512]{4,3,2,1,0:T(8,128)(2,1)} %param.5) | copy-start | bytes 2359300
  2.1 25.6 %copy-start.2 = (s32[8,8,3]{1,0,2:T(8,128)S(1)}, s32[8,8,3]{1,0,2:T(8,128)}, u32[]{:S(2)}) copy-start(s32[8,8,3]{1,0,2:T(8,128)} %param.8) | copy-start | bytes 2308
  2.1 29.1 %copy-start.1 = (s32[8,8]{1,0:T(8,128)S(1)}, s32[8,8]{1,0:T(8,128)}, u32[]{:S(2)}) copy-start(s32[8,8]{1,0:T(8,128)} %count_ref.5) | copy-start | bytes 772
  2.1 28.7 %all-to-all-start = ((bf16[32,24,4,128]{3,2,1,0:T(4,128)(2,1)}), bf16[32,24,4,128]{3,2,1,0:T(4,128)(2,1)S(1)}, u32[]{:S(2)}, u32[]{:S(2)}) async-start(bf16[32,24,4,128]{3,2,1,0:T(4,128)(2,1)} %pick_screened.1), calls=%async_computation | async-start | bytes 1572864 | tf_op jit(solution)/shard_map/all_to_all | solution.py:332
  9.6 4.7 %collective-permute-start = (bf16[24,16,128]{2,1,0:T(8,128)(2,1)S(1)}, bf16[24,16,128]{2,1,0:T(8,128)(2,1)S(1)}, u32[]{:S(2)}, u32[]{:S(2)}) collective-permute-start(bf16[24,16,128]{2,1,0:T(8,128)(2,1)S(1)} %get-tuple-element.24), channel_id=1, source_target_pairs={{0,4},{4,0},{8,12},{12,8},{16,20},{20,16},{24,28},{28,24},{1,5},{5... | collective-permute-start | bytes 294920 | tf_op jit(solution)/shard_map/ppermute | solution.py:327
  10.0 15.3 %collective-permute-start.1 = (bf16[24,16,128]{2,1,0:T(8,128)(2,1)S(1)}, bf16[24,16,128]{2,1,0:T(8,128)(2,1)S(1)}, u32[]{:S(2)}, u32[]{:S(2)}) collective-permute-start(bf16[24,16,128]{2,1,0:T(8,128)(2,1)S(1)} %get-tuple-element.25), channel_id=1, source_target_pairs={{0,8},{4,12},{8,0},{12,4},{16,24},{20,28},{24,16},{28,20},{1,9},{5... | collective-permute-start | bytes 294920 | tf_op jit(solution)/shard_map/ppermute | solution.py:327
  11.6 16.2 %collective-permute-start.2 = (bf16[24,16,128]{2,1,0:T(8,128)(2,1)S(1)}, bf16[24,16,128]{2,1,0:T(8,128)(2,1)S(1)}, u32[]{:S(2)}, u32[]{:S(2)}) collective-permute-start(bf16[24,16,128]{2,1,0:T(8,128)(2,1)S(1)} %get-tuple-element.26), channel_id=1, source_target_pairs={{0,12},{4,8},{8,4},{12,0},{16,28},{20,24},{24,20},{28,16},{1,13},{... | collective-permute-start | bytes 294920 | tf_op jit(solution)/shard_map/ppermute | solution.py:327
  11.6 29.5 %collective-permute-start.3 = (bf16[24,16,128]{2,1,0:T(8,128)(2,1)S(1)}, bf16[24,16,128]{2,1,0:T(8,128)(2,1)S(1)}, u32[]{:S(2)}, u32[]{:S(2)}) collective-permute-start(bf16[24,16,128]{2,1,0:T(8,128)(2,1)S(1)} %get-tuple-element.29), channel_id=1, source_target_pairs={{0,16},{4,20},{8,24},{12,28},{16,0},{20,4},{24,8},{28,12},{1,17},{... | collective-permute-start | bytes 294920 | tf_op jit(solution)/shard_map/ppermute | solution.py:327
  14.2 28.0 %collective-permute-start.4 = (bf16[24,16,128]{2,1,0:T(8,128)(2,1)S(1)}, bf16[24,16,128]{2,1,0:T(8,128)(2,1)S(1)}, u32[]{:S(2)}, u32[]{:S(2)}) collective-permute-start(bf16[24,16,128]{2,1,0:T(8,128)(2,1)S(1)} %get-tuple-element.30), channel_id=1, source_target_pairs={{0,20},{4,16},{8,28},{12,24},{16,4},{20,0},{24,12},{28,8},{1,21},{... | collective-permute-start | bytes 294920 | tf_op jit(solution)/shard_map/ppermute | solution.py:327
  14.3 27.9 %collective-permute-start.5 = (bf16[24,16,128]{2,1,0:T(8,128)(2,1)S(1)}, bf16[24,16,128]{2,1,0:T(8,128)(2,1)S(1)}, u32[]{:S(2)}, u32[]{:S(2)}) collective-permute-start(bf16[24,16,128]{2,1,0:T(8,128)(2,1)S(1)} %get-tuple-element.31), channel_id=1, source_target_pairs={{0,24},{4,28},{8,16},{12,20},{16,8},{20,12},{24,0},{28,4},{1,25},{... | collective-permute-start | bytes 294920 | tf_op jit(solution)/shard_map/ppermute | solution.py:327
  25.3 17.0 %collective-permute-start.6 = (bf16[24,16,128]{2,1,0:T(8,128)(2,1)S(1)}, bf16[24,16,128]{2,1,0:T(8,128)(2,1)S(1)}, u32[]{:S(2)}, u32[]{:S(2)}) collective-permute-start(bf16[24,16,128]{2,1,0:T(8,128)(2,1)S(1)} %get-tuple-element.32), channel_id=1, source_target_pairs={{0,28},{4,24},{8,20},{12,16},{16,12},{20,8},{24,4},{28,0},{1,29},{... | collective-permute-start | bytes 294920 | tf_op jit(solution)/shard_map/ppermute | solution.py:327
  44.6 12.8 %collective-permute-start.12 = (s16[25,16,128]{2,1,0:T(8,128)(2,1)S(1)}, s16[25,16,128]{2,1,0:T(8,128)(2,1)S(1)}, u32[]{:S(2)}, u32[]{:S(2)}) collective-permute-start(s16[25,16,128]{2,1,0:T(8,128)(2,1)S(1)} %get-tuple-element.39), channel_id=1, source_target_pairs={{0,24},{4,28},{8,16},{12,20},{16,8},{20,12},{24,0},{28,4},{1,25},{... | collective-permute-start | bytes 307208 | tf_op jit(solution)/shard_map/ppermute | solution.py:327
  45.9 11.5 %collective-permute-start.13 = (s16[25,16,128]{2,1,0:T(8,128)(2,1)S(1)}, s16[25,16,128]{2,1,0:T(8,128)(2,1)S(1)}, u32[]{:S(2)}, u32[]{:S(2)}) collective-permute-start(s16[25,16,128]{2,1,0:T(8,128)(2,1)S(1)} %get-tuple-element.40), channel_id=1, source_target_pairs={{0,28},{4,24},{8,20},{12,16},{16,12},{20,8},{24,4},{28,0},{1,29},{... | collective-permute-start | bytes 307208 | tf_op jit(solution)/shard_map/ppermute | solution.py:327
  50.7 12.6 %collective-permute-start.10 = (s16[25,16,128]{2,1,0:T(8,128)(2,1)S(1)}, s16[25,16,128]{2,1,0:T(8,128)(2,1)S(1)}, u32[]{:S(2)}, u32[]{:S(2)}) collective-permute-start(s16[25,16,128]{2,1,0:T(8,128)(2,1)S(1)} %get-tuple-element.37), channel_id=1, source_target_pairs={{0,16},{4,20},{8,24},{12,28},{16,0},{20,4},{24,8},{28,12},{1,17},{... | collective-permute-start | bytes 307208 | tf_op jit(solution)/shard_map/ppermute | solution.py:327
  55.6 8.2 %collective-permute-start.11 = (s16[25,16,128]{2,1,0:T(8,128)(2,1)S(1)}, s16[25,16,128]{2,1,0:T(8,128)(2,1)S(1)}, u32[]{:S(2)}, u32[]{:S(2)}) collective-permute-start(s16[25,16,128]{2,1,0:T(8,128)(2,1)S(1)} %get-tuple-element.38), channel_id=1, source_target_pairs={{0,8},{4,12},{8,0},{12,4},{16,24},{20,28},{24,16},{28,20},{1,9},{5... | collective-permute-start | bytes 307208 | tf_op jit(solution)/shard_map/ppermute | solution.py:327
  55.6 9.5 %collective-permute-start.7 = (s16[25,16,128]{2,1,0:T(8,128)(2,1)S(1)}, s16[25,16,128]{2,1,0:T(8,128)(2,1)S(1)}, u32[]{:S(2)}, u32[]{:S(2)}) collective-permute-start(s16[25,16,128]{2,1,0:T(8,128)(2,1)S(1)} %get-tuple-element.34), channel_id=1, source_target_pairs={{0,12},{4,8},{8,4},{12,0},{16,28},{20,24},{24,20},{28,16},{1,13},{... | collective-permute-start | bytes 307208 | tf_op jit(solution)/shard_map/ppermute | solution.py:327
  57.4 10.0 %collective-permute-start.8 = (s16[25,16,128]{2,1,0:T(8,128)(2,1)S(1)}, s16[25,16,128]{2,1,0:T(8,128)(2,1)S(1)}, u32[]{:S(2)}, u32[]{:S(2)}) collective-permute-start(s16[25,16,128]{2,1,0:T(8,128)(2,1)S(1)} %get-tuple-element.35), channel_id=1, source_target_pairs={{0,20},{4,16},{8,28},{12,24},{16,4},{20,0},{24,12},{28,8},{1,21},{... | collective-permute-start | bytes 307208 | tf_op jit(solution)/shard_map/ppermute | solution.py:327
  57.5 9.9 %collective-permute-start.9 = (s16[25,16,128]{2,1,0:T(8,128)(2,1)S(1)}, s16[25,16,128]{2,1,0:T(8,128)(2,1)S(1)}, u32[]{:S(2)}, u32[]{:S(2)}) collective-permute-start(s16[25,16,128]{2,1,0:T(8,128)(2,1)S(1)} %get-tuple-element.36), channel_id=1, source_target_pairs={{0,4},{4,0},{8,12},{12,8},{16,20},{20,16},{24,28},{28,24},{1,5},{5... | collective-permute-start | bytes 307208 | tf_op jit(solution)/shard_map/ppermute | solution.py:327

commit v7 on v6

--- a/solution.py
+++ b/solution.py
@@ -180,16 +180,16 @@
     )(me, after, *greens)
 
 
-def add_terms(s, slots, side, group, kind, table_ref, count_ref, g_half, w_all, sums):
+def add_terms(s, slots, side, group, kind, table_ref, g_half, w_all, sums):
     low = side * s.half
     real, imag = 2 * kind, 2 * kind + 1
 
     def turn(source, sums):
         sums = list(sums)
-        count = count_ref[group, source]
         for slot in range(slots):
-            shift = jnp.clip(table_ref[group * s.groups + source, slot], 0, s.energies - 1)
-            live = jnp.where(slot < count, 1.0, 0.0).astype(jnp.float32)
+            asked = table_ref[group * s.groups + source, slot]
+            shift = jnp.maximum(asked, 0)
+            live = jnp.where(asked >= 0, 1.0, 0.0).astype(jnp.float32)
             start = (group - source - low + 1) * s.energies - shift
             w_real = w_all[source, real * s.energies + shift] * live
             w_imag = w_all[source, imag * s.energies + shift] * live
@@ -204,30 +204,30 @@
     return lax.fori_loop(first, jnp.maximum(group - low + 1, first), turn, tuple(sums))
 
 
-def partial_kernel(s, slots, me_ref, table_ref, count_ref, g_half, w_all, out_ref):
+def partial_kernel(s, slots, me_ref, table_ref, g_half, w_all, out_ref):
     me = me_ref[0]
 
     @pl.loop(0, 2 * s.groups)
     def _(at):
         k, kind = at // 2, at % 2
         zeros = [jnp.zeros(s.plane, jnp.float32) for _ in range(2 * s.energies)]
-        sums = add_terms(s, slots, me // s.half, me ^ k, kind, table_ref, count_ref, g_half, w_all, zeros)
+        sums = add_terms(s, slots, me // s.half, me ^ k, kind, table_ref, g_half, w_all, zeros)
         for j, total in enumerate(sums):
             out_ref[k, kind * 2 * s.energies + j] = total
 
 
-def partial_of(s, me, table, count, g_half, w_all):
+def partial_of(s, me, table, g_half, w_all):
     return pl.pallas_call(
         functools.partial(partial_kernel, s, table.shape[1]),
         out_shape=jax.ShapeDtypeStruct((s.groups, s.planes) + s.plane, jnp.float32),
-        in_specs=[SMEM] * 3 + [VMEM] * 2,
+        in_specs=[SMEM] * 2 + [VMEM] * 2,
         out_specs=VMEM,
         compiler_params=PARAMS,
         name="partial",
-    )(me, table, count, g_half, w_all)
-
-
-def sigma_kernel(s, slots, ks, me_ref, table_ref, count_ref, begun, w_all, g_far, *outs):
+    )(me, table, g_half, w_all)
+
+
+def sigma_kernel(s, slots, ks, me_ref, table_ref, begun, w_all, g_far, *outs):
     me = me_ref[0]
     side = me // s.half
     row = lax.broadcasted_iota(jnp.int32, s.plane, 0)
@@ -237,7 +237,7 @@
             codes = list(codes)
             first = kind * 2 * s.energies
             sums = [begun[k, first + j] for j in range(2 * s.energies)]
-            sums = add_terms(s, slots, 1 - side, me ^ k, kind, table_ref, count_ref, g_far, w_all, sums)
+            sums = add_terms(s, slots, 1 - side, me ^ k, kind, table_ref, g_far, w_all, sums)
             sums = [total * SCALE for total in sums]
             if k == 0:
                 for j, total in enumerate(sums):
@@ -263,17 +263,17 @@
                 outs[at][s.planes + j] = codes[j].astype(jnp.int32).astype(jnp.int16)
 
 
-def sigma_of(s, me, table, count, begun, w_all, g_far, ks):
+def sigma_of(s, me, table, begun, w_all, g_far, ks):
     own = jax.ShapeDtypeStruct((s.planes,) + s.plane, jnp.float32)
     coded = jax.ShapeDtypeStruct((s.planes + s.scale_planes,) + s.plane, jnp.int16)
     return pl.pallas_call(
         functools.partial(sigma_kernel, s, table.shape[1], ks),
         out_shape=[own if k == 0 else coded for k in ks],
-        in_specs=[SMEM] * 3 + [VMEM] * 3,
+        in_specs=[SMEM] * 2 + [VMEM] * 3,
         out_specs=[VMEM] * len(ks),
         compiler_params=PARAMS,
         name="sigma",
-    )(me, table, count, begun, w_all, g_far)
+    )(me, table, begun, w_all, g_far)
 
 
 def unpack_kernel(s, order, me_ref, *refs):
@@ -345,14 +345,16 @@
 
     screens = send_screened(s, cell_map, screened)
     greens = [swap(s, block, k) for k, block in enumerate(cut_green(s, me, green))]
-    table = shift_table.reshape(s.groups * s.groups, shift_table.shape[2])
+    slots = jnp.arange(shift_table.shape[2], dtype=jnp.int32)
+    table = jnp.where(slots < shift_count[:, :, None], jnp.clip(shift_table, 0, s.energies - 1), -1)
+    table = table.reshape(s.groups * s.groups, shift_table.shape[2])
     g_near, w_all = stage_near(s, me, screens, greens[:half])
-    begun = partial_of(s, me, table, shift_count, g_near, w_all)
+    begun = partial_of(s, me, table, g_near, w_all)
     g_far = stage_far(s, me, greens[half:], begun)
-    first, later = far[2:], [0] + near[3:] + far[1:2] + near[1:2] + far[:1] + near[2:3]
+    first, later = far[2:], [0] + near[2:3] + near[3:] + near[1:2] + far[:1] + far[1:2]
     sums = {}
     for ks in (first, later):
-        for k, block in zip(ks, sigma_of(s, me, table, shift_count, begun, w_all, g_far, ks)):
+        for k, block in zip(ks, sigma_of(s, me, table, begun, w_all, g_far, ks)):
             sums[k] = swap(s, block, k)
     return unpack(s, me, sums, later + first).reshape(green.shape)
 

time: 68.9 us -> 68.8 us (level)
  transfers between devices with their start and end apart: 15 -> 15, of which waited for: 8 -> 6; matrix products, arithmetic and copies ran while one was open for 0% -> 0% of each run, Pallas kernels for 11% -> 11%
where the time goes in v7:
time: 68.8 us; the launch traced here: 68.5 us
  starting transfers between devices  29.4 us (43%)
  waiting for transfers between devices  25.8 us (38%)
  Pallas kernels  13 us (19%)
    ppermute x14, waiting for transfers between devices, swap(): lax.ppermute(block, 'energy', [(i, i ^ k) for i in range(s.groups)])  22.8 us
    ppermute x14, starting transfers between devices, swap(): lax.ppermute(block, 'energy', [(i, i ^ k) for i in range(s.groups)])  22.1 us
    all_to_all x1, starting transfers between devices, send_screened(): lax.all_to_all(pick_screened(s, cell_map, screened), ('energy', 'cell'),...  7.3 us
    pallas_call x1, Pallas kernels, partial_of(): pl.pallas_call(functools.partial(partial_kernel, s, table.shape[1]), out_...  4.9 us
    pallas_call x2, Pallas kernels, sigma_of(): pl.pallas_call(functools.partial(sigma_kernel, s, table.shape[1], ks), ou...  4.15 us
    all_to_all x1, waiting for transfers between devices, send_screened(): lax.all_to_all(pick_screened(s, cell_map, screened), ('energy', 'cell'),...  3 us
    pallas_call x1, Pallas kernels, pick_screened(): pl.pallas_call(functools.partial(pick_kernel, s), out_shape=out, in_specs...  2.11 us
  transfers between devices with their start and end apart: 15, of which 6 were waited for; matrix products, arithmetic and copies ran while one was open for 0% of the time, Pallas kernels for 11%

profile of v7, /device:TPU:0, one launch (start us, length us, event | category | flops | bytes accessed | tf_op | source)
XLA Modules:
  0.0 68.5 jit_solution(4222325412455464606)
XLA Ops:
  0.0 2.1 %pick_screened.1 = bf16[32,24,4,128]{3,2,1,0:T(4,128)(2,1)} custom-call(s32[8]{0:T(128)} %map_hbm.1, bf16[24,8,4,512]{3,2,1,0:T(4,128)(2,1)} %bitcast.9), custom_call_target="tpu_custom_call" | custom-call | tf_op jit(solution)/shard_map/pick_screened/pallas_call | solution.py:83
  2.1 7.3 %all-to-all-start = ((bf16[32,24,4,128]{3,2,1,0:T(4,128)(2,1)}), bf16[32,24,4,128]{3,2,1,0:T(4,128)(2,1)S(1)}, u32[]{:S(2)}, u32[]{:S(2)}) async-start(bf16[32,24,4,128]{3,2,1,0:T(4,128)(2,1)} %pick_screened.1), calls=%async_computation | async-start | bytes 1572864 | tf_op jit(solution)/shard_map/all_to_all | solution.py:332
  9.6 0.3 collective-permute-start
  10.0 1.7 %collective-permute-start.1 = (bf16[24,16,128]{2,1,0:T(8,128)(2,1)S(1)}, bf16[24,16,128]{2,1,0:T(8,128)(2,1)S(1)}, u32[]{:S(2)}, u32[]{:S(2)}) collective-permute-start(bf16[24,16,128]{2,1,0:T(8,128)(2,1)S(1)} %get-tuple-element.25), channel_id=1, source_target_pairs={{0,8},{4,12},{8,0},{12,4},{16,24},{20,28},{24,16},{28,20},{1,9},{5... | collective-permute-start | bytes 294920 | tf_op jit(solution)/shard_map/ppermute | solution.py:327
  11.6 2.6 %collective-permute-start.3 = (bf16[24,16,128]{2,1,0:T(8,128)(2,1)S(1)}, bf16[24,16,128]{2,1,0:T(8,128)(2,1)S(1)}, u32[]{:S(2)}, u32[]{:S(2)}) collective-permute-start(bf16[24,16,128]{2,1,0:T(8,128)(2,1)S(1)} %get-tuple-element.29), channel_id=1, source_target_pairs={{0,16},{4,20},{8,24},{12,28},{16,0},{20,4},{24,8},{28,12},{1,17},{... | collective-permute-start | bytes 294920 | tf_op jit(solution)/shard_map/ppermute | solution.py:327
  14.4 3.5 %collective-permute-start.5 = (bf16[24,16,128]{2,1,0:T(8,128)(2,1)S(1)}, bf16[24,16,128]{2,1,0:T(8,128)(2,1)S(1)}, u32[]{:S(2)}, u32[]{:S(2)}) collective-permute-start(bf16[24,16,128]{2,1,0:T(8,128)(2,1)S(1)} %get-tuple-element.31), channel_id=1, source_target_pairs={{0,24},{4,28},{8,16},{12,20},{16,8},{20,12},{24,0},{28,4},{1,25},{... | collective-permute-start | bytes 294920 | tf_op jit(solution)/shard_map/ppermute | solution.py:327
  17.9 7.4 %collective-permute-done.1.refs_2_ = bf16[24,16,128]{2,1,0:T(8,128)(2,1)S(1)} collective-permute-done((bf16[24,16,128]{2,1,0:T(8,128)(2,1)S(1)}, bf16[24,16,128]{2,1,0:T(8,128)(2,1)S(1)}, u32[]{:S(2)}, u32[]{:S(2)}) %collective-permute-start.1) | collective-permute-done | bytes 98336 | tf_op jit(solution)/shard_map/ppermute | solution.py:327
  25.3 2.5 %collective-permute-start.6 = (bf16[24,16,128]{2,1,0:T(8,128)(2,1)S(1)}, bf16[24,16,128]{2,1,0:T(8,128)(2,1)S(1)}, u32[]{:S(2)}, u32[]{:S(2)}) collective-permute-start(bf16[24,16,128]{2,1,0:T(8,128)(2,1)S(1)} %get-tuple-element.32), channel_id=1, source_target_pairs={{0,28},{4,24},{8,20},{12,16},{16,12},{20,8},{24,4},{28,0},{1,29},{... | collective-permute-start | bytes 294920 | tf_op jit(solution)/shard_map/ppermute | solution.py:327
  27.8 3.0 %all-to-all-done.screens_ref = bf16[32,24,4,128]{3,2,1,0:T(4,128)(2,1)S(1)} async-done(((bf16[32,24,4,128]{3,2,1,0:T(4,128)(2,1)}), bf16[32,24,4,128]{3,2,1,0:T(4,128)(2,1)S(1)}, u32[]{:S(2)}, u32[]{:S(2)}) %all-to-all-start) | async-done | bytes 786464 | tf_op jit(solution)/shard_map/all_to_all | solution.py:332
  30.8 0.4 stage_near.1
  31.2 4.9 %partial.1.after_ref.begun = f32[8,24,16,128]{3,2,1,0:T(8,128)S(1)} custom-call(s32[1]{0:T(128)} %bitcast.me_ref, s32[64,3]{1,0:T(8,128)S(1)} %bitcast.6, f32[144,16,128]{2,1,0:T(8,128)S(1)} %get-tuple-element.27.g_half, f32[8,24,16,128]{3,2,1,0:T(8,128)S(1)} %get-tuple-element.28.w_all), custom_call_target="tpu_custom_call" | custom-call | tf_op jit(solution)/shard_map/partial/pallas_call | solution.py:220
  36.1 5.0 %collective-permute-done.3.refs_0_ = bf16[24,16,128]{2,1,0:T(8,128)(2,1)S(1)} collective-permute-done((bf16[24,16,128]{2,1,0:T(8,128)(2,1)S(1)}, bf16[24,16,128]{2,1,0:T(8,128)(2,1)S(1)}, u32[]{:S(2)}, u32[]{:S(2)}) %collective-permute-start.3) | collective-permute-done | bytes 98336 | tf_op jit(solution)/shard_map/ppermute | solution.py:327
  41.1 1.2 %collective-permute-done.4.refs_1_ = bf16[24,16,128]{2,1,0:T(8,128)(2,1)S(1)} collective-permute-done((bf16[24,16,128]{2,1,0:T(8,128)(2,1)S(1)}, bf16[24,16,128]{2,1,0:T(8,128)(2,1)S(1)}, u32[]{:S(2)}, u32[]{:S(2)}) %collective-permute-start.4) | collective-permute-done | bytes 98336 | tf_op jit(solution)/shard_map/ppermute | solution.py:327
  42.4 2.1 %sigma.3 = (s16[25,16,128]{2,1,0:T(8,128)(2,1)S(1)}, s16[25,16,128]{2,1,0:T(8,128)(2,1)S(1)}) custom-call(s32[1]{0:T(128)} %bitcast.me_ref, s32[64,3]{1,0:T(8,128)S(1)} %bitcast.7, f32[8,24,16,128]{3,2,1,0:T(8,128)S(1)} %partial.1.after_ref.begun, f32[8,24,16,128]{3,2,1,0:T(8,128)S(1)} %get-tuple-element.28.w_all, f32[144,16,128]{2,1,0:T(8,128)S(1)} %stage_far.1.g_far), custom_call_target="tpu_custom_call" | custom-call | tf_op jit(solution)/shard_map/sigma/pallas_call | solution.py:269
  44.5 1.3 %collective-permute-start.12 = (s16[25,16,128]{2,1,0:T(8,128)(2,1)S(1)}, s16[25,16,128]{2,1,0:T(8,128)(2,1)S(1)}, u32[]{:S(2)}, u32[]{:S(2)}) collective-permute-start(s16[25,16,128]{2,1,0:T(8,128)(2,1)S(1)} %get-tuple-element.39), channel_id=1, source_target_pairs={{0,24},{4,28},{8,16},{12,20},{16,8},{20,12},{24,0},{28,4},{1,25},{... | collective-permute-start | bytes 307208 | tf_op jit(solution)/shard_map/ppermute | solution.py:327
  45.9 2.7 %collective-permute-start.13 = (s16[25,16,128]{2,1,0:T(8,128)(2,1)S(1)}, s16[25,16,128]{2,1,0:T(8,128)(2,1)S(1)}, u32[]{:S(2)}, u32[]{:S(2)}) collective-permute-start(s16[25,16,128]{2,1,0:T(8,128)(2,1)S(1)} %get-tuple-element.40), channel_id=1, source_target_pairs={{0,28},{4,24},{8,20},{12,16},{16,12},{20,8},{24,4},{28,0},{1,29},{... | collective-permute-start | bytes 307208 | tf_op jit(solution)/shard_map/ppermute | solution.py:327
  48.5 2.0 %sigma.2 = (f32[24,16,128]{2,1,0:T(8,128)S(1)}, s16[25,16,128]{2,1,0:T(8,128)(2,1)S(1)}, s16[25,16,128]{2,1,0:T(8,128)(2,1)S(1)}, s16[25,16,128]{2,1,0:T(8,128)(...) custom-call(s32[1]{0:T(128)} %bitcast.me_ref, s32[64,3]{1,0:T(8,128)S(1)} %bitcast.8, ...), custom_call_target="tpu_custom_call" | custom-call | tf_op jit(solution)/shard_map/sigma/pallas_call | solution.py:269
  50.5 5.0 %collective-permute-start.10 = (s16[25,16,128]{2,1,0:T(8,128)(2,1)S(1)}, s16[25,16,128]{2,1,0:T(8,128)(2,1)S(1)}, u32[]{:S(2)}, u32[]{:S(2)}) collective-permute-start(s16[25,16,128]{2,1,0:T(8,128)(2,1)S(1)} %get-tuple-element.37), channel_id=1, source_target_pairs={{0,16},{4,20},{8,24},{12,28},{16,0},{20,4},{24,8},{28,12},{1,17},{... | collective-permute-start | bytes 307208 | tf_op jit(solution)/shard_map/ppermute | solution.py:327
  55.5 0.4 collective-permute-start.11
  55.9 1.4 %collective-permute-start.8 = (s16[25,16,128]{2,1,0:T(8,128)(2,1)S(1)}, s16[25,16,128]{2,1,0:T(8,128)(2,1)S(1)}, u32[]{:S(2)}, u32[]{:S(2)}) collective-permute-start(s16[25,16,128]{2,1,0:T(8,128)(2,1)S(1)} %get-tuple-element.35), channel_id=1, source_target_pairs={{0,12},{4,8},{8,4},{12,0},{16,28},{20,24},{24,20},{28,16},{1,13},{... | collective-permute-start | bytes 307208 | tf_op jit(solution)/shard_map/ppermute | solution.py:327
  57.3 0.8 %collective-permute-start.9 = (s16[25,16,128]{2,1,0:T(8,128)(2,1)S(1)}, s16[25,16,128]{2,1,0:T(8,128)(2,1)S(1)}, u32[]{:S(2)}, u32[]{:S(2)}) collective-permute-start(s16[25,16,128]{2,1,0:T(8,128)(2,1)S(1)} %get-tuple-element.36), channel_id=1, source_target_pairs={{0,4},{4,0},{8,12},{12,8},{16,20},{20,16},{24,28},{28,24},{1,5},{5... | collective-permute-start | bytes 307208 | tf_op jit(solution)/shard_map/ppermute | solution.py:327
  58.0 7.2 %collective-permute-done.10.refs_4_ = s16[25,16,128]{2,1,0:T(8,128)(2,1)S(1)} collective-permute-done((s16[25,16,128]{2,1,0:T(8,128)(2,1)S(1)}, s16[25,16,128]{2,1,0:T(8,128)(2,1)S(1)}, u32[]{:S(2)}, u32[]{:S(2)}) %collective-permute-start.10) | collective-permute-done | bytes 102432 | tf_op jit(solution)/shard_map/ppermute | solution.py:327
  65.2 2.1 %collective-permute-done.11.refs_5_ = s16[25,16,128]{2,1,0:T(8,128)(2,1)S(1)} collective-permute-done((s16[25,16,128]{2,1,0:T(8,128)(2,1)S(1)}, s16[25,16,128]{2,1,0:T(8,128)(2,1)S(1)}, u32[]{:S(2)}, u32[]{:S(2)}) %collective-permute-start.11) | collective-permute-done | bytes 102432 | tf_op jit(solution)/shard_map/ppermute | solution.py:327
  67.3 1.3 %unpack.1 = f32[24,2,16,512]{3,2,1,0:T(8,128)} custom-call(s32[1]{0:T(128)} %bitcast.me_ref, f32[24,16,128]{2,1,0:T(8,128)S(1)} %get-tuple-element.33.refs_0_, s16[25,16,128]{2,1,0:T(8,128)(2,1)S(1)} %collective-permute-done.7.refs_1_, s16[25,16,128]{2,1,0:T(8,128)(2,1)S(1)} %collective-permute-done.8.refs_2_, ...), custom_call_target="tpu_custom_call" | custom-call | tf_op jit(solution)/shard_map/unpack/pallas_call | solution.py:311
  (22 shorter events, 0.5 us)
Async XLA Ops:
  0.0 9.5 %copy-start = (bf16[4,6,2,16,512]{4,3,2,1,0:T(8,128)(2,1)S(1)}, bf16[4,6,2,16,512]{4,3,2,1,0:T(8,128)(2,1)}, u32[]{:S(2)}) copy-start(bf16[4,6,2,16,512]{4,3,2,1,0:T(8,128)(2,1)} %param.5) | copy-start | bytes 2359300
  2.1 25.6 %copy-start.1 = (s32[8,8,3]{1,0,2:T(8,128)S(1)}, s32[8,8,3]{1,0,2:T(8,128)}, u32[]{:S(2)}) copy-start(s32[8,8,3]{1,0,2:T(8,128)} %param.8) | copy-start | bytes 2308
  2.1 25.6 %copy-start.2 = (s32[8,8]{1,0:T(8,128)S(1)}, s32[8,8]{1,0:T(8,128)}, u32[]{:S(2)}) copy-start(s32[8,8]{1,0:T(8,128)} %param.9) | copy-start | bytes 772
  2.1 28.7 %all-to-all-start = ((bf16[32,24,4,128]{3,2,1,0:T(4,128)(2,1)}), bf16[32,24,4,128]{3,2,1,0:T(4,128)(2,1)S(1)}, u32[]{:S(2)}, u32[]{:S(2)}) async-start(bf16[32,24,4,128]{3,2,1,0:T(4,128)(2,1)} %pick_screened.1), calls=%async_computation | async-start | bytes 1572864 | tf_op jit(solution)/shard_map/all_to_all | solution.py:332
  9.6 4.7 %collective-permute-start = (bf16[24,16,128]{2,1,0:T(8,128)(2,1)S(1)}, bf16[24,16,128]{2,1,0:T(8,128)(2,1)S(1)}, u32[]{:S(2)}, u32[]{:S(2)}) collective-permute-start(bf16[24,16,128]{2,1,0:T(8,128)(2,1)S(1)} %get-tuple-element.24), channel_id=1, source_target_pairs={{0,4},{4,0},{8,12},{12,8},{16,20},{20,16},{24,28},{28,24},{1,5},{5... | collective-permute-start | bytes 294920 | tf_op jit(solution)/shard_map/ppermute | solution.py:327
  10.0 15.3 %collective-permute-start.1 = (bf16[24,16,128]{2,1,0:T(8,128)(2,1)S(1)}, bf16[24,16,128]{2,1,0:T(8,128)(2,1)S(1)}, u32[]{:S(2)}, u32[]{:S(2)}) collective-permute-start(bf16[24,16,128]{2,1,0:T(8,128)(2,1)S(1)} %get-tuple-element.25), channel_id=1, source_target_pairs={{0,8},{4,12},{8,0},{12,4},{16,24},{20,28},{24,16},{28,20},{1,9},{5... | collective-permute-start | bytes 294920 | tf_op jit(solution)/shard_map/ppermute | solution.py:327
  11.6 16.2 %collective-permute-start.2 = (bf16[24,16,128]{2,1,0:T(8,128)(2,1)S(1)}, bf16[24,16,128]{2,1,0:T(8,128)(2,1)S(1)}, u32[]{:S(2)}, u32[]{:S(2)}) collective-permute-start(bf16[24,16,128]{2,1,0:T(8,128)(2,1)S(1)} %get-tuple-element.26), channel_id=1, source_target_pairs={{0,12},{4,8},{8,4},{12,0},{16,28},{20,24},{24,20},{28,16},{1,13},{... | collective-permute-start | bytes 294920 | tf_op jit(solution)/shard_map/ppermute | solution.py:327
  11.6 29.5 %collective-permute-start.3 = (bf16[24,16,128]{2,1,0:T(8,128)(2,1)S(1)}, bf16[24,16,128]{2,1,0:T(8,128)(2,1)S(1)}, u32[]{:S(2)}, u32[]{:S(2)}) collective-permute-start(bf16[24,16,128]{2,1,0:T(8,128)(2,1)S(1)} %get-tuple-element.29), channel_id=1, source_target_pairs={{0,16},{4,20},{8,24},{12,28},{16,0},{20,4},{24,8},{28,12},{1,17},{... | collective-permute-start | bytes 294920 | tf_op jit(solution)/shard_map/ppermute | solution.py:327
  14.2 28.0 %collective-permute-start.4 = (bf16[24,16,128]{2,1,0:T(8,128)(2,1)S(1)}, bf16[24,16,128]{2,1,0:T(8,128)(2,1)S(1)}, u32[]{:S(2)}, u32[]{:S(2)}) collective-permute-start(bf16[24,16,128]{2,1,0:T(8,128)(2,1)S(1)} %get-tuple-element.30), channel_id=1, source_target_pairs={{0,20},{4,16},{8,28},{12,24},{16,4},{20,0},{24,12},{28,8},{1,21},{... | collective-permute-start | bytes 294920 | tf_op jit(solution)/shard_map/ppermute | solution.py:327
  14.4 27.9 %collective-permute-start.5 = (bf16[24,16,128]{2,1,0:T(8,128)(2,1)S(1)}, bf16[24,16,128]{2,1,0:T(8,128)(2,1)S(1)}, u32[]{:S(2)}, u32[]{:S(2)}) collective-permute-start(bf16[24,16,128]{2,1,0:T(8,128)(2,1)S(1)} %get-tuple-element.31), channel_id=1, source_target_pairs={{0,24},{4,28},{8,16},{12,20},{16,8},{20,12},{24,0},{28,4},{1,25},{... | collective-permute-start | bytes 294920 | tf_op jit(solution)/shard_map/ppermute | solution.py:327
  25.3 17.0 %collective-permute-start.6 = (bf16[24,16,128]{2,1,0:T(8,128)(2,1)S(1)}, bf16[24,16,128]{2,1,0:T(8,128)(2,1)S(1)}, u32[]{:S(2)}, u32[]{:S(2)}) collective-permute-start(bf16[24,16,128]{2,1,0:T(8,128)(2,1)S(1)} %get-tuple-element.32), channel_id=1, source_target_pairs={{0,28},{4,24},{8,20},{12,16},{16,12},{20,8},{24,4},{28,0},{1,29},{... | collective-permute-start | bytes 294920 | tf_op jit(solution)/shard_map/ppermute | solution.py:327
  44.5 11.3 %collective-permute-start.12 = (s16[25,16,128]{2,1,0:T(8,128)(2,1)S(1)}, s16[25,16,128]{2,1,0:T(8,128)(2,1)S(1)}, u32[]{:S(2)}, u32[]{:S(2)}) collective-permute-start(s16[25,16,128]{2,1,0:T(8,128)(2,1)S(1)} %get-tuple-element.39), channel_id=1, source_target_pairs={{0,24},{4,28},{8,16},{12,20},{16,8},{20,12},{24,0},{28,4},{1,25},{... | collective-permute-start | bytes 307208 | tf_op jit(solution)/shard_map/ppermute | solution.py:327
  45.9 11.4 %collective-permute-start.13 = (s16[25,16,128]{2,1,0:T(8,128)(2,1)S(1)}, s16[25,16,128]{2,1,0:T(8,128)(2,1)S(1)}, u32[]{:S(2)}, u32[]{:S(2)}) collective-permute-start(s16[25,16,128]{2,1,0:T(8,128)(2,1)S(1)} %get-tuple-element.40), channel_id=1, source_target_pairs={{0,28},{4,24},{8,20},{12,16},{16,12},{20,8},{24,4},{28,0},{1,29},{... | collective-permute-start | bytes 307208 | tf_op jit(solution)/shard_map/ppermute | solution.py:327
  50.5 14.6 %collective-permute-start.10 = (s16[25,16,128]{2,1,0:T(8,128)(2,1)S(1)}, s16[25,16,128]{2,1,0:T(8,128)(2,1)S(1)}, u32[]{:S(2)}, u32[]{:S(2)}) collective-permute-start(s16[25,16,128]{2,1,0:T(8,128)(2,1)S(1)} %get-tuple-element.37), channel_id=1, source_target_pairs={{0,16},{4,20},{8,24},{12,28},{16,0},{20,4},{24,8},{28,12},{1,17},{... | collective-permute-start | bytes 307208 | tf_op jit(solution)/shard_map/ppermute | solution.py:327
  55.5 11.7 %collective-permute-start.11 = (s16[25,16,128]{2,1,0:T(8,128)(2,1)S(1)}, s16[25,16,128]{2,1,0:T(8,128)(2,1)S(1)}, u32[]{:S(2)}, u32[]{:S(2)}) collective-permute-start(s16[25,16,128]{2,1,0:T(8,128)(2,1)S(1)} %get-tuple-element.38), channel_id=1, source_target_pairs={{0,20},{4,16},{8,28},{12,24},{16,4},{20,0},{24,12},{28,8},{1,21},{... | collective-permute-start | bytes 307208 | tf_op jit(solution)/shard_map/ppermute | solution.py:327
  55.9 11.4 %collective-permute-start.7 = (s16[25,16,128]{2,1,0:T(8,128)(2,1)S(1)}, s16[25,16,128]{2,1,0:T(8,128)(2,1)S(1)}, u32[]{:S(2)}, u32[]{:S(2)}) collective-permute-start(s16[25,16,128]{2,1,0:T(8,128)(2,1)S(1)} %get-tuple-element.34), channel_id=1, source_target_pairs={{0,8},{4,12},{8,0},{12,4},{16,24},{20,28},{24,16},{28,20},{1,9},{5... | collective-permute-start | bytes 307208 | tf_op jit(solution)/shard_map/ppermute | solution.py:327
  55.9 11.4 %collective-permute-start.8 = (s16[25,16,128]{2,1,0:T(8,128)(2,1)S(1)}, s16[25,16,128]{2,1,0:T(8,128)(2,1)S(1)}, u32[]{:S(2)}, u32[]{:S(2)}) collective-permute-start(s16[25,16,128]{2,1,0:T(8,128)(2,1)S(1)} %get-tuple-element.35), channel_id=1, source_target_pairs={{0,12},{4,8},{8,4},{12,0},{16,28},{20,24},{24,20},{28,16},{1,13},{... | collective-permute-start | bytes 307208 | tf_op jit(solution)/shard_map/ppermute | solution.py:327
  57.3 10.0 %collective-permute-start.9 = (s16[25,16,128]{2,1,0:T(8,128)(2,1)S(1)}, s16[25,16,128]{2,1,0:T(8,128)(2,1)S(1)}, u32[]{:S(2)}, u32[]{:S(2)}) collective-permute-start(s16[25,16,128]{2,1,0:T(8,128)(2,1)S(1)} %get-tuple-element.36), channel_id=1, source_target_pairs={{0,4},{4,0},{8,12},{12,8},{16,20},{20,16},{24,28},{28,24},{1,5},{5... | collective-permute-start | bytes 307208 | tf_op jit(solution)/shard_map/ppermute | solution.py:327

commit v8 on v7

--- a/solution.py
+++ b/solution.py
@@ -9,8 +9,9 @@
 
 SCALE = 0.2
 LANES = 128
-PAIR = 2
+PAIR = 4
 STEPS = 32700.0
+STRIP = 8
 FINE = 64.0
 TINY = 1e-34
 PICKS = 8
@@ -33,7 +34,8 @@
         self.half = groups // 2
         self.held_planes = (self.half + 2) * self.energies
         self.scales = self.planes // PAIR
-        self.scale_planes = -(-self.scales // self.plane[0])
+        self.strips = self.plane[0] // STRIP
+        self.scale_strips = -(-self.scales // STRIP)
 
     def where(self, index):
         cell, tile, part = index // self.slices, (index // self.parts) % self.tiles, index % self.parts
@@ -230,7 +232,7 @@
 def sigma_kernel(s, slots, ks, me_ref, table_ref, begun, w_all, g_far, *outs):
     me = me_ref[0]
     side = me // s.half
-    row = lax.broadcasted_iota(jnp.int32, s.plane, 0)
+    row = lax.broadcasted_iota(jnp.int32, (STRIP, LANES), 0)
     for at, k in enumerate(ks):
 
         def turn(kind, codes):
@@ -250,22 +252,24 @@
                 code = jnp.ceil(jnp.log2(largest) * FINE)
                 inverse = jnp.exp2(code * (-1.0 / FINE)) * STEPS
                 where = (first + low) // PAIR
-                for i in range(s.scale_planes):
-                    codes[i] = jnp.where(row + i * s.plane[0] == where, code, codes[i])
+                for i in range(s.scale_strips):
+                    codes[i] = jnp.where(row + i * STRIP == where, code, codes[i])
                 for j, total in enumerate(pair):
                     coded = jnp.round(total * inverse).astype(jnp.int32)
-                    outs[at][first + low + j] = coded.astype(jnp.int16)
+                    for i in range(s.strips):
+                        strip = coded[i * STRIP : (i + 1) * STRIP].astype(jnp.int16)
+                        outs[at][(first + low + j) * s.strips + i] = strip
             return tuple(codes)
 
-        codes = lax.fori_loop(0, 2, turn, tuple(jnp.zeros(s.plane, jnp.float32) for _ in range(s.scale_planes)))
+        codes = lax.fori_loop(0, 2, turn, tuple(jnp.zeros((STRIP, LANES), jnp.float32) for _ in range(s.scale_strips)))
         if k != 0:
-            for j in range(s.scale_planes):
-                outs[at][s.planes + j] = codes[j].astype(jnp.int32).astype(jnp.int16)
+            for j in range(s.scale_strips):
+                outs[at][s.planes * s.strips + j] = codes[j].astype(jnp.int32).astype(jnp.int16)
 
 
 def sigma_of(s, me, table, begun, w_all, g_far, ks):
     own = jax.ShapeDtypeStruct((s.planes,) + s.plane, jnp.float32)
-    coded = jax.ShapeDtypeStruct((s.planes + s.scale_planes,) + s.plane, jnp.int16)
+    coded = jax.ShapeDtypeStruct((s.planes * s.strips + s.scale_strips, STRIP, LANES), jnp.int16)
     return pl.pallas_call(
         functools.partial(sigma_kernel, s, table.shape[1], ks),
         out_shape=[own if k == 0 else coded for k in ks],
@@ -287,18 +291,20 @@
         rows = slice(None) if s.parts == 1 else pl.ds(pl.multiple_of(part * s.plane[0], s.plane[0]), s.plane[0])
         places.append((cell, rows, lanes))
         if k != 0:
-            for j in range(s.scale_planes):
-                code = block[s.planes + j].astype(jnp.int32).astype(jnp.float32)
-                scales[k, j * s.plane[0] : (j + 1) * s.plane[0]] = jnp.exp2(code * (1.0 / FINE)) * (1.0 / STEPS)
+            for j in range(s.scale_strips):
+                code = block[s.planes * s.strips + j].astype(jnp.int32).astype(jnp.float32)
+                scales[k, j * STRIP : (j + 1) * STRIP] = jnp.exp2(code * (1.0 / FINE)) * (1.0 / STEPS)
     leaving = []
     for comp in range(s.comps):
         chunk = pl.ds(comp * s.energies, s.energies)
         for plane in range(comp * s.energies, (comp + 1) * s.energies):
             pair = plane // PAIR
             for k, (cell, rows, lanes) in enumerate(places):
-                value = blocks[k][plane]
-                if k != 0:
-                    value = value.astype(jnp.int32).astype(jnp.float32) * scales[k, pair : pair + 1]
+                if k == 0:
+                    value = blocks[0][plane]
+                else:
+                    strips = [blocks[k][plane * s.strips + i].astype(jnp.int32) for i in range(s.strips)]
+                    value = jnp.concatenate(strips, axis=0).astype(jnp.float32) * scales[k, pair : pair + 1]
                 whole_ref[plane, cell, rows, lanes] = value
         leaving.append(pltpu.make_async_copy(whole_ref.at[chunk], whole_hbm.at[chunk], sems.at[comp]))
         leaving[-1].start()
@@ -315,7 +321,7 @@
         out_specs=ANY,
         scratch_shapes=[
             pltpu.VMEM(shape, jnp.float32),
-            pltpu.VMEM((s.groups, s.scale_planes * s.plane[0], LANES), jnp.float32),
+            pltpu.VMEM((s.groups, s.scale_strips * STRIP, LANES), jnp.float32),
             pltpu.SemaphoreType.DMA((s.comps,)),
         ],
         compiler_params=PARAMS,

time: 68.8 us -> 68.4 us (level)
  no operation moved by 1% of the time
where the time goes in v8:
time: 68.4 us; the launch traced here: 68.2 us
  starting transfers between devices  29.4 us (43%)
  waiting for transfers between devices  25.6 us (37%)
  Pallas kernels  12.9 us (19%)
    ppermute x14, waiting for transfers between devices, swap(): lax.ppermute(block, 'energy', [(i, i ^ k) for i in range(s.groups)])  22.6 us
    ppermute x14, starting transfers between devices, swap(): lax.ppermute(block, 'energy', [(i, i ^ k) for i in range(s.groups)])  22.1 us
    all_to_all x1, starting transfers between devices, send_screened(): lax.all_to_all(pick_screened(s, cell_map, screened), ('energy', 'cell'),...  7.3 us
    pallas_call x1, Pallas kernels, partial_of(): pl.pallas_call(functools.partial(partial_kernel, s, table.shape[1]), out_...  4.9 us
    pallas_call x2, Pallas kernels, sigma_of(): pl.pallas_call(functools.partial(sigma_kernel, s, table.shape[1], ks), ou...  4.04 us
    all_to_all x1, waiting for transfers between devices, send_screened(): lax.all_to_all(pick_screened(s, cell_map, screened), ('energy', 'cell'),...  3 us
    pallas_call x1, Pallas kernels, pick_screened(): pl.pallas_call(functools.partial(pick_kernel, s), out_shape=out, in_specs...  2.11 us
  transfers between devices with their start and end apart: 15, of which 6 were waited for; matrix products, arithmetic and copies ran while one was open for 0% of the time, Pallas kernels for 11%

profile of v8, /device:TPU:0, one launch (start us, length us, event | category | flops | bytes accessed | tf_op | source)
XLA Modules:
  0.0 68.2 jit_solution(8869904032085448313)
XLA Ops:
  0.0 2.1 %pick_screened.1 = bf16[32,24,4,128]{3,2,1,0:T(4,128)(2,1)} custom-call(s32[8]{0:T(128)} %map_hbm.1, bf16[24,8,4,512]{3,2,1,0:T(4,128)(2,1)} %bitcast.9), custom_call_target="tpu_custom_call" | custom-call | tf_op jit(solution)/shard_map/pick_screened/pallas_call | solution.py:85
  2.1 7.3 %all-to-all-start = ((bf16[32,24,4,128]{3,2,1,0:T(4,128)(2,1)}), bf16[32,24,4,128]{3,2,1,0:T(4,128)(2,1)S(1)}, u32[]{:S(2)}, u32[]{:S(2)}) async-start(bf16[32,24,4,128]{3,2,1,0:T(4,128)(2,1)} %pick_screened.1), calls=%async_computation | async-start | bytes 1572864 | tf_op jit(solution)/shard_map/all_to_all | solution.py:338
  9.6 0.3 collective-permute-start
  10.0 1.7 %collective-permute-start.1 = (bf16[24,16,128]{2,1,0:T(8,128)(2,1)S(1)}, bf16[24,16,128]{2,1,0:T(8,128)(2,1)S(1)}, u32[]{:S(2)}, u32[]{:S(2)}) collective-permute-start(bf16[24,16,128]{2,1,0:T(8,128)(2,1)S(1)} %get-tuple-element.25), channel_id=1, source_target_pairs={{0,8},{4,12},{8,0},{12,4},{16,24},{20,28},{24,16},{28,20},{1,9},{5... | collective-permute-start | bytes 294920 | tf_op jit(solution)/shard_map/ppermute | solution.py:333
  11.6 2.6 %collective-permute-start.3 = (bf16[24,16,128]{2,1,0:T(8,128)(2,1)S(1)}, bf16[24,16,128]{2,1,0:T(8,128)(2,1)S(1)}, u32[]{:S(2)}, u32[]{:S(2)}) collective-permute-start(bf16[24,16,128]{2,1,0:T(8,128)(2,1)S(1)} %get-tuple-element.29), channel_id=1, source_target_pairs={{0,16},{4,20},{8,24},{12,28},{16,0},{20,4},{24,8},{28,12},{1,17},{... | collective-permute-start | bytes 294920 | tf_op jit(solution)/shard_map/ppermute | solution.py:333
  14.3 3.5 %collective-permute-start.5 = (bf16[24,16,128]{2,1,0:T(8,128)(2,1)S(1)}, bf16[24,16,128]{2,1,0:T(8,128)(2,1)S(1)}, u32[]{:S(2)}, u32[]{:S(2)}) collective-permute-start(bf16[24,16,128]{2,1,0:T(8,128)(2,1)S(1)} %get-tuple-element.31), channel_id=1, source_target_pairs={{0,24},{4,28},{8,16},{12,20},{16,8},{20,12},{24,0},{28,4},{1,25},{... | collective-permute-start | bytes 294920 | tf_op jit(solution)/shard_map/ppermute | solution.py:333
  17.9 7.4 %collective-permute-done.1.refs_2_ = bf16[24,16,128]{2,1,0:T(8,128)(2,1)S(1)} collective-permute-done((bf16[24,16,128]{2,1,0:T(8,128)(2,1)S(1)}, bf16[24,16,128]{2,1,0:T(8,128)(2,1)S(1)}, u32[]{:S(2)}, u32[]{:S(2)}) %collective-permute-start.1) | collective-permute-done | bytes 98336 | tf_op jit(solution)/shard_map/ppermute | solution.py:333
  25.3 2.5 %collective-permute-start.6 = (bf16[24,16,128]{2,1,0:T(8,128)(2,1)S(1)}, bf16[24,16,128]{2,1,0:T(8,128)(2,1)S(1)}, u32[]{:S(2)}, u32[]{:S(2)}) collective-permute-start(bf16[24,16,128]{2,1,0:T(8,128)(2,1)S(1)} %get-tuple-element.32), channel_id=1, source_target_pairs={{0,28},{4,24},{8,20},{12,16},{16,12},{20,8},{24,4},{28,0},{1,29},{... | collective-permute-start | bytes 294920 | tf_op jit(solution)/shard_map/ppermute | solution.py:333
  27.8 3.0 %all-to-all-done.screens_ref = bf16[32,24,4,128]{3,2,1,0:T(4,128)(2,1)S(1)} async-done(((bf16[32,24,4,128]{3,2,1,0:T(4,128)(2,1)}), bf16[32,24,4,128]{3,2,1,0:T(4,128)(2,1)S(1)}, u32[]{:S(2)}, u32[]{:S(2)}) %all-to-all-start) | async-done | bytes 786464 | tf_op jit(solution)/shard_map/all_to_all | solution.py:338
  30.8 0.4 stage_near.1
  31.2 4.9 %partial.1.after_ref.begun = f32[8,24,16,128]{3,2,1,0:T(8,128)S(1)} custom-call(s32[1]{0:T(128)} %bitcast.me_ref, s32[64,3]{1,0:T(8,128)S(1)} %bitcast.6, f32[144,16,128]{2,1,0:T(8,128)S(1)} %get-tuple-element.27.g_half, f32[8,24,16,128]{3,2,1,0:T(8,128)S(1)} %get-tuple-element.28.w_all), custom_call_target="tpu_custom_call" | custom-call | tf_op jit(solution)/shard_map/partial/pallas_call | solution.py:222
  36.1 5.0 %collective-permute-done.3.refs_0_ = bf16[24,16,128]{2,1,0:T(8,128)(2,1)S(1)} collective-permute-done((bf16[24,16,128]{2,1,0:T(8,128)(2,1)S(1)}, bf16[24,16,128]{2,1,0:T(8,128)(2,1)S(1)}, u32[]{:S(2)}, u32[]{:S(2)}) %collective-permute-start.3) | collective-permute-done | bytes 98336 | tf_op jit(solution)/shard_map/ppermute | solution.py:333
  41.1 1.2 %collective-permute-done.4.refs_1_ = bf16[24,16,128]{2,1,0:T(8,128)(2,1)S(1)} collective-permute-done((bf16[24,16,128]{2,1,0:T(8,128)(2,1)S(1)}, bf16[24,16,128]{2,1,0:T(8,128)(2,1)S(1)}, u32[]{:S(2)}, u32[]{:S(2)}) %collective-permute-start.4) | collective-permute-done | bytes 98336 | tf_op jit(solution)/shard_map/ppermute | solution.py:333
  42.4 2.1 %sigma.3 = (s16[49,8,128]{2,1,0:T(8,128)(2,1)S(1)}, s16[49,8,128]{2,1,0:T(8,128)(2,1)S(1)}) custom-call(s32[1]{0:T(128)} %bitcast.me_ref, s32[64,3]{1,0:T(8,128)S(1)} %bitcast.7, f32[8,24,16,128]{3,2,1,0:T(8,128)S(1)} %partial.1.after_ref.begun, f32[8,24,16,128]{3,2,1,0:T(8,128)S(1)} %get-tuple-element.28.w_all, f32[144,16,128]{2,1,0:T(8,128)S(1)} %stage_far.1.g_far), custom_call_target="tpu_custom_call" | custom-call | tf_op jit(solution)/shard_map/sigma/pallas_call | solution.py:273
  44.5 1.3 %collective-permute-start.12 = (s16[49,8,128]{2,1,0:T(8,128)(2,1)S(1)}, s16[49,8,128]{2,1,0:T(8,128)(2,1)S(1)}, u32[]{:S(2)}, u32[]{:S(2)}) collective-permute-start(s16[49,8,128]{2,1,0:T(8,128)(2,1)S(1)} %get-tuple-element.39), channel_id=1, source_target_pairs={{0,24},{4,28},{8,16},{12,20},{16,8},{20,12},{24,0},{28,4},{1,25},{... | collective-permute-start | bytes 301064 | tf_op jit(solution)/shard_map/ppermute | solution.py:333
  45.8 2.6 %collective-permute-start.13 = (s16[49,8,128]{2,1,0:T(8,128)(2,1)S(1)}, s16[49,8,128]{2,1,0:T(8,128)(2,1)S(1)}, u32[]{:S(2)}, u32[]{:S(2)}) collective-permute-start(s16[49,8,128]{2,1,0:T(8,128)(2,1)S(1)} %get-tuple-element.40), channel_id=1, source_target_pairs={{0,28},{4,24},{8,20},{12,16},{16,12},{20,8},{24,4},{28,0},{1,29},{... | collective-permute-start | bytes 301064 | tf_op jit(solution)/shard_map/ppermute | solution.py:333
  48.5 2.0 %sigma.2 = (f32[24,16,128]{2,1,0:T(8,128)S(1)}, s16[49,8,128]{2,1,0:T(8,128)(2,1)S(1)}, s16[49,8,128]{2,1,0:T(8,128)(2,1)S(1)}, s16[49,8,128]{2,1,0:T(8,128)(2,1...) custom-call(s32[1]{0:T(128)} %bitcast.me_ref, s32[64,3]{1,0:T(8,128)S(1)} %bitcast.8, ...), custom_call_target="tpu_custom_call" | custom-call | tf_op jit(solution)/shard_map/sigma/pallas_call | solution.py:273
  50.4 4.9 %collective-permute-start.10 = (s16[49,8,128]{2,1,0:T(8,128)(2,1)S(1)}, s16[49,8,128]{2,1,0:T(8,128)(2,1)S(1)}, u32[]{:S(2)}, u32[]{:S(2)}) collective-permute-start(s16[49,8,128]{2,1,0:T(8,128)(2,1)S(1)} %get-tuple-element.37), channel_id=1, source_target_pairs={{0,16},{4,20},{8,24},{12,28},{16,0},{20,4},{24,8},{28,12},{1,17},{... | collective-permute-start | bytes 301064 | tf_op jit(solution)/shard_map/ppermute | solution.py:333
  55.4 0.4 collective-permute-start.11
  55.7 1.4 %collective-permute-start.8 = (s16[49,8,128]{2,1,0:T(8,128)(2,1)S(1)}, s16[49,8,128]{2,1,0:T(8,128)(2,1)S(1)}, u32[]{:S(2)}, u32[]{:S(2)}) collective-permute-start(s16[49,8,128]{2,1,0:T(8,128)(2,1)S(1)} %get-tuple-element.35), channel_id=1, source_target_pairs={{0,12},{4,8},{8,4},{12,0},{16,28},{20,24},{24,20},{28,16},{1,13},{... | collective-permute-start | bytes 301064 | tf_op jit(solution)/shard_map/ppermute | solution.py:333
  57.1 0.8 %collective-permute-start.9 = (s16[49,8,128]{2,1,0:T(8,128)(2,1)S(1)}, s16[49,8,128]{2,1,0:T(8,128)(2,1)S(1)}, u32[]{:S(2)}, u32[]{:S(2)}) collective-permute-start(s16[49,8,128]{2,1,0:T(8,128)(2,1)S(1)} %get-tuple-element.36), channel_id=1, source_target_pairs={{0,4},{4,0},{8,12},{12,8},{16,20},{20,16},{24,28},{28,24},{1,5},{5... | collective-permute-start | bytes 301064 | tf_op jit(solution)/shard_map/ppermute | solution.py:333
  57.9 7.0 %collective-permute-done.10.refs_4_ = s16[49,8,128]{2,1,0:T(8,128)(2,1)S(1)} collective-permute-done((s16[49,8,128]{2,1,0:T(8,128)(2,1)S(1)}, s16[49,8,128]{2,1,0:T(8,128)(2,1)S(1)}, u32[]{:S(2)}, u32[]{:S(2)}) %collective-permute-start.10) | collective-permute-done | bytes 100384 | tf_op jit(solution)/shard_map/ppermute | solution.py:333
  64.9 2.0 %collective-permute-done.11.refs_5_ = s16[49,8,128]{2,1,0:T(8,128)(2,1)S(1)} collective-permute-done((s16[49,8,128]{2,1,0:T(8,128)(2,1)S(1)}, s16[49,8,128]{2,1,0:T(8,128)(2,1)S(1)}, u32[]{:S(2)}, u32[]{:S(2)}) %collective-permute-start.11) | collective-permute-done | bytes 100384 | tf_op jit(solution)/shard_map/ppermute | solution.py:333
  66.9 1.3 %unpack.1 = f32[24,2,16,512]{3,2,1,0:T(8,128)} custom-call(s32[1]{0:T(128)} %bitcast.me_ref, f32[24,16,128]{2,1,0:T(8,128)S(1)} %get-tuple-element.33.refs_0_, s16[49,8,128]{2,1,0:T(8,128)(2,1)S(1)} %collective-permute-done.7.refs_1_, s16[49,8,128]{2,1,0:T(8,128)(2,1)S(1)} %collective-permute-done.8.refs_2_, ...), custom_call_target="tpu_custom_call" | custom-call | tf_op jit(solution)/shard_map/unpack/pallas_call | solution.py:317
  (22 shorter events, 0.6 us)
Async XLA Ops:
  0.0 9.5 %copy-start = (bf16[4,6,2,16,512]{4,3,2,1,0:T(8,128)(2,1)S(1)}, bf16[4,6,2,16,512]{4,3,2,1,0:T(8,128)(2,1)}, u32[]{:S(2)}) copy-start(bf16[4,6,2,16,512]{4,3,2,1,0:T(8,128)(2,1)} %param.5) | copy-start | bytes 2359300
  2.1 25.6 %copy-start.1 = (s32[8,8,3]{1,0,2:T(8,128)S(1)}, s32[8,8,3]{1,0,2:T(8,128)}, u32[]{:S(2)}) copy-start(s32[8,8,3]{1,0,2:T(8,128)} %param.8) | copy-start | bytes 2308
  2.1 25.6 %copy-start.2 = (s32[8,8]{1,0:T(8,128)S(1)}, s32[8,8]{1,0:T(8,128)}, u32[]{:S(2)}) copy-start(s32[8,8]{1,0:T(8,128)} %param.9) | copy-start | bytes 772
  2.1 28.7 %all-to-all-start = ((bf16[32,24,4,128]{3,2,1,0:T(4,128)(2,1)}), bf16[32,24,4,128]{3,2,1,0:T(4,128)(2,1)S(1)}, u32[]{:S(2)}, u32[]{:S(2)}) async-start(bf16[32,24,4,128]{3,2,1,0:T(4,128)(2,1)} %pick_screened.1), calls=%async_computation | async-start | bytes 1572864 | tf_op jit(solution)/shard_map/all_to_all | solution.py:338
  9.6 4.7 %collective-permute-start = (bf16[24,16,128]{2,1,0:T(8,128)(2,1)S(1)}, bf16[24,16,128]{2,1,0:T(8,128)(2,1)S(1)}, u32[]{:S(2)}, u32[]{:S(2)}) collective-permute-start(bf16[24,16,128]{2,1,0:T(8,128)(2,1)S(1)} %get-tuple-element.24), channel_id=1, source_target_pairs={{0,4},{4,0},{8,12},{12,8},{16,20},{20,16},{24,28},{28,24},{1,5},{5... | collective-permute-start | bytes 294920 | tf_op jit(solution)/shard_map/ppermute | solution.py:333
  10.0 15.3 %collective-permute-start.1 = (bf16[24,16,128]{2,1,0:T(8,128)(2,1)S(1)}, bf16[24,16,128]{2,1,0:T(8,128)(2,1)S(1)}, u32[]{:S(2)}, u32[]{:S(2)}) collective-permute-start(bf16[24,16,128]{2,1,0:T(8,128)(2,1)S(1)} %get-tuple-element.25), channel_id=1, source_target_pairs={{0,8},{4,12},{8,0},{12,4},{16,24},{20,28},{24,16},{28,20},{1,9},{5... | collective-permute-start | bytes 294920 | tf_op jit(solution)/shard_map/ppermute | solution.py:333
  11.6 16.2 %collective-permute-start.2 = (bf16[24,16,128]{2,1,0:T(8,128)(2,1)S(1)}, bf16[24,16,128]{2,1,0:T(8,128)(2,1)S(1)}, u32[]{:S(2)}, u32[]{:S(2)}) collective-permute-start(bf16[24,16,128]{2,1,0:T(8,128)(2,1)S(1)} %get-tuple-element.26), channel_id=1, source_target_pairs={{0,12},{4,8},{8,4},{12,0},{16,28},{20,24},{24,20},{28,16},{1,13},{... | collective-permute-start | bytes 294920 | tf_op jit(solution)/shard_map/ppermute | solution.py:333
  11.6 29.5 %collective-permute-start.3 = (bf16[24,16,128]{2,1,0:T(8,128)(2,1)S(1)}, bf16[24,16,128]{2,1,0:T(8,128)(2,1)S(1)}, u32[]{:S(2)}, u32[]{:S(2)}) collective-permute-start(bf16[24,16,128]{2,1,0:T(8,128)(2,1)S(1)} %get-tuple-element.29), channel_id=1, source_target_pairs={{0,16},{4,20},{8,24},{12,28},{16,0},{20,4},{24,8},{28,12},{1,17},{... | collective-permute-start | bytes 294920 | tf_op jit(solution)/shard_map/ppermute | solution.py:333
  14.2 28.0 %collective-permute-start.4 = (bf16[24,16,128]{2,1,0:T(8,128)(2,1)S(1)}, bf16[24,16,128]{2,1,0:T(8,128)(2,1)S(1)}, u32[]{:S(2)}, u32[]{:S(2)}) collective-permute-start(bf16[24,16,128]{2,1,0:T(8,128)(2,1)S(1)} %get-tuple-element.30), channel_id=1, source_target_pairs={{0,20},{4,16},{8,28},{12,24},{16,4},{20,0},{24,12},{28,8},{1,21},{... | collective-permute-start | bytes 294920 | tf_op jit(solution)/shard_map/ppermute | solution.py:333
  14.3 27.9 %collective-permute-start.5 = (bf16[24,16,128]{2,1,0:T(8,128)(2,1)S(1)}, bf16[24,16,128]{2,1,0:T(8,128)(2,1)S(1)}, u32[]{:S(2)}, u32[]{:S(2)}) collective-permute-start(bf16[24,16,128]{2,1,0:T(8,128)(2,1)S(1)} %get-tuple-element.31), channel_id=1, source_target_pairs={{0,24},{4,28},{8,16},{12,20},{16,8},{20,12},{24,0},{28,4},{1,25},{... | collective-permute-start | bytes 294920 | tf_op jit(solution)/shard_map/ppermute | solution.py:333
  25.3 17.0 %collective-permute-start.6 = (bf16[24,16,128]{2,1,0:T(8,128)(2,1)S(1)}, bf16[24,16,128]{2,1,0:T(8,128)(2,1)S(1)}, u32[]{:S(2)}, u32[]{:S(2)}) collective-permute-start(bf16[24,16,128]{2,1,0:T(8,128)(2,1)S(1)} %get-tuple-element.32), channel_id=1, source_target_pairs={{0,28},{4,24},{8,20},{12,16},{16,12},{20,8},{24,4},{28,0},{1,29},{... | collective-permute-start | bytes 294920 | tf_op jit(solution)/shard_map/ppermute | solution.py:333
  44.5 11.2 %collective-permute-start.12 = (s16[49,8,128]{2,1,0:T(8,128)(2,1)S(1)}, s16[49,8,128]{2,1,0:T(8,128)(2,1)S(1)}, u32[]{:S(2)}, u32[]{:S(2)}) collective-permute-start(s16[49,8,128]{2,1,0:T(8,128)(2,1)S(1)} %get-tuple-element.39), channel_id=1, source_target_pairs={{0,24},{4,28},{8,16},{12,20},{16,8},{20,12},{24,0},{28,4},{1,25},{... | collective-permute-start | bytes 301064 | tf_op jit(solution)/shard_map/ppermute | solution.py:333
  45.8 11.3 %collective-permute-start.13 = (s16[49,8,128]{2,1,0:T(8,128)(2,1)S(1)}, s16[49,8,128]{2,1,0:T(8,128)(2,1)S(1)}, u32[]{:S(2)}, u32[]{:S(2)}) collective-permute-start(s16[49,8,128]{2,1,0:T(8,128)(2,1)S(1)} %get-tuple-element.40), channel_id=1, source_target_pairs={{0,28},{4,24},{8,20},{12,16},{16,12},{20,8},{24,4},{28,0},{1,29},{... | collective-permute-start | bytes 301064 | tf_op jit(solution)/shard_map/ppermute | solution.py:333
  50.4 14.4 %collective-permute-start.10 = (s16[49,8,128]{2,1,0:T(8,128)(2,1)S(1)}, s16[49,8,128]{2,1,0:T(8,128)(2,1)S(1)}, u32[]{:S(2)}, u32[]{:S(2)}) collective-permute-start(s16[49,8,128]{2,1,0:T(8,128)(2,1)S(1)} %get-tuple-element.37), channel_id=1, source_target_pairs={{0,16},{4,20},{8,24},{12,28},{16,0},{20,4},{24,8},{28,12},{1,17},{... | collective-permute-start | bytes 301064 | tf_op jit(solution)/shard_map/ppermute | solution.py:333
  55.4 11.5 %collective-permute-start.11 = (s16[49,8,128]{2,1,0:T(8,128)(2,1)S(1)}, s16[49,8,128]{2,1,0:T(8,128)(2,1)S(1)}, u32[]{:S(2)}, u32[]{:S(2)}) collective-permute-start(s16[49,8,128]{2,1,0:T(8,128)(2,1)S(1)} %get-tuple-element.38), channel_id=1, source_target_pairs={{0,20},{4,16},{8,28},{12,24},{16,4},{20,0},{24,12},{28,8},{1,21},{... | collective-permute-start | bytes 301064 | tf_op jit(solution)/shard_map/ppermute | solution.py:333
  55.7 11.2 %collective-permute-start.7 = (s16[49,8,128]{2,1,0:T(8,128)(2,1)S(1)}, s16[49,8,128]{2,1,0:T(8,128)(2,1)S(1)}, u32[]{:S(2)}, u32[]{:S(2)}) collective-permute-start(s16[49,8,128]{2,1,0:T(8,128)(2,1)S(1)} %get-tuple-element.34), channel_id=1, source_target_pairs={{0,8},{4,12},{8,0},{12,4},{16,24},{20,28},{24,16},{28,20},{1,9},{5... | collective-permute-start | bytes 301064 | tf_op jit(solution)/shard_map/ppermute | solution.py:333
  55.7 11.1 %collective-permute-start.8 = (s16[49,8,128]{2,1,0:T(8,128)(2,1)S(1)}, s16[49,8,128]{2,1,0:T(8,128)(2,1)S(1)}, u32[]{:S(2)}, u32[]{:S(2)}) collective-permute-start(s16[49,8,128]{2,1,0:T(8,128)(2,1)S(1)} %get-tuple-element.35), channel_id=1, source_target_pairs={{0,12},{4,8},{8,4},{12,0},{16,28},{20,24},{24,20},{28,16},{1,13},{... | collective-permute-start | bytes 301064 | tf_op jit(solution)/shard_map/ppermute | solution.py:333
  57.1 9.8 %collective-permute-start.9 = (s16[49,8,128]{2,1,0:T(8,128)(2,1)S(1)}, s16[49,8,128]{2,1,0:T(8,128)(2,1)S(1)}, u32[]{:S(2)}, u32[]{:S(2)}) collective-permute-start(s16[49,8,128]{2,1,0:T(8,128)(2,1)S(1)} %get-tuple-element.36), channel_id=1, source_target_pairs={{0,4},{4,0},{8,12},{12,8},{16,20},{20,16},{24,28},{28,24},{1,5},{5... | collective-permute-start | bytes 301064 | tf_op jit(solution)/shard_map/ppermute | solution.py:333

commit v9 on v8

--- a/solution.py
+++ b/solution.py
@@ -145,21 +145,24 @@
     g_half, w_all = refs[-2:]
     stage_green(s, me_ref[0], 0, refs[:-2], g_half)
 
+    for source in range(s.groups):
+        w_all[source, s.planes] = jnp.zeros(s.plane, jnp.float32)
+
     @pl.loop(0, s.planes)
     def _(plane):
         for source in range(s.groups):
             if s.parts > 1:
-                w_all[source, plane] = screens_ref[source, plane].astype(jnp.float32)
+                w_all[source, plane] = screens_ref[source, plane].astype(jnp.float32) * SCALE
                 continue
             for c in range(s.cells):
-                piece = screens_ref[source * s.cells + c, plane].astype(jnp.float32)
+                piece = screens_ref[source * s.cells + c, plane].astype(jnp.float32) * SCALE
                 w_all[source, plane, c * s.held : (c + 1) * s.held, :] = piece
 
 
 def stage_near(s, me, screens, greens):
     return pl.pallas_call(
         functools.partial(stage_near_kernel, s),
-        out_shape=[held(s), jax.ShapeDtypeStruct((s.groups, s.planes) + s.plane, jnp.float32)],
+        out_shape=[held(s), jax.ShapeDtypeStruct((s.groups, s.planes + 1) + s.plane, jnp.float32)],
         in_specs=[SMEM] + [VMEM] * (len(greens) + 1),
         out_specs=[VMEM] * 2,
         compiler_params=PARAMS,
@@ -191,10 +194,10 @@
         for slot in range(slots):
             asked = table_ref[group * s.groups + source, slot]
             shift = jnp.maximum(asked, 0)
-            live = jnp.where(asked >= 0, 1.0, 0.0).astype(jnp.float32)
+            dead = asked < 0
             start = (group - source - low + 1) * s.energies - shift
-            w_real = w_all[source, real * s.energies + shift] * live
-            w_imag = w_all[source, imag * s.energies + shift] * live
+            w_real = w_all[source, jnp.where(dead, s.planes, real * s.energies + shift)]
+            w_imag = w_all[source, jnp.where(dead, s.planes, imag * s.energies + shift)]
             for j in range(s.energies):
                 g_real = g_half[real * s.held_planes + start + j]
                 g_imag = g_half[imag * s.held_planes + start + j]
@@ -240,7 +243,6 @@
             first = kind * 2 * s.energies
             sums = [begun[k, first + j] for j in range(2 * s.energies)]
             sums = add_terms(s, slots, 1 - side, me ^ k, kind, table_ref, g_far, w_all, sums)
-            sums = [total * SCALE for total in sums]
             if k == 0:
                 for j, total in enumerate(sums):
                     outs[at][first + j] = total

time: 68.4 us -> 68.4 us (level)
  no operation moved by 1% of the time
where the time goes in v9:
time: 68.4 us; the launch traced here: 68.1 us
  starting transfers between devices  29.4 us (43%)
  waiting for transfers between devices  25.4 us (37%)
  Pallas kernels  13.1 us (19%)
    ppermute x14, waiting for transfers between devices, swap(): lax.ppermute(block, 'energy', [(i, i ^ k) for i in range(s.groups)])  22.4 us
    ppermute x14, starting transfers between devices, swap(): lax.ppermute(block, 'energy', [(i, i ^ k) for i in range(s.groups)])  22.1 us
    all_to_all x1, starting transfers between devices, send_screened(): lax.all_to_all(pick_screened(s, cell_map, screened), ('energy', 'cell'),...  7.3 us
    pallas_call x1, Pallas kernels, partial_of(): pl.pallas_call(functools.partial(partial_kernel, s, table.shape[1]), out_...  4.84 us
    pallas_call x2, Pallas kernels, sigma_of(): pl.pallas_call(functools.partial(sigma_kernel, s, table.shape[1], ks), ou...  4 us
    all_to_all x1, waiting for transfers between devices, send_screened(): lax.all_to_all(pick_screened(s, cell_map, screened), ('energy', 'cell'),...  3 us
    pallas_call x1, Pallas kernels, pick_screened(): pl.pallas_call(functools.partial(pick_kernel, s), out_shape=out, in_specs...  2.11 us
  transfers between devices with their start and end apart: 15, of which 6 were waited for; matrix products, arithmetic and copies ran while one was open for 0% of the time, Pallas kernels for 11%

profile of v9, /device:TPU:0, one launch (start us, length us, event | category | flops | bytes accessed | tf_op | source)
XLA Modules:
  0.0 68.1 jit_solution(25808958520917496)
XLA Ops:
  0.0 2.1 %pick_screened.1 = bf16[32,24,4,128]{3,2,1,0:T(4,128)(2,1)} custom-call(s32[8]{0:T(128)} %map_hbm.1, bf16[24,8,4,512]{3,2,1,0:T(4,128)(2,1)} %bitcast.9), custom_call_target="tpu_custom_call" | custom-call | tf_op jit(solution)/shard_map/pick_screened/pallas_call | solution.py:85
  2.1 7.3 %all-to-all-start = ((bf16[32,24,4,128]{3,2,1,0:T(4,128)(2,1)}), bf16[32,24,4,128]{3,2,1,0:T(4,128)(2,1)S(1)}, u32[]{:S(2)}, u32[]{:S(2)}) async-start(bf16[32,24,4,128]{3,2,1,0:T(4,128)(2,1)} %pick_screened.1), calls=%async_computation | async-start | bytes 1572864 | tf_op jit(solution)/shard_map/all_to_all | solution.py:340
  9.6 0.3 collective-permute-start
  10.0 1.7 %collective-permute-start.1 = (bf16[24,16,128]{2,1,0:T(8,128)(2,1)S(1)}, bf16[24,16,128]{2,1,0:T(8,128)(2,1)S(1)}, u32[]{:S(2)}, u32[]{:S(2)}) collective-permute-start(bf16[24,16,128]{2,1,0:T(8,128)(2,1)S(1)} %get-tuple-element.25), channel_id=1, source_target_pairs={{0,8},{4,12},{8,0},{12,4},{16,24},{20,28},{24,16},{28,20},{1,9},{5... | collective-permute-start | bytes 294920 | tf_op jit(solution)/shard_map/ppermute | solution.py:335
  11.6 2.6 %collective-permute-start.3 = (bf16[24,16,128]{2,1,0:T(8,128)(2,1)S(1)}, bf16[24,16,128]{2,1,0:T(8,128)(2,1)S(1)}, u32[]{:S(2)}, u32[]{:S(2)}) collective-permute-start(bf16[24,16,128]{2,1,0:T(8,128)(2,1)S(1)} %get-tuple-element.29), channel_id=1, source_target_pairs={{0,16},{4,20},{8,24},{12,28},{16,0},{20,4},{24,8},{28,12},{1,17},{... | collective-permute-start | bytes 294920 | tf_op jit(solution)/shard_map/ppermute | solution.py:335
  14.4 3.5 %collective-permute-start.5 = (bf16[24,16,128]{2,1,0:T(8,128)(2,1)S(1)}, bf16[24,16,128]{2,1,0:T(8,128)(2,1)S(1)}, u32[]{:S(2)}, u32[]{:S(2)}) collective-permute-start(bf16[24,16,128]{2,1,0:T(8,128)(2,1)S(1)} %get-tuple-element.31), channel_id=1, source_target_pairs={{0,24},{4,28},{8,16},{12,20},{16,8},{20,12},{24,0},{28,4},{1,25},{... | collective-permute-start | bytes 294920 | tf_op jit(solution)/shard_map/ppermute | solution.py:335
  17.9 7.4 %collective-permute-done.1.refs_2_ = bf16[24,16,128]{2,1,0:T(8,128)(2,1)S(1)} collective-permute-done((bf16[24,16,128]{2,1,0:T(8,128)(2,1)S(1)}, bf16[24,16,128]{2,1,0:T(8,128)(2,1)S(1)}, u32[]{:S(2)}, u32[]{:S(2)}) %collective-permute-start.1) | collective-permute-done | bytes 98336 | tf_op jit(solution)/shard_map/ppermute | solution.py:335
  25.3 2.5 %collective-permute-start.6 = (bf16[24,16,128]{2,1,0:T(8,128)(2,1)S(1)}, bf16[24,16,128]{2,1,0:T(8,128)(2,1)S(1)}, u32[]{:S(2)}, u32[]{:S(2)}) collective-permute-start(bf16[24,16,128]{2,1,0:T(8,128)(2,1)S(1)} %get-tuple-element.32), channel_id=1, source_target_pairs={{0,28},{4,24},{8,20},{12,16},{16,12},{20,8},{24,4},{28,0},{1,29},{... | collective-permute-start | bytes 294920 | tf_op jit(solution)/shard_map/ppermute | solution.py:335
  27.8 3.0 %all-to-all-done.screens_ref = bf16[32,24,4,128]{3,2,1,0:T(4,128)(2,1)S(1)} async-done(((bf16[32,24,4,128]{3,2,1,0:T(4,128)(2,1)}), bf16[32,24,4,128]{3,2,1,0:T(4,128)(2,1)S(1)}, u32[]{:S(2)}, u32[]{:S(2)}) %all-to-all-start) | async-done | bytes 786464 | tf_op jit(solution)/shard_map/all_to_all | solution.py:340
  30.8 0.6 stage_near.1
  31.5 4.8 %partial.1.after_ref.begun = f32[8,24,16,128]{3,2,1,0:T(8,128)S(1)} custom-call(s32[1]{0:T(128)} %bitcast.me_ref, s32[64,3]{1,0:T(8,128)S(1)} %bitcast.6, f32[144,16,128]{2,1,0:T(8,128)S(1)} %get-tuple-element.27.g_half, f32[8,25,16,128]{3,2,1,0:T(8,128)S(1)} %get-tuple-element.28.w_all), custom_call_target="tpu_custom_call" | custom-call | tf_op jit(solution)/shard_map/partial/pallas_call | solution.py:225
  36.3 4.8 %collective-permute-done.3.refs_0_ = bf16[24,16,128]{2,1,0:T(8,128)(2,1)S(1)} collective-permute-done((bf16[24,16,128]{2,1,0:T(8,128)(2,1)S(1)}, bf16[24,16,128]{2,1,0:T(8,128)(2,1)S(1)}, u32[]{:S(2)}, u32[]{:S(2)}) %collective-permute-start.3) | collective-permute-done | bytes 98336 | tf_op jit(solution)/shard_map/ppermute | solution.py:335
  41.1 1.2 %collective-permute-done.4.refs_1_ = bf16[24,16,128]{2,1,0:T(8,128)(2,1)S(1)} collective-permute-done((bf16[24,16,128]{2,1,0:T(8,128)(2,1)S(1)}, bf16[24,16,128]{2,1,0:T(8,128)(2,1)S(1)}, u32[]{:S(2)}, u32[]{:S(2)}) %collective-permute-start.4) | collective-permute-done | bytes 98336 | tf_op jit(solution)/shard_map/ppermute | solution.py:335
  42.4 2.1 %sigma.3 = (s16[49,8,128]{2,1,0:T(8,128)(2,1)S(1)}, s16[49,8,128]{2,1,0:T(8,128)(2,1)S(1)}) custom-call(s32[1]{0:T(128)} %bitcast.me_ref, s32[64,3]{1,0:T(8,128)S(1)} %bitcast.7, f32[8,24,16,128]{3,2,1,0:T(8,128)S(1)} %partial.1.after_ref.begun, f32[8,25,16,128]{3,2,1,0:T(8,128)S(1)} %get-tuple-element.28.w_all, f32[144,16,128]{2,1,0:T(8,128)S(1)} %stage_far.1.g_far), custom_call_target="tpu_custom_call" | custom-call | tf_op jit(solution)/shard_map/sigma/pallas_call | solution.py:275
  44.5 1.4 %collective-permute-start.12 = (s16[49,8,128]{2,1,0:T(8,128)(2,1)S(1)}, s16[49,8,128]{2,1,0:T(8,128)(2,1)S(1)}, u32[]{:S(2)}, u32[]{:S(2)}) collective-permute-start(s16[49,8,128]{2,1,0:T(8,128)(2,1)S(1)} %get-tuple-element.39), channel_id=1, source_target_pairs={{0,24},{4,28},{8,16},{12,20},{16,8},{20,12},{24,0},{28,4},{1,25},{... | collective-permute-start | bytes 301064 | tf_op jit(solution)/shard_map/ppermute | solution.py:335
  45.8 2.6 %collective-permute-start.13 = (s16[49,8,128]{2,1,0:T(8,128)(2,1)S(1)}, s16[49,8,128]{2,1,0:T(8,128)(2,1)S(1)}, u32[]{:S(2)}, u32[]{:S(2)}) collective-permute-start(s16[49,8,128]{2,1,0:T(8,128)(2,1)S(1)} %get-tuple-element.40), channel_id=1, source_target_pairs={{0,28},{4,24},{8,20},{12,16},{16,12},{20,8},{24,4},{28,0},{1,29},{... | collective-permute-start | bytes 301064 | tf_op jit(solution)/shard_map/ppermute | solution.py:335
  48.5 1.9 %sigma.2 = (f32[24,16,128]{2,1,0:T(8,128)S(1)}, s16[49,8,128]{2,1,0:T(8,128)(2,1)S(1)}, s16[49,8,128]{2,1,0:T(8,128)(2,1)S(1)}, s16[49,8,128]{2,1,0:T(8,128)(2,1...) custom-call(s32[1]{0:T(128)} %bitcast.me_ref, s32[64,3]{1,0:T(8,128)S(1)} %bitcast.8, ...), custom_call_target="tpu_custom_call" | custom-call | tf_op jit(solution)/shard_map/sigma/pallas_call | solution.py:275
  50.4 4.9 %collective-permute-start.10 = (s16[49,8,128]{2,1,0:T(8,128)(2,1)S(1)}, s16[49,8,128]{2,1,0:T(8,128)(2,1)S(1)}, u32[]{:S(2)}, u32[]{:S(2)}) collective-permute-start(s16[49,8,128]{2,1,0:T(8,128)(2,1)S(1)} %get-tuple-element.37), channel_id=1, source_target_pairs={{0,16},{4,20},{8,24},{12,28},{16,0},{20,4},{24,8},{28,12},{1,17},{... | collective-permute-start | bytes 301064 | tf_op jit(solution)/shard_map/ppermute | solution.py:335
  55.3 0.4 collective-permute-start.11
  55.7 1.3 %collective-permute-start.8 = (s16[49,8,128]{2,1,0:T(8,128)(2,1)S(1)}, s16[49,8,128]{2,1,0:T(8,128)(2,1)S(1)}, u32[]{:S(2)}, u32[]{:S(2)}) collective-permute-start(s16[49,8,128]{2,1,0:T(8,128)(2,1)S(1)} %get-tuple-element.35), channel_id=1, source_target_pairs={{0,12},{4,8},{8,4},{12,0},{16,28},{20,24},{24,20},{28,16},{1,13},{... | collective-permute-start | bytes 301064 | tf_op jit(solution)/shard_map/ppermute | solution.py:335
  57.0 0.8 %collective-permute-start.9 = (s16[49,8,128]{2,1,0:T(8,128)(2,1)S(1)}, s16[49,8,128]{2,1,0:T(8,128)(2,1)S(1)}, u32[]{:S(2)}, u32[]{:S(2)}) collective-permute-start(s16[49,8,128]{2,1,0:T(8,128)(2,1)S(1)} %get-tuple-element.36), channel_id=1, source_target_pairs={{0,4},{4,0},{8,12},{12,8},{16,20},{20,16},{24,28},{28,24},{1,5},{5... | collective-permute-start | bytes 301064 | tf_op jit(solution)/shard_map/ppermute | solution.py:335
  57.8 7.0 %collective-permute-done.10.refs_4_ = s16[49,8,128]{2,1,0:T(8,128)(2,1)S(1)} collective-permute-done((s16[49,8,128]{2,1,0:T(8,128)(2,1)S(1)}, s16[49,8,128]{2,1,0:T(8,128)(2,1)S(1)}, u32[]{:S(2)}, u32[]{:S(2)}) %collective-permute-start.10) | collective-permute-done | bytes 100384 | tf_op jit(solution)/shard_map/ppermute | solution.py:335
  64.8 2.0 %collective-permute-done.11.refs_5_ = s16[49,8,128]{2,1,0:T(8,128)(2,1)S(1)} collective-permute-done((s16[49,8,128]{2,1,0:T(8,128)(2,1)S(1)}, s16[49,8,128]{2,1,0:T(8,128)(2,1)S(1)}, u32[]{:S(2)}, u32[]{:S(2)}) %collective-permute-start.11) | collective-permute-done | bytes 100384 | tf_op jit(solution)/shard_map/ppermute | solution.py:335
  66.8 1.3 %unpack.1 = f32[24,2,16,512]{3,2,1,0:T(8,128)} custom-call(s32[1]{0:T(128)} %bitcast.me_ref, f32[24,16,128]{2,1,0:T(8,128)S(1)} %get-tuple-element.33.refs_0_, s16[49,8,128]{2,1,0:T(8,128)(2,1)S(1)} %collective-permute-done.7.refs_1_, s16[49,8,128]{2,1,0:T(8,128)(2,1)S(1)} %collective-permute-done.8.refs_2_, ...), custom_call_target="tpu_custom_call" | custom-call | tf_op jit(solution)/shard_map/unpack/pallas_call | solution.py:319
  (22 shorter events, 0.6 us)
Async XLA Ops:
  0.0 9.5 %copy-start = (bf16[4,6,2,16,512]{4,3,2,1,0:T(8,128)(2,1)S(1)}, bf16[4,6,2,16,512]{4,3,2,1,0:T(8,128)(2,1)}, u32[]{:S(2)}) copy-start(bf16[4,6,2,16,512]{4,3,2,1,0:T(8,128)(2,1)} %param.5) | copy-start | bytes 2359300
  2.1 25.6 %copy-start.1 = (s32[8,8,3]{1,0,2:T(8,128)S(1)}, s32[8,8,3]{1,0,2:T(8,128)}, u32[]{:S(2)}) copy-start(s32[8,8,3]{1,0,2:T(8,128)} %param.8) | copy-start | bytes 2308
  2.1 25.6 %copy-start.2 = (s32[8,8]{1,0:T(8,128)S(1)}, s32[8,8]{1,0:T(8,128)}, u32[]{:S(2)}) copy-start(s32[8,8]{1,0:T(8,128)} %param.9) | copy-start | bytes 772
  2.1 28.7 %all-to-all-start = ((bf16[32,24,4,128]{3,2,1,0:T(4,128)(2,1)}), bf16[32,24,4,128]{3,2,1,0:T(4,128)(2,1)S(1)}, u32[]{:S(2)}, u32[]{:S(2)}) async-start(bf16[32,24,4,128]{3,2,1,0:T(4,128)(2,1)} %pick_screened.1), calls=%async_computation | async-start | bytes 1572864 | tf_op jit(solution)/shard_map/all_to_all | solution.py:340
  9.6 4.7 %collective-permute-start = (bf16[24,16,128]{2,1,0:T(8,128)(2,1)S(1)}, bf16[24,16,128]{2,1,0:T(8,128)(2,1)S(1)}, u32[]{:S(2)}, u32[]{:S(2)}) collective-permute-start(bf16[24,16,128]{2,1,0:T(8,128)(2,1)S(1)} %get-tuple-element.24), channel_id=1, source_target_pairs={{0,4},{4,0},{8,12},{12,8},{16,20},{20,16},{24,28},{28,24},{1,5},{5... | collective-permute-start | bytes 294920 | tf_op jit(solution)/shard_map/ppermute | solution.py:335
  10.0 15.3 %collective-permute-start.1 = (bf16[24,16,128]{2,1,0:T(8,128)(2,1)S(1)}, bf16[24,16,128]{2,1,0:T(8,128)(2,1)S(1)}, u32[]{:S(2)}, u32[]{:S(2)}) collective-permute-start(bf16[24,16,128]{2,1,0:T(8,128)(2,1)S(1)} %get-tuple-element.25), channel_id=1, source_target_pairs={{0,8},{4,12},{8,0},{12,4},{16,24},{20,28},{24,16},{28,20},{1,9},{5... | collective-permute-start | bytes 294920 | tf_op jit(solution)/shard_map/ppermute | solution.py:335
  11.6 16.2 %collective-permute-start.2 = (bf16[24,16,128]{2,1,0:T(8,128)(2,1)S(1)}, bf16[24,16,128]{2,1,0:T(8,128)(2,1)S(1)}, u32[]{:S(2)}, u32[]{:S(2)}) collective-permute-start(bf16[24,16,128]{2,1,0:T(8,128)(2,1)S(1)} %get-tuple-element.26), channel_id=1, source_target_pairs={{0,12},{4,8},{8,4},{12,0},{16,28},{20,24},{24,20},{28,16},{1,13},{... | collective-permute-start | bytes 294920 | tf_op jit(solution)/shard_map/ppermute | solution.py:335
  11.6 29.5 %collective-permute-start.3 = (bf16[24,16,128]{2,1,0:T(8,128)(2,1)S(1)}, bf16[24,16,128]{2,1,0:T(8,128)(2,1)S(1)}, u32[]{:S(2)}, u32[]{:S(2)}) collective-permute-start(bf16[24,16,128]{2,1,0:T(8,128)(2,1)S(1)} %get-tuple-element.29), channel_id=1, source_target_pairs={{0,16},{4,20},{8,24},{12,28},{16,0},{20,4},{24,8},{28,12},{1,17},{... | collective-permute-start | bytes 294920 | tf_op jit(solution)/shard_map/ppermute | solution.py:335
  14.2 28.0 %collective-permute-start.4 = (bf16[24,16,128]{2,1,0:T(8,128)(2,1)S(1)}, bf16[24,16,128]{2,1,0:T(8,128)(2,1)S(1)}, u32[]{:S(2)}, u32[]{:S(2)}) collective-permute-start(bf16[24,16,128]{2,1,0:T(8,128)(2,1)S(1)} %get-tuple-element.30), channel_id=1, source_target_pairs={{0,20},{4,16},{8,28},{12,24},{16,4},{20,0},{24,12},{28,8},{1,21},{... | collective-permute-start | bytes 294920 | tf_op jit(solution)/shard_map/ppermute | solution.py:335
  14.4 27.9 %collective-permute-start.5 = (bf16[24,16,128]{2,1,0:T(8,128)(2,1)S(1)}, bf16[24,16,128]{2,1,0:T(8,128)(2,1)S(1)}, u32[]{:S(2)}, u32[]{:S(2)}) collective-permute-start(bf16[24,16,128]{2,1,0:T(8,128)(2,1)S(1)} %get-tuple-element.31), channel_id=1, source_target_pairs={{0,24},{4,28},{8,16},{12,20},{16,8},{20,12},{24,0},{28,4},{1,25},{... | collective-permute-start | bytes 294920 | tf_op jit(solution)/shard_map/ppermute | solution.py:335
  25.3 17.0 %collective-permute-start.6 = (bf16[24,16,128]{2,1,0:T(8,128)(2,1)S(1)}, bf16[24,16,128]{2,1,0:T(8,128)(2,1)S(1)}, u32[]{:S(2)}, u32[]{:S(2)}) collective-permute-start(bf16[24,16,128]{2,1,0:T(8,128)(2,1)S(1)} %get-tuple-element.32), channel_id=1, source_target_pairs={{0,28},{4,24},{8,20},{12,16},{16,12},{20,8},{24,4},{28,0},{1,29},{... | collective-permute-start | bytes 294920 | tf_op jit(solution)/shard_map/ppermute | solution.py:335
  44.5 11.2 %collective-permute-start.12 = (s16[49,8,128]{2,1,0:T(8,128)(2,1)S(1)}, s16[49,8,128]{2,1,0:T(8,128)(2,1)S(1)}, u32[]{:S(2)}, u32[]{:S(2)}) collective-permute-start(s16[49,8,128]{2,1,0:T(8,128)(2,1)S(1)} %get-tuple-element.39), channel_id=1, source_target_pairs={{0,24},{4,28},{8,16},{12,20},{16,8},{20,12},{24,0},{28,4},{1,25},{... | collective-permute-start | bytes 301064 | tf_op jit(solution)/shard_map/ppermute | solution.py:335
  45.8 11.2 %collective-permute-start.13 = (s16[49,8,128]{2,1,0:T(8,128)(2,1)S(1)}, s16[49,8,128]{2,1,0:T(8,128)(2,1)S(1)}, u32[]{:S(2)}, u32[]{:S(2)}) collective-permute-start(s16[49,8,128]{2,1,0:T(8,128)(2,1)S(1)} %get-tuple-element.40), channel_id=1, source_target_pairs={{0,28},{4,24},{8,20},{12,16},{16,12},{20,8},{24,4},{28,0},{1,29},{... | collective-permute-start | bytes 301064 | tf_op jit(solution)/shard_map/ppermute | solution.py:335
  50.4 14.4 %collective-permute-start.10 = (s16[49,8,128]{2,1,0:T(8,128)(2,1)S(1)}, s16[49,8,128]{2,1,0:T(8,128)(2,1)S(1)}, u32[]{:S(2)}, u32[]{:S(2)}) collective-permute-start(s16[49,8,128]{2,1,0:T(8,128)(2,1)S(1)} %get-tuple-element.37), channel_id=1, source_target_pairs={{0,16},{4,20},{8,24},{12,28},{16,0},{20,4},{24,8},{28,12},{1,17},{... | collective-permute-start | bytes 301064 | tf_op jit(solution)/shard_map/ppermute | solution.py:335
  55.3 11.6 %collective-permute-start.11 = (s16[49,8,128]{2,1,0:T(8,128)(2,1)S(1)}, s16[49,8,128]{2,1,0:T(8,128)(2,1)S(1)}, u32[]{:S(2)}, u32[]{:S(2)}) collective-permute-start(s16[49,8,128]{2,1,0:T(8,128)(2,1)S(1)} %get-tuple-element.38), channel_id=1, source_target_pairs={{0,20},{4,16},{8,28},{12,24},{16,4},{20,0},{24,12},{28,8},{1,21},{... | collective-permute-start | bytes 301064 | tf_op jit(solution)/shard_map/ppermute | solution.py:335
  55.6 11.2 %collective-permute-start.7 = (s16[49,8,128]{2,1,0:T(8,128)(2,1)S(1)}, s16[49,8,128]{2,1,0:T(8,128)(2,1)S(1)}, u32[]{:S(2)}, u32[]{:S(2)}) collective-permute-start(s16[49,8,128]{2,1,0:T(8,128)(2,1)S(1)} %get-tuple-element.34), channel_id=1, source_target_pairs={{0,8},{4,12},{8,0},{12,4},{16,24},{20,28},{24,16},{28,20},{1,9},{5... | collective-permute-start | bytes 301064 | tf_op jit(solution)/shard_map/ppermute | solution.py:335
  55.7 11.1 %collective-permute-start.8 = (s16[49,8,128]{2,1,0:T(8,128)(2,1)S(1)}, s16[49,8,128]{2,1,0:T(8,128)(2,1)S(1)}, u32[]{:S(2)}, u32[]{:S(2)}) collective-permute-start(s16[49,8,128]{2,1,0:T(8,128)(2,1)S(1)} %get-tuple-element.35), channel_id=1, source_target_pairs={{0,12},{4,8},{8,4},{12,0},{16,28},{20,24},{24,20},{28,16},{1,13},{... | collective-permute-start | bytes 301064 | tf_op jit(solution)/shard_map/ppermute | solution.py:335
  57.0 9.8 %collective-permute-start.9 = (s16[49,8,128]{2,1,0:T(8,128)(2,1)S(1)}, s16[49,8,128]{2,1,0:T(8,128)(2,1)S(1)}, u32[]{:S(2)}, u32[]{:S(2)}) collective-permute-start(s16[49,8,128]{2,1,0:T(8,128)(2,1)S(1)} %get-tuple-element.36), channel_id=1, source_target_pairs={{0,4},{4,0},{8,12},{12,8},{16,20},{20,16},{24,28},{28,24},{1,5},{5... | collective-permute-start | bytes 301064 | tf_op jit(solution)/shard_map/ppermute | solution.py:335
